TPU v7x, 256 devices: a whole 4x4x8 slice. The times are simulated.
256 devices in a mesh: row: 16 (over z, y_hi), col: 16 (over y_lo, x, core).
Axes of the slice: x: 4, y: 4 (y_hi: 2, y_lo: 2; y = y_hi * 2 + y_lo), z: 8, core: 2. Of those that a mesh axis runs over, the one named last changes fastest.
Arguments:
- object_field: float32 [2, 8192, 8192], P(None, 'row', 'col'), may hold values from -6 to 6
- probe: float32 [2, 256, 256], replicated, may hold values from -5 to 5
- positions: int32 [512, 2], P(('row', 'col')), may hold values from 0 to 8191, as said below
- amplitudes: float32 [512, 256, 256], P(('row', 'col')), may hold values from 0 to 3
- counts: int32 [256], P(('row', 'col')), may hold values from 1 to 2, as said below
Outputs:
- object_grad: float32 [2, 8192, 8192], P(None, 'row', 'col')
- probe_grad: float32 [2, 256, 256], replicated
Inputs may be any that keep to these rules, and one draw needn't show every extreme that they name: Every slot's window starts inside the tile of the device that holds the slot: positions of slot s lie in tile s div 2, numbered row by row over 16 x 16 tiles. `counts`: some tile has exactly 2 live slots.
All inputs are finite; a program needn't handle non-finite values.
Results may differ from a plain program's by a relative error of at most 0.0003.
Values sent between devices are 32-bit elements; how exact they have to be, the bound alone decides.
No kernel may reach another device: no remote copies, remote signals or barrier semaphores. Data moves between devices by JAX's collectives and lax.ppermute only.
A program may use at most 64 MiB of HBM per device.

v0:
```python
import functools
import math

import jax
import jax.numpy as jnp
import ml_dtypes
import numpy as np
from jax import lax
from jax.experimental import pallas as pl
from jax.experimental.pallas import tpu as pltpu
from jax.sharding import PartitionSpec as P

AXES = ("row", "col")
HBM = pl.BlockSpec(memory_space=pltpu.HBM)
SMEM = pl.BlockSpec(memory_space=pltpu.SMEM)
VMEM = pl.BlockSpec(memory_space=pltpu.VMEM)
MIB = 1024 * 1024
SIZES = {"x": 4, "y": 4, "z": 8, "core": 2}


def shifted(block, axis, distance):
    devices = range(lax.axis_size(axis))
    route = [(i - distance, i) for i in devices if i - distance in devices]
    return lax.ppermute(block, axis, route)


def dft_tables(window):
    index = np.arange(window)
    phases = (np.outer(index, index) % window) * (2.0 * math.pi / window)
    tables = []
    for part in (np.cos(phases), -np.sin(phases)):
        part = part / math.sqrt(window)
        high = part.astype(ml_dtypes.bfloat16)
        tables += [high, (part - high.astype(np.float64)).astype(ml_dtypes.bfloat16)]
    return np.stack(tables)


def split(value):
    high = value.astype(jnp.bfloat16)
    return high, (value - high.astype(jnp.float32)).astype(jnp.bfloat16)


def dot(first, second):
    return jnp.dot(first, second, preferred_element_type=jnp.float32)


def times_table(re, im, tables, sign):
    w = re.shape[0]
    high, low = split(jnp.concatenate([re, im], axis=0))
    by_re = dot(high, tables[0]) + (dot(low, tables[0]) + dot(high, tables[1]))
    by_im = dot(high, tables[2]) + (dot(low, tables[2]) + dot(high, tables[3]))
    if sign > 0:
        return by_re[:w] - by_im[w:], by_re[w:] + by_im[:w]
    return by_re[:w] + by_im[w:], by_re[w:] - by_im[:w]


def table_times(re, im, tables, sign):
    w = re.shape[1]
    high, low = split(jnp.concatenate([re, im], axis=1))
    by_re = dot(tables[0], high) + (dot(tables[0], low) + dot(tables[1], high))
    by_im = dot(tables[2], high) + (dot(tables[2], low) + dot(tables[3], high))
    if sign > 0:
        return by_re[:, :w] - by_im[:, w:], by_re[:, w:] + by_im[:, :w]
    return by_re[:, :w] + by_im[:, w:], by_re[:, w:] - by_im[:, :w]


def slots_kernel(
    window, tile,
    counts_ref, pos_ref, place_ref, object_hbm, right_hbm, below0_hbm, below1_hbm, corner_hbm,
    seam_right_hbm, seam_corner_hbm, probe_hbm, amp_hbm, tables_hbm,
    tile_out, right_out, below0_out, below1_out, corner_out, keep_out, send_out,
    ext, grad, probe, turned, amp, tables, patch, probe_grad, sems,
):
    w, t = window, tile
    e = t + w
    live = counts_ref[0]
    core, at_seam = place_ref[0], place_ref[1]
    moves = [
        (probe_hbm, probe),
        (tables_hbm, tables),
        (amp_hbm, amp),
        (object_hbm, ext.at[:, 0:t, 0:t]),
        (below0_hbm, ext.at[:, t:e, 0:w]),
        (below1_hbm, ext.at[:, t:e, w:t]),
    ]
    copies = [pltpu.make_async_copy(a, b, sems.at[i]) for i, (a, b) in enumerate(moves)]
    for copy in copies:
        copy.start()

    def choose(act):
        sources = [(right_hbm.at[:, 0:w], right_hbm.at[:, w:t], corner_hbm), (seam_right_hbm, corner_hbm, seam_corner_hbm)]
        for flag, parts in enumerate(sources):
            @pl.when(at_seam == flag)
            def _():
                for i, part in enumerate(parts):
                    act(pltpu.make_async_copy(part, ext.at[:, i * w : i * w + w, t:e], sems.at[6 + i]))

    choose(lambda copy: copy.start())
    grad[...] = jnp.zeros_like(grad)
    probe_grad[...] = jnp.zeros_like(probe_grad)
    copies[0].wait()

    def turn(slot, carry):
        row = lax.rem(lax.rem(pos_ref[slot, 0], t), w)
        col = lax.rem(lax.rem(pos_ref[slot, 1], t), w)
        for plane in range(2):
            turned[slot, plane] = pltpu.roll(pltpu.roll(probe[plane], row, 0), col, 1)
        return carry

    lax.fori_loop(0, live, turn, 0)
    for copy in copies[1:]:
        copy.wait()
    choose(lambda copy: copy.wait())
    moves = [
        (grad.at[:, t:e, t:e], corner_out),
        (grad.at[:, t:e, w:t], below1_out),
        (grad.at[:, t:e, 0:w], below0_out),
        (grad.at[:, 0:t, t:e], right_out),
        (grad.at[:, 0:t, 0:t], tile_out),
    ]
    results = [pltpu.make_async_copy(a, b, sems.at[i]) for i, (a, b) in enumerate(moves)]
    rows = lax.broadcasted_iota(jnp.int32, (w, w), 0)
    cols = lax.broadcasted_iota(jnp.int32, (w, w), 1)

    def one_slot(slot, carry):
        top = lax.rem(pos_ref[slot, 0], t)
        left = lax.rem(pos_ref[slot, 1], t)
        row_turn, col_turn = lax.rem(top, w), lax.rem(left, w)
        row_at = pl.multiple_of((top // w) * w, w)
        col_at = pl.multiple_of((left // w) * w, w)
        in_low = rows < row_turn
        in_right = cols < col_turn
        blocks = [
            (pl.ds(row_at, w), pl.ds(col_at, w), ~in_low & ~in_right),
            (pl.ds(row_at, w), pl.ds(col_at + w, w), ~in_low & in_right),
            (pl.ds(row_at + w, w), pl.ds(col_at, w), in_low & ~in_right),
            (pl.ds(row_at + w, w), pl.ds(col_at + w, w), in_low & in_right),
        ]
        for plane in range(2):
            parts = [ext[plane, at_rows, at_cols] for at_rows, at_cols, _ in blocks]
            patch[plane] = jnp.where(
                in_low, jnp.where(in_right, parts[3], parts[2]), jnp.where(in_right, parts[1], parts[0])
            )
        re = turned[slot, 0] * patch[0] - turned[slot, 1] * patch[1]
        im = turned[slot, 0] * patch[1] + turned[slot, 1] * patch[0]
        re, im = times_table(re, im, tables, 1)
        re, im = table_times(re, im, tables, 1)
        factor = 1.0 - amp[slot] / jnp.sqrt(re * re + im * im + 1.0)
        re, im = times_table(factor * re, factor * im, tables, -1)
        re, im = table_times(re, im, tables, -1)
        terms = (turned[slot, 0] * re + turned[slot, 1] * im, turned[slot, 0] * im - turned[slot, 1] * re)
        for at_rows, at_cols, mask in blocks:
            for plane in range(2):
                grad[plane, at_rows, at_cols] += jnp.where(mask, terms[plane], 0.0)

        @pl.when(slot == live - 1)
        def _():
            for copy in results:
                copy.start()

        terms = (patch[0] * re + patch[1] * im, patch[0] * im - patch[1] * re)
        for plane in range(2):
            term = pltpu.roll(terms[plane], lax.rem(w - row_turn, w), 0)
            probe_grad[plane] += pltpu.roll(term, lax.rem(w - col_turn, w), 1)
        return carry

    lax.fori_loop(0, live, one_slot, 0)
    keep = pltpu.make_async_copy(probe_grad.at[core], keep_out, sems.at[7])
    send = pltpu.make_async_copy(probe_grad.at[1 - core], send_out, sems.at[8])
    for copy in (send, keep):
        copy.start()
    for copy in (send, keep, *results):
        copy.wait()


def slot_terms(counts, positions, where, object_field, halos, probe, amplitudes):
    w, t = probe.shape[1], object_field.shape[1]
    slots = positions.shape[0]
    f32 = functools.partial(jax.ShapeDtypeStruct, dtype=jnp.float32)
    block = f32((2, w, w))
    return pl.pallas_call(
        functools.partial(slots_kernel, w, t),
        out_shape=[f32((2, t, t)), f32((2, t, w)), block, block, block, f32((w, w)), f32((w, w))],
        in_specs=[SMEM] * 3 + [HBM] * 10,
        out_specs=[HBM] * 7,
        scratch_shapes=[
            pltpu.VMEM((2, t + w, t + w), jnp.float32),
            pltpu.VMEM((2, t + w, t + w), jnp.float32),
            pltpu.VMEM((2, w, w), jnp.float32),
            pltpu.VMEM((slots, 2, w, w), jnp.float32),
            pltpu.VMEM((slots, w, w), jnp.float32),
            pltpu.VMEM((4, w, w), jnp.bfloat16),
            pltpu.VMEM((2, w, w), jnp.float32),
            pltpu.VMEM((2, w, w), jnp.float32),
            pltpu.SemaphoreType.DMA((9,)),
        ],
        compiler_params=pltpu.CompilerParams(vmem_limit_bytes=60 * MIB),
        cost_estimate=pl.CostEstimate(flops=3 * 10**9, bytes_accessed=14 * MIB, transcendentals=0),
        name="slot_terms",
    )(counts, positions, where, object_field, *halos, probe, amplitudes, jnp.asarray(dft_tables(w)))


def combine_kernel(half, tile_ref, left_ref, seam_ref, above0_ref, above1_ref, out_ref):
    w = left_ref.shape[2]
    first, second = tile_ref[:, :, :w] + (left_ref[...] + seam_ref[...]), tile_ref[:, :, w:]

    @pl.when(pl.program_id(0) < half)
    def _():
        out_ref[:, :, :w] = first + above0_ref[...]
        out_ref[:, :, w:] = second + above1_ref[...]

    @pl.when(pl.program_id(0) >= half)
    def _():
        out_ref[:, :, :w] = first
        out_ref[:, :, w:] = second


def combined(tile_grad, from_left, from_seam, above0, above1):
    t, w = tile_grad.shape[1], from_left.shape[2]
    step = w // 4
    half = w // step
    above = pl.BlockSpec((2, step, w), lambda i: (0, jnp.minimum(i, half - 1), 0))
    return pl.pallas_call(
        functools.partial(combine_kernel, half),
        out_shape=jax.ShapeDtypeStruct(tile_grad.shape, jnp.float32),
        grid=(t // step,),
        in_specs=[
            pl.BlockSpec((2, step, t), lambda i: (0, i, 0)),
            pl.BlockSpec((2, step, w), lambda i: (0, i, 0)),
            pl.BlockSpec((2, step, w), lambda i: (0, i, 0)),
            above,
            above,
        ],
        out_specs=pl.BlockSpec((2, step, t), lambda i: (0, i, 0)),
        cost_estimate=pl.CostEstimate(flops=10**6, bytes_accessed=6 * MIB, transcendentals=0),
        name="combined",
    )(tile_grad, from_left, from_seam, above0, above1)


def place(x, y, z, core):
    return (z % 8 * 2 + y % 4 // 2) * 16 + y % 2 * 8 + x % 4 * 2 + core % 2


def moved(value, **distance):
    route = []
    for x in range(4):
        for y in range(4):
            for z in range(8):
                for core in range(2):
                    target = place(
                        x + distance.get("x", 0), y + distance.get("y", 0),
                        z + distance.get("z", 0), core + distance.get("core", 0),
                    )
                    route.append((place(x, y, z, core), target))
    return lax.ppermute(value, AXES, route)


def add_kernel(groups, *refs):
    count = sum(groups)
    outs = refs[count + (len(refs) - count - len(groups)) // 2 :]
    at = 0
    for out, size in zip(outs, groups):
        parts = refs[at : at + size] if size > 1 else [refs[at].at[i] for i in range(refs[at].shape[0])]
        out[...] = functools.reduce(jnp.add, [part[...] for part in parts])
        at += size


def added(groups, *arrived, vmem=4):
    shapes = [group[0].shape[1:] if len(group) == 1 else group[0].shape for group in groups]
    parts = [part for group in groups for part in group]
    n, m, k = len(parts), len(arrived), len(groups)
    result = pl.pallas_call(
        functools.partial(add_kernel, [len(group) for group in groups]),
        out_shape=[jax.ShapeDtypeStruct(s, jnp.float32) for s in shapes]
        + [jax.ShapeDtypeStruct(a.shape, a.dtype) for a in arrived],
        in_specs=[VMEM] * n + [HBM] * m,
        out_specs=[VMEM] * k + [HBM] * m,
        input_output_aliases={n + i: k + i for i in range(m)},
        compiler_params=pltpu.CompilerParams(vmem_limit_bytes=vmem * MIB),
        name="added",
    )(*parts, *arrived)
    return result


def summed(value, axis, *arrived):
    parts = [moved(value, **{axis: d}) for d in range(1, SIZES[axis])]
    return added([[value] + parts], *arrived)


def z_exchange(chunks):
    groups = [[place(x, y, z, c) for z in range(8)] for x in range(4) for y in range(4) for c in range(2)]
    return lax.all_to_all(chunks, AXES, 0, 0, tiled=True, axis_index_groups=groups)


def total(value, above1, from_left, above0):
    w = value.shape[0]
    core = lax.axis_index("col") % 2
    value = z_exchange(value.reshape(8, w // 8, w))
    value = added([[value]])[0]
    value, above0, above1 = summed(value, "x", above0, above1)
    value, from_left = summed(value, "y", from_left)
    value = z_exchange(jnp.broadcast_to(value, (8,) + value.shape)).reshape(w, w)
    other = moved(value, core=1)
    planes = jnp.where(core == 0, jnp.stack([value, other]), jnp.stack([other, value]))
    return planes, (above1, from_left, above0)


def halos_in(object_field, window):
    rows, cols = lax.axis_size("row"), lax.axis_size("col")
    seam = cols // 2
    w = window
    own0 = object_field[:, :w, :w]
    plain = [(i + 1, i) for i in range(cols - 1) if i + 1 != seam]
    below0 = shifted(own0, "row", -1)
    below1 = shifted(object_field[:, :w, w:], "row", -1)
    right = lax.ppermute(object_field[:, :, :w], "col", plain)
    relayed = lax.ppermute(object_field[:, w:, :w], "col", [(seam, 0)])
    seam_right = lax.ppermute(own0, "col", [(seam, seam - 1)])
    route = [((r + 1) * cols + seam, r * cols + seam - 1) for r in range(rows - 1)]
    seam_corner = lax.ppermute(own0, AXES, route)
    first = lax.axis_index("col") == 0
    corner = lax.ppermute(jnp.where(first, relayed, below0), "col", plain + [(0, seam - 1)])
    return right, below0, below1, corner, seam_right, seam_corner


def shards(object_field, probe, positions, amplitudes, counts):
    window = probe.shape[1]
    col = lax.axis_index("col")
    core = col % 2
    at_seam = (col == lax.axis_size("col") // 2 - 1).astype(jnp.int32)
    halos = halos_in(object_field, window)
    where = jnp.stack([core, at_seam])
    tile_grad, right_grad, below0_grad, below1_grad, corner_grad, keep, send = slot_terms(
        counts, positions, where, object_field, halos, probe, amplitudes
    )
    corner_in = shifted(corner_grad, "col", 1)
    above1 = shifted(below1_grad, "row", 1)
    rows, cols = lax.axis_size("row"), lax.axis_size("col")
    staged = (rows, cols) == (16, 16)
    other = moved(send, core=1) if staged else send
    value, below0_grad, right_grad = added([[keep, other], [below0_grad, corner_in]], right_grad, vmem=60)
    above0 = shifted(below0_grad, "row", 1)
    plain = [(i, i + 1) for i in range(cols - 1) if i + 1 != cols // 2]
    from_left = lax.ppermute(right_grad, "col", plain)
    from_seam = lax.ppermute(right_grad, "col", [(cols // 2 - 1, cols // 2)])
    if staged:
        probe_total, (above1, from_left, above0) = total(value, above1, from_left, above0)
    else:
        probe_total = lax.psum(jnp.where(core == 0, jnp.stack([keep, send]), jnp.stack([send, keep])), AXES)
    return combined(tile_grad, from_left, from_seam, above0, above1), probe_total


def solution(mesh):
    return jax.shard_map(
        shards,
        mesh=mesh,
        in_specs=(
            P(None, "row", "col"),
            P(),
            P(("row", "col"), None),
            P(("row", "col"), None, None),
            P(("row", "col")),
        ),
        out_specs=(P(None, "row", "col"), P()),
        check_vma=False,
    )
```

profile of v0, /device:TPU:1, one launch (start us, length us, event | category | flops | bytes accessed | tf_op | source)
XLA Modules:
  0.0 145.8 jit_solution(9195994818366278017)
XLA Ops:
  0.6 2.5 %fusion = (f32[2,256,256]{2,1,0:T(8,128)S(1)}, f32[2,256,256]{2,1,0:T(8,128)}, f32[2,256,256]{2,1,0:T(8,128)S(1)}) fusion(f32[2,512,512]{2,1,0:T(8,128)} %object_hbm.1), kind=kLoop, calls=%fused_computation.3 | loop fusion | bytes 3145728 | tf_op jit(solution)/shard_map/slice | solution.py:317
  3.8 1.3 collective-permute-start.1
  5.2 5.7 %collective-permute-start = (f32[2,512,256]{2,1,0:T(8,128)S(1)}, f32[2,512,256]{2,1,0:T(8,128)}, u32[]{:S(2)}, u32[]{:S(2)}) collective-permute-start(f32[2,512,256]{2,1,0:T(8,128)S(1)} %slice.12), channel_id=1, source_target_pairs={{1,0},{2,1},{3,2},{4,3},{5,4},{6,5},{7,6},{9,8},{10,9},{11,10},{12... | collective-permute-start | bytes 3145736 | tf_op jit(solution)/shard_map/ppermute | solution.py:316
  11.0 1.5 %collective-permute-start.6 = (f32[2,256,256]{2,1,0:T(8,128)S(1)}, f32[2,256,256]{2,1,0:T(8,128)}, u32[]{:S(2)}, u32[]{:S(2)}) collective-permute-start(f32[2,256,256]{2,1,0:T(8,128)S(1)} %get-tuple-element.34), channel_id=1, source_target_pairs={{24,7},{40,23},{56,39},{72,55},{88,71},{104,87},{120,103},{136,119... | collective-permute-start | bytes 1572872 | tf_op jit(solution)/shard_map/ppermute | solution.py:320
  12.4 1.4 collective-permute-start.5
  15.2 3.2 %collective-permute-done.1.below0_hbm = f32[2,256,256]{2,1,0:T(8,128)S(1)} collective-permute-done((f32[2,256,256]{2,1,0:T(8,128)S(1)}, f32[2,256,256]{2,1,0:T(8,128)S(1)}, u32[]{:S(2)}, u32[]{:S(2)}) %collective-permute-start.1) | collective-permute-done | bytes 524320 | tf_op jit(solution)/shard_map/ppermute | solution.py:24
  18.4 17.3 %collective-permute-start.4 = (f32[2,256,256]{2,1,0:T(8,128)S(1)}, f32[2,256,256]{2,1,0:T(8,128)S(1)}, u32[]{:S(2)}, u32[]{:S(2)}) collective-permute-start(f32[2,256,256]{2,1,0:T(8,128)S(1)} %broadcast_select_fusion), channel_id=1, source_target_pairs={{1,0},{2,1},{3,2},{4,3},{5,4},{6,5},{7,6},{9,8},{10,9},{11,10},{12... | collective-permute-start | bytes 1572872 | tf_op jit(solution)/shard_map/ppermute | solution.py:322
  38.0 10.3 %slot_terms.1 = (f32[2,512,512]{2,1,0:T(8,128)}, f32[2,512,256]{2,1,0:T(8,128)}, f32[2,256,256]{2,1,0:T(8,128)}, f32[2,256,256]{2,1,0:T(8,128)}, f32[2,256,256]{...) custom-call(s32[1]{0:T(128)S(6)} %copy.16.counts_ref, s32[2,2]{1,0:T(2,128)} %pos_ref.1, s32[2]{0:T(128)} %pad_add_fusion.place_ref, ...), custom_call_target="tpu_custom_call" | custom-call | flops 3000000000 | bytes 14680064 | tf_op jit(solution)/shard_map/slot_terms/pallas_call | solution.py:181
  48.4 1.9 %collective-permute-start.8 = (f32[2,256,256]{2,1,0:T(8,128)}, f32[2,256,256]{2,1,0:T(8,128)S(1)}, u32[]{:S(2)}, u32[]{:S(2)}) collective-permute-start(f32[2,256,256]{2,1,0:T(8,128)} %get-tuple-element.21), channel_id=1, source_target_pairs={{0,1},{1,2},{2,3},{3,4},{4,5},{5,6},{6,7},{7,8},{8,9},{9,10},{10,1... | collective-permute-start | bytes 1572872 | tf_op jit(solution)/shard_map/ppermute | solution.py:24
  50.3 7.6 %collective-permute-start.7 = (f32[256,256]{1,0:T(8,128)}, f32[256,256]{1,0:T(8,128)S(1)}, u32[]{:S(2)}, u32[]{:S(2)}) collective-permute-start(f32[256,256]{1,0:T(8,128)} %get-tuple-element.19), channel_id=1, source_target_pairs={{0,1},{1,0},{32,33},{33,32},{64,65},{65,64},{96,97},{97,96},{128,1... | collective-permute-start | bytes 786440 | tf_op jit(solution)/shard_map/ppermute | solution.py:255
  57.9 1.8 %collective-permute-done.7.refs_1_ = f32[256,256]{1,0:T(8,128)S(1)} collective-permute-done((f32[256,256]{1,0:T(8,128)}, f32[256,256]{1,0:T(8,128)S(1)}, u32[]{:S(2)}, u32[]{:S(2)}) %collective-permute-start.7) | collective-permute-done | bytes 262176 | tf_op jit(solution)/shard_map/ppermute | solution.py:255
  60.6 2.3 %added.4 = (f32[256,256]{1,0:T(8,128)}, f32[2,256,256]{2,1,0:T(8,128)}, f32[2,512,256]{2,1,0:T(8,128)}) custom-call(f32[256,256]{1,0:T(8,128)} %get-tuple-element.18.refs_0_, f32[256,256]{1,0:T(8,128)} %copy-done.7, f32[2,256,256]{2,1,0:T(8,128)} %get-tuple-element.20.refs_2_, f32[2,256,256]{2,1,0:T(8,128)} %copy-done.5, ...), custom_call_target="tpu_custom_call", output_to_operand_aliasing={{2}: (4, {})} | custom-call | tf_op jit(solution)/shard_map/added/pallas_call | solution.py:272
  62.9 1.9 %collective-permute-start.17 = (f32[2,512,256]{2,1,0:T(8,128)}, f32[2,512,256]{2,1,0:T(8,128)S(1)}, u32[]{:S(2)}, u32[]{:S(2)}) collective-permute-start(f32[2,512,256]{2,1,0:T(8,128)} %get-tuple-element.27), channel_id=1, source_target_pairs={{0,1},{1,2},{2,3},{3,4},{4,5},{5,6},{6,7},{8,9},{9,10},{10,11},{11... | collective-permute-start | bytes 3145736 | tf_op jit(solution)/shard_map/ppermute | solution.py:344
  64.8 5.1 %collective-permute-start.13 = (f32[2,256,256]{2,1,0:T(8,128)}, f32[2,256,256]{2,1,0:T(8,128)S(1)}, u32[]{:S(2)}, u32[]{:S(2)}) collective-permute-start(f32[2,256,256]{2,1,0:T(8,128)} %get-tuple-element.25), channel_id=1, source_target_pairs={{0,16},{16,32},{32,48},{48,64},{64,80},{80,96},{96,112},{112,128},... | collective-permute-start | bytes 1572872 | tf_op jit(solution)/shard_map/ppermute | solution.py:24
  69.9 6.4 %all-to-all-start = ((f32[8,32,256]{2,1,0:T(8,128)}), f32[8,32,256]{2,1,0:T(8,128)S(1)}, u32[]{:S(2)}, u32[]{:S(2)}) async-start(f32[8,32,256]{2,1,0:T(8,128)} %bitcast.8), calls=%async_computation | async-start | bytes 524288 | tf_op jit(solution)/shard_map/all_to_all | solution.py:292
  76.3 2.2 %collective-permute-start.12 = (f32[2,256,256]{2,1,0:T(8,128)}, f32[2,256,256]{2,1,0:T(8,128)S(1)}, u32[]{:S(2)}, u32[]{:S(2)}) collective-permute-start(f32[2,256,256]{2,1,0:T(8,128)} %get-tuple-element.24), channel_id=1, source_target_pairs={{0,16},{16,32},{32,48},{48,64},{64,80},{80,96},{96,112},{112,128},... | collective-permute-start | bytes 1572872 | tf_op jit(solution)/shard_map/ppermute | solution.py:24
  79.3 8.6 %all-to-all-done.refs_0_ = f32[8,32,256]{2,1,0:T(8,128)S(1)} async-done(((f32[8,32,256]{2,1,0:T(8,128)}), f32[8,32,256]{2,1,0:T(8,128)S(1)}, u32[]{:S(2)}, u32[]{:S(2)}) %all-to-all-start) | async-done | bytes 262176 | tf_op jit(solution)/shard_map/all_to_all | solution.py:292
  87.9 8.2 %collective-permute-start.11 = (f32[32,256]{1,0:T(8,128)S(1)}, f32[32,256]{1,0:T(8,128)S(1)}, u32[]{:S(2)}, u32[]{:S(2)}) collective-permute-start(f32[32,256]{1,0:T(8,128)S(1)} %added.5.refs_0_), channel_id=1, source_target_pairs={{0,6},{1,7},{32,38},{33,39},{64,70},{65,71},{96,102},{97,103},{128... | collective-permute-start | bytes 98312 | tf_op jit(solution)/shard_map/ppermute | solution.py:255
  97.1 3.3 %collective-permute-done.10.refs_2_ = f32[32,256]{1,0:T(8,128)S(1)} collective-permute-done((f32[32,256]{1,0:T(8,128)S(1)}, f32[32,256]{1,0:T(8,128)S(1)}, u32[]{:S(2)}, u32[]{:S(2)}) %collective-permute-start.10) | collective-permute-done | bytes 32800 | tf_op jit(solution)/shard_map/ppermute | solution.py:255
  100.5 9.2 %collective-permute-done.9.refs_1_ = f32[32,256]{1,0:T(8,128)S(1)} collective-permute-done((f32[32,256]{1,0:T(8,128)S(1)}, f32[32,256]{1,0:T(8,128)S(1)}, u32[]{:S(2)}, u32[]{:S(2)}) %collective-permute-start.9) | collective-permute-done | bytes 32800 | tf_op jit(solution)/shard_map/ppermute | solution.py:255
  109.8 4.2 %collective-permute-start.15 = (f32[32,256]{1,0:T(8,128)S(1)}, f32[32,256]{1,0:T(8,128)S(1)}, u32[]{:S(2)}, u32[]{:S(2)}) collective-permute-start(f32[32,256]{1,0:T(8,128)S(1)} %get-tuple-element.26.refs_0_), channel_id=1, source_target_pairs={{0,16},{1,17},{32,48},{33,49},{64,80},{65,81},{96,112},{97,113},{1... | collective-permute-start | bytes 98312 | tf_op jit(solution)/shard_map/ppermute | solution.py:255
  115.3 2.7 %collective-permute-done.14.refs_1_ = f32[32,256]{1,0:T(8,128)S(1)} collective-permute-done((f32[32,256]{1,0:T(8,128)S(1)}, f32[32,256]{1,0:T(8,128)S(1)}, u32[]{:S(2)}, u32[]{:S(2)}) %collective-permute-start.14) | collective-permute-done | bytes 32800 | tf_op jit(solution)/shard_map/ppermute | solution.py:255
  119.0 18.2 %all_to_all.10 = f32[8,32,256]{2,1,0:T(8,128)S(1)} all-to-all(f32[8,32,256]{2,1,0:T(8,128)S(1)} %broadcast_in_dim.3), channel_id=1, replica_groups={{0,32,64,96,128,160,192,224},{1,33,65,97,129,161,193,225},{8,40,72,104,..., dimensions={0} | all-to-all | bytes 524288 | tf_op jit(solution)/shard_map/all_to_all | solution.py:292
  138.6 6.3 %combined.1 = f32[2,512,512]{2,1,0:T(8,128)} custom-call(f32[2,512,512]{2,1,0:T(8,128)} %get-tuple-element.17.tile_ref, f32[2,512,256]{2,1,0:T(8,128)} %copy-done, f32[2,512,256]{2,1,0:T(8,128)} %copy-done.4, f32[2,256,256]{2,1,0:T(8,128)} %copy-done.2, f32[2,256,256]{2,1,0:T(8,128)} %copy-done.1), custom_call_target="tpu_custom_call" | custom-call | flops 1000000 | bytes 6291456 | tf_op jit(solution)/shard_map/combined/pallas_call | solution.py:223
  (49 shorter events, 11.1 us)
Async XLA Ops:
  3.1 10.8 %collective-permute-start.3 = (f32[2,256,256]{2,1,0:T(8,128)S(1)}, f32[2,256,256]{2,1,0:T(8,128)S(1)}, u32[]{:S(2)}, u32[]{:S(2)}) collective-permute-start(f32[2,256,256]{2,1,0:T(8,128)S(1)} %get-tuple-element.32), channel_id=1, source_target_pairs={{8,0},{24,16},{40,32},{56,48},{72,64},{88,80},{104,96},{120,112},{... | collective-permute-start | bytes 1572872 | tf_op jit(solution)/shard_map/ppermute | solution.py:317
  3.8 14.5 %collective-permute-start.1 = (f32[2,256,256]{2,1,0:T(8,128)S(1)}, f32[2,256,256]{2,1,0:T(8,128)S(1)}, u32[]{:S(2)}, u32[]{:S(2)}) collective-permute-start(f32[2,256,256]{2,1,0:T(8,128)S(1)} %get-tuple-element.34), channel_id=1, source_target_pairs={{16,0},{32,16},{48,32},{64,48},{80,64},{96,80},{112,96},{128,112},... | collective-permute-start | bytes 1572872 | tf_op jit(solution)/shard_map/ppermute | solution.py:24
  5.2 31.8 %collective-permute-start = (f32[2,512,256]{2,1,0:T(8,128)S(1)}, f32[2,512,256]{2,1,0:T(8,128)}, u32[]{:S(2)}, u32[]{:S(2)}) collective-permute-start(f32[2,512,256]{2,1,0:T(8,128)S(1)} %slice.12), channel_id=1, source_target_pairs={{1,0},{2,1},{3,2},{4,3},{5,4},{6,5},{7,6},{9,8},{10,9},{11,10},{12... | collective-permute-start | bytes 3145736 | tf_op jit(solution)/shard_map/ppermute | solution.py:316
  11.0 26.0 %collective-permute-start.6 = (f32[2,256,256]{2,1,0:T(8,128)S(1)}, f32[2,256,256]{2,1,0:T(8,128)}, u32[]{:S(2)}, u32[]{:S(2)}) collective-permute-start(f32[2,256,256]{2,1,0:T(8,128)S(1)} %get-tuple-element.34), channel_id=1, source_target_pairs={{24,7},{40,23},{56,39},{72,55},{88,71},{104,87},{120,103},{136,119... | collective-permute-start | bytes 1572872 | tf_op jit(solution)/shard_map/ppermute | solution.py:320
  12.4 24.6 %collective-permute-start.5 = (f32[2,256,256]{2,1,0:T(8,128)S(1)}, f32[2,256,256]{2,1,0:T(8,128)}, u32[]{:S(2)}, u32[]{:S(2)}) collective-permute-start(f32[2,256,256]{2,1,0:T(8,128)S(1)} %get-tuple-element.34), channel_id=1, source_target_pairs={{8,7},{24,23},{40,39},{56,55},{72,71},{88,87},{104,103},{120,119},... | collective-permute-start | bytes 1572872 | tf_op jit(solution)/shard_map/ppermute | solution.py:318
  13.9 23.1 %collective-permute-start.2 = (f32[2,256,256]{2,1,0:T(8,128)}, f32[2,256,256]{2,1,0:T(8,128)}, u32[]{:S(2)}, u32[]{:S(2)}) collective-permute-start(f32[2,256,256]{2,1,0:T(8,128)} %get-tuple-element.33), channel_id=1, source_target_pairs={{16,0},{32,16},{48,32},{64,48},{80,64},{96,80},{112,96},{128,112},... | collective-permute-start | bytes 1572872 | tf_op jit(solution)/shard_map/ppermute | solution.py:24
  18.3 18.9 %copy-start.6 = (f32[2,256,256]{2,1,0:T(8,128)}, f32[2,256,256]{2,1,0:T(8,128)S(1)}, u32[]{:S(2)}) copy-start(f32[2,256,256]{2,1,0:T(8,128)S(1)} %collective-permute-done.1.below0_hbm) | copy-start | bytes 1572868
  18.4 18.8 %collective-permute-start.4 = (f32[2,256,256]{2,1,0:T(8,128)S(1)}, f32[2,256,256]{2,1,0:T(8,128)S(1)}, u32[]{:S(2)}, u32[]{:S(2)}) collective-permute-start(f32[2,256,256]{2,1,0:T(8,128)S(1)} %broadcast_select_fusion), channel_id=1, source_target_pairs={{1,0},{2,1},{3,2},{4,3},{5,4},{6,5},{7,6},{9,8},{10,9},{11,10},{12... | collective-permute-start | bytes 1572872 | tf_op jit(solution)/shard_map/ppermute | solution.py:322
  48.4 11.4 %collective-permute-start.8 = (f32[2,256,256]{2,1,0:T(8,128)}, f32[2,256,256]{2,1,0:T(8,128)S(1)}, u32[]{:S(2)}, u32[]{:S(2)}) collective-permute-start(f32[2,256,256]{2,1,0:T(8,128)} %get-tuple-element.21), channel_id=1, source_target_pairs={{0,1},{1,2},{2,3},{3,4},{4,5},{5,6},{6,7},{7,8},{8,9},{9,10},{10,1... | collective-permute-start | bytes 1572872 | tf_op jit(solution)/shard_map/ppermute | solution.py:24
  50.3 9.4 %collective-permute-start.7 = (f32[256,256]{1,0:T(8,128)}, f32[256,256]{1,0:T(8,128)S(1)}, u32[]{:S(2)}, u32[]{:S(2)}) collective-permute-start(f32[256,256]{1,0:T(8,128)} %get-tuple-element.19), channel_id=1, source_target_pairs={{0,1},{1,0},{32,33},{33,32},{64,65},{65,64},{96,97},{97,96},{128,1... | collective-permute-start | bytes 786440 | tf_op jit(solution)/shard_map/ppermute | solution.py:255
  62.9 55.1 %collective-permute-start.17 = (f32[2,512,256]{2,1,0:T(8,128)}, f32[2,512,256]{2,1,0:T(8,128)S(1)}, u32[]{:S(2)}, u32[]{:S(2)}) collective-permute-start(f32[2,512,256]{2,1,0:T(8,128)} %get-tuple-element.27), channel_id=1, source_target_pairs={{0,1},{1,2},{2,3},{3,4},{4,5},{5,6},{6,7},{8,9},{9,10},{10,11},{11... | collective-permute-start | bytes 3145736 | tf_op jit(solution)/shard_map/ppermute | solution.py:344
  64.8 31.3 %collective-permute-start.13 = (f32[2,256,256]{2,1,0:T(8,128)}, f32[2,256,256]{2,1,0:T(8,128)S(1)}, u32[]{:S(2)}, u32[]{:S(2)}) collective-permute-start(f32[2,256,256]{2,1,0:T(8,128)} %get-tuple-element.25), channel_id=1, source_target_pairs={{0,16},{16,32},{32,48},{48,64},{64,80},{80,96},{96,112},{112,128},... | collective-permute-start | bytes 1572872 | tf_op jit(solution)/shard_map/ppermute | solution.py:24
  69.9 18.0 %all-to-all-start = ((f32[8,32,256]{2,1,0:T(8,128)}), f32[8,32,256]{2,1,0:T(8,128)S(1)}, u32[]{:S(2)}, u32[]{:S(2)}) async-start(f32[8,32,256]{2,1,0:T(8,128)} %bitcast.8), calls=%async_computation | async-start | bytes 524288 | tf_op jit(solution)/shard_map/all_to_all | solution.py:292
  76.3 33.4 %collective-permute-start.12 = (f32[2,256,256]{2,1,0:T(8,128)}, f32[2,256,256]{2,1,0:T(8,128)S(1)}, u32[]{:S(2)}, u32[]{:S(2)}) collective-permute-start(f32[2,256,256]{2,1,0:T(8,128)} %get-tuple-element.24), channel_id=1, source_target_pairs={{0,16},{16,32},{32,48},{48,64},{64,80},{80,96},{96,112},{112,128},... | collective-permute-start | bytes 1572872 | tf_op jit(solution)/shard_map/ppermute | solution.py:24
  78.6 59.1 %collective-permute-start.18 = (f32[2,512,256]{2,1,0:T(8,128)}, f32[2,512,256]{2,1,0:T(8,128)S(1)}, u32[]{:S(2)}, u32[]{:S(2)}) collective-permute-start(f32[2,512,256]{2,1,0:T(8,128)} %get-tuple-element.27), channel_id=1, source_target_pairs={{7,8},{23,24},{39,40},{55,56},{71,72},{87,88},{103,104},{119,120},... | collective-permute-start | bytes 3145736 | tf_op jit(solution)/shard_map/ppermute | solution.py:345
  87.9 9.2 %collective-permute-start.11 = (f32[32,256]{1,0:T(8,128)S(1)}, f32[32,256]{1,0:T(8,128)S(1)}, u32[]{:S(2)}, u32[]{:S(2)}) collective-permute-start(f32[32,256]{1,0:T(8,128)S(1)} %added.5.refs_0_), channel_id=1, source_target_pairs={{0,6},{1,7},{32,38},{33,39},{64,70},{65,71},{96,102},{97,103},{128... | collective-permute-start | bytes 98312 | tf_op jit(solution)/shard_map/ppermute | solution.py:255
  96.1 4.4 %collective-permute-start.10 = (f32[32,256]{1,0:T(8,128)S(1)}, f32[32,256]{1,0:T(8,128)S(1)}, u32[]{:S(2)}, u32[]{:S(2)}) collective-permute-start(f32[32,256]{1,0:T(8,128)S(1)} %added.5.refs_0_), channel_id=1, source_target_pairs={{0,4},{1,5},{32,36},{33,37},{64,68},{65,69},{96,100},{97,101},{128... | collective-permute-start | bytes 98312 | tf_op jit(solution)/shard_map/ppermute | solution.py:255
  97.1 12.6 %collective-permute-start.9 = (f32[32,256]{1,0:T(8,128)S(1)}, f32[32,256]{1,0:T(8,128)S(1)}, u32[]{:S(2)}, u32[]{:S(2)}) collective-permute-start(f32[32,256]{1,0:T(8,128)S(1)} %added.5.refs_0_), channel_id=1, source_target_pairs={{0,2},{1,3},{32,34},{33,35},{64,66},{65,67},{96,98},{97,99},{128,1... | collective-permute-start | bytes 98312 | tf_op jit(solution)/shard_map/ppermute | solution.py:255
  109.7 27.9 %copy-start.1 = (f32[2,256,256]{2,1,0:T(8,128)}, f32[2,256,256]{2,1,0:T(8,128)S(1)}, u32[]{:S(2)}) copy-start(f32[2,256,256]{2,1,0:T(8,128)S(1)} %get-tuple-element.30.above1_ref) | copy-start | bytes 1572868
  109.7 27.9 %copy-start.2 = (f32[2,256,256]{2,1,0:T(8,128)}, f32[2,256,256]{2,1,0:T(8,128)S(1)}, u32[]{:S(2)}) copy-start(f32[2,256,256]{2,1,0:T(8,128)S(1)} %get-tuple-element.29.above0_ref) | copy-start | bytes 1572868
  109.8 5.0 %collective-permute-start.16 = (f32[32,256]{1,0:T(8,128)S(1)}, f32[32,256]{1,0:T(8,128)S(1)}, u32[]{:S(2)}, u32[]{:S(2)}) collective-permute-start(f32[32,256]{1,0:T(8,128)S(1)} %get-tuple-element.26.refs_0_), channel_id=1, source_target_pairs={{0,24},{1,25},{32,56},{33,57},{64,88},{65,89},{96,120},{97,121},{1... | collective-permute-start | bytes 98312 | tf_op jit(solution)/shard_map/ppermute | solution.py:255
  109.8 5.5 %collective-permute-start.15 = (f32[32,256]{1,0:T(8,128)S(1)}, f32[32,256]{1,0:T(8,128)S(1)}, u32[]{:S(2)}, u32[]{:S(2)}) collective-permute-start(f32[32,256]{1,0:T(8,128)S(1)} %get-tuple-element.26.refs_0_), channel_id=1, source_target_pairs={{0,16},{1,17},{32,48},{33,49},{64,80},{65,81},{96,112},{97,113},{1... | collective-permute-start | bytes 98312 | tf_op jit(solution)/shard_map/ppermute | solution.py:255
  114.0 4.0 %collective-permute-start.14 = (f32[32,256]{1,0:T(8,128)S(1)}, f32[32,256]{1,0:T(8,128)S(1)}, u32[]{:S(2)}, u32[]{:S(2)}) collective-permute-start(f32[32,256]{1,0:T(8,128)S(1)} %get-tuple-element.26.refs_0_), channel_id=1, source_target_pairs={{0,8},{1,9},{32,40},{33,41},{64,72},{65,73},{96,104},{97,105},{128... | collective-permute-start | bytes 98312 | tf_op jit(solution)/shard_map/ppermute | solution.py:255
  137.3 7.7 %collective-permute-start.19 = (f32[256,256]{1,0:T(8,128)S(1)}, f32[256,256]{1,0:T(8,128)S(1)}, u32[]{:S(2)}, u32[]{:S(2)}) collective-permute-start(f32[256,256]{1,0:T(8,128)S(1)} %bitcast.6), channel_id=1, source_target_pairs={{0,1},{1,0},{32,33},{33,32},{64,65},{65,64},{96,97},{97,96},{128,1... | collective-permute-start | bytes 786440 | tf_op jit(solution)/shard_map/ppermute | solution.py:255
  (6 other events, 8.8 us)
where the time goes:
time: 146 us
  starting transfers between devices  68.7 us (47%)
  waiting for transfers between devices  30.7 us (21%)
  Pallas kernels  19 us (13%)
  blocking collectives  18.2 us (12%)
  local copies, waits for them, and re-layouts  6.21 us (4%)
  other arithmetic  1.5 us (1%)
  between operations  1.49 us (1%)
    ppermute x8, starting transfers between devices, moved(): return lax.ppermute(value, AXES, route)  21.2 us
    ppermute x8, waiting for transfers between devices, moved(): return lax.ppermute(value, AXES, route)  18.7 us
    all_to_all x1, blocking collectives, z_exchange(): lax.all_to_all(chunks, AXES, 0, 0, tiled=True, axis_index_groups=groups)  18.2 us
    ppermute x1, starting transfers between devices, halos_in(): lax.ppermute(jnp.where(first, relayed, below0), 'col', plain + [(0, seam...  17.3 us
    ppermute x5, starting transfers between devices, shifted(): return lax.ppermute(block, axis, route)  11.8 us
    pallas_call x1, Pallas kernels, slot_terms(): pl.pallas_call(functools.partial(slots_kernel, w, t), out_shape=[f32((2,...  10.3 us
    all_to_all x1, waiting for transfers between devices, z_exchange(): lax.all_to_all(chunks, AXES, 0, 0, tiled=True, axis_index_groups=groups)  8.6 us
    all_to_all x1, starting transfers between devices, z_exchange(): lax.all_to_all(chunks, AXES, 0, 0, tiled=True, axis_index_groups=groups)  6.43 us
  transfers between devices with their start and end apart: 21, of which 9 were waited for; matrix products, arithmetic and copies ran while one was open for 1% of the time, Pallas kernels for 4%

commit v1 on v0

--- a/solution.py
+++ b/solution.py
@@ -66,8 +66,8 @@
 
 def slots_kernel(
     window, tile,
-    counts_ref, pos_ref, place_ref, object_hbm, right_hbm, below0_hbm, below1_hbm, corner_hbm,
-    seam_right_hbm, seam_corner_hbm, probe_hbm, amp_hbm, tables_hbm,
+    counts_ref, pos_ref, place_ref, object_hbm, right0_hbm, right1_hbm, below0_hbm, below1_hbm,
+    corner_hbm, probe_hbm, amp_hbm, tables_hbm,
     tile_out, right_out, below0_out, below1_out, corner_out, keep_out, send_out,
     ext, grad, probe, turned, amp, tables, patch, probe_grad, sems,
 ):
@@ -80,6 +80,7 @@
         (tables_hbm, tables),
         (amp_hbm, amp),
         (object_hbm, ext.at[:, 0:t, 0:t]),
+        (right0_hbm, ext.at[:, 0:w, t:e]),
         (below0_hbm, ext.at[:, t:e, 0:w]),
         (below1_hbm, ext.at[:, t:e, w:t]),
     ]
@@ -88,12 +89,11 @@
         copy.start()
 
     def choose(act):
-        sources = [(right_hbm.at[:, 0:w], right_hbm.at[:, w:t], corner_hbm), (seam_right_hbm, corner_hbm, seam_corner_hbm)]
-        for flag, parts in enumerate(sources):
+        for flag, parts in enumerate([(right1_hbm, corner_hbm), (corner_hbm, right1_hbm)]):
             @pl.when(at_seam == flag)
             def _():
                 for i, part in enumerate(parts):
-                    act(pltpu.make_async_copy(part, ext.at[:, i * w : i * w + w, t:e], sems.at[6 + i]))
+                    act(pltpu.make_async_copy(part, ext.at[:, (i + 1) * w : (i + 2) * w, t:e], sems.at[7 + i]))
 
     choose(lambda copy: copy.start())
     grad[...] = jnp.zeros_like(grad)
@@ -181,7 +181,7 @@
     return pl.pallas_call(
         functools.partial(slots_kernel, w, t),
         out_shape=[f32((2, t, t)), f32((2, t, w)), block, block, block, f32((w, w)), f32((w, w))],
-        in_specs=[SMEM] * 3 + [HBM] * 10,
+        in_specs=[SMEM] * 3 + [HBM] * 9,
         out_specs=[HBM] * 7,
         scratch_shapes=[
             pltpu.VMEM((2, t + w, t + w), jnp.float32),
@@ -200,41 +200,60 @@
     )(counts, positions, where, object_field, *halos, probe, amplitudes, jnp.asarray(dft_tables(w)))
 
 
-def combine_kernel(half, tile_ref, left_ref, seam_ref, above0_ref, above1_ref, out_ref):
-    w = left_ref.shape[2]
-    first, second = tile_ref[:, :, :w] + (left_ref[...] + seam_ref[...]), tile_ref[:, :, w:]
-
-    @pl.when(pl.program_id(0) < half)
-    def _():
-        out_ref[:, :, :w] = first + above0_ref[...]
-        out_ref[:, :, w:] = second + above1_ref[...]
-
-    @pl.when(pl.program_id(0) >= half)
-    def _():
-        out_ref[:, :, :w] = first
-        out_ref[:, :, w:] = second
-
-
-def combined(tile_grad, from_left, from_seam, above0, above1):
+def combine_kernel(
+    window, place_ref, tile_hbm, left_hbm, seam_hbm, above0_hbm, above1_hbm, out_hbm, tile, side, above0, above1, sems
+):
+    w, t = window, tile.shape[1]
+    after_seam = place_ref[2]
+    mine = [
+        pltpu.make_async_copy(tile_hbm.at[:, 0:w, :], tile.at[:, 0:w, :], sems.at[0]),
+        pltpu.make_async_copy(tile_hbm.at[:, w:t, 0:w], tile.at[:, w:t, 0:w], sems.at[1]),
+        pltpu.make_async_copy(above0_hbm, above0, sems.at[2]),
+        pltpu.make_async_copy(above1_hbm, above1, sems.at[3]),
+    ]
+    for copy in mine:
+        copy.start()
+
+    def choose(act):
+        for flag, source in enumerate((left_hbm, seam_hbm)):
+            @pl.when(after_seam == flag)
+            def _():
+                act(pltpu.make_async_copy(source, side, sems.at[4]))
+
+    choose(lambda copy: copy.start())
+    for copy in mine:
+        copy.wait()
+    tile[:, 0:w, w:t] += above1[...]
+    choose(lambda copy: copy.wait())
+    tile[:, 0:w, 0:w] += above0[...] + side[:, 0:w]
+    top = pltpu.make_async_copy(tile.at[:, 0:w, :], out_hbm.at[:, 0:w, :], sems.at[0])
+    top.start()
+    tile[:, w:t, 0:w] += side[:, w:t]
+    low = pltpu.make_async_copy(tile.at[:, w:t, 0:w], out_hbm.at[:, w:t, 0:w], sems.at[1])
+    low.start()
+    top.wait()
+    low.wait()
+
+
+def combined(where, tile_grad, from_left, from_seam, above0, above1):
     t, w = tile_grad.shape[1], from_left.shape[2]
-    step = w // 4
-    half = w // step
-    above = pl.BlockSpec((2, step, w), lambda i: (0, jnp.minimum(i, half - 1), 0))
     return pl.pallas_call(
-        functools.partial(combine_kernel, half),
+        functools.partial(combine_kernel, w),
         out_shape=jax.ShapeDtypeStruct(tile_grad.shape, jnp.float32),
-        grid=(t // step,),
-        in_specs=[
-            pl.BlockSpec((2, step, t), lambda i: (0, i, 0)),
-            pl.BlockSpec((2, step, w), lambda i: (0, i, 0)),
-            pl.BlockSpec((2, step, w), lambda i: (0, i, 0)),
-            above,
-            above,
+        in_specs=[SMEM] + [HBM] * 5,
+        out_specs=HBM,
+        scratch_shapes=[
+            pltpu.VMEM((2, t, t), jnp.float32),
+            pltpu.VMEM((2, t, w), jnp.float32),
+            pltpu.VMEM((2, w, w), jnp.float32),
+            pltpu.VMEM((2, w, w), jnp.float32),
+            pltpu.SemaphoreType.DMA((5,)),
         ],
-        out_specs=pl.BlockSpec((2, step, t), lambda i: (0, i, 0)),
+        input_output_aliases={1: 0},
+        compiler_params=pltpu.CompilerParams(vmem_limit_bytes=12 * MIB),
         cost_estimate=pl.CostEstimate(flops=10**6, bytes_accessed=6 * MIB, transcendentals=0),
         name="combined",
-    )(tile_grad, from_left, from_seam, above0, above1)
+    )(where, tile_grad, from_left, from_seam, above0, above1)
 
 
 def place(x, y, z, core):
@@ -292,62 +311,58 @@
     return lax.all_to_all(chunks, AXES, 0, 0, tiled=True, axis_index_groups=groups)
 
 
-def total(value, above1, from_left, above0):
-    w = value.shape[0]
-    core = lax.axis_index("col") % 2
-    value = z_exchange(value.reshape(8, w // 8, w))
-    value = added([[value]])[0]
-    value, above0, above1 = summed(value, "x", above0, above1)
-    value, from_left = summed(value, "y", from_left)
-    value = z_exchange(jnp.broadcast_to(value, (8,) + value.shape)).reshape(w, w)
-    other = moved(value, core=1)
-    planes = jnp.where(core == 0, jnp.stack([value, other]), jnp.stack([other, value]))
-    return planes, (above1, from_left, above0)
-
-
 def halos_in(object_field, window):
     rows, cols = lax.axis_size("row"), lax.axis_size("col")
+    col = lax.axis_index("col")
     seam = cols // 2
     w = window
-    own0 = object_field[:, :w, :w]
+    own0, own1 = object_field[:, :w, :w], object_field[:, w:, :w]
     plain = [(i + 1, i) for i in range(cols - 1) if i + 1 != seam]
     below0 = shifted(own0, "row", -1)
     below1 = shifted(object_field[:, :w, w:], "row", -1)
-    right = lax.ppermute(object_field[:, :, :w], "col", plain)
-    relayed = lax.ppermute(object_field[:, w:, :w], "col", [(seam, 0)])
-    seam_right = lax.ppermute(own0, "col", [(seam, seam - 1)])
-    route = [((r + 1) * cols + seam, r * cols + seam - 1) for r in range(rows - 1)]
-    seam_corner = lax.ppermute(own0, AXES, route)
-    first = lax.axis_index("col") == 0
-    corner = lax.ppermute(jnp.where(first, relayed, below0), "col", plain + [(0, seam - 1)])
-    return right, below0, below1, corner, seam_right, seam_corner
+    relayed = lax.ppermute(own1, "col", [(seam, 0)])
+    right0 = shifted(own0, "col", -1)
+    route = [(r * cols + a, r * cols + b) for r in range(rows) for a, b in plain]
+    route += [((r + 1) * cols + seam, r * cols + seam - 1) for r in range(rows - 1)]
+    right1 = lax.ppermute(jnp.where(col == seam, own0, own1), AXES, route)
+    corner = lax.ppermute(jnp.where(col == 0, relayed, below0), "col", plain + [(0, seam - 1)])
+    return right0, right1, below0, below1, corner
 
 
 def shards(object_field, probe, positions, amplitudes, counts):
     window = probe.shape[1]
     col = lax.axis_index("col")
     core = col % 2
-    at_seam = (col == lax.axis_size("col") // 2 - 1).astype(jnp.int32)
+    seam = lax.axis_size("col") // 2
     halos = halos_in(object_field, window)
-    where = jnp.stack([core, at_seam])
+    where = jnp.stack([core, (col == seam - 1).astype(jnp.int32), (col == seam).astype(jnp.int32)])
     tile_grad, right_grad, below0_grad, below1_grad, corner_grad, keep, send = slot_terms(
         counts, positions, where, object_field, halos, probe, amplitudes
     )
     corner_in = shifted(corner_grad, "col", 1)
     above1 = shifted(below1_grad, "row", 1)
     rows, cols = lax.axis_size("row"), lax.axis_size("col")
-    staged = (rows, cols) == (16, 16)
-    other = moved(send, core=1) if staged else send
-    value, below0_grad, right_grad = added([[keep, other], [below0_grad, corner_in]], right_grad, vmem=60)
-    above0 = shifted(below0_grad, "row", 1)
-    plain = [(i, i + 1) for i in range(cols - 1) if i + 1 != cols // 2]
-    from_left = lax.ppermute(right_grad, "col", plain)
-    from_seam = lax.ppermute(right_grad, "col", [(cols // 2 - 1, cols // 2)])
-    if staged:
-        probe_total, (above1, from_left, above0) = total(value, above1, from_left, above0)
+    plain = [(i, i + 1) for i in range(cols - 1) if i + 1 != seam]
+
+    def halos_out(below0_grad, right_grad):
+        above0 = shifted(below0_grad, "row", 1)
+        from_left = lax.ppermute(right_grad, "col", plain)
+        return above0, from_left, lax.ppermute(right_grad, "col", [(seam - 1, seam)])
+
+    if (rows, cols) == (16, 16):
+        value = keep + moved(send, core=1)
+        value = z_exchange(value.reshape(8, window // 8, window))
+        value, below0_grad, right_grad, above1 = added([[value], [below0_grad, corner_in]], right_grad, above1, vmem=8)
+        above0, from_left, from_seam = halos_out(below0_grad, right_grad)
+        value = summed(value, "x")[0]
+        value, above0, from_left, from_seam = summed(value, "y", above0, from_left, from_seam)
+        value = z_exchange(jnp.broadcast_to(value, (8,) + value.shape)).reshape(window, window)
+        other = moved(value, core=1)
+        probe_total = jnp.where(core == 0, jnp.stack([value, other]), jnp.stack([other, value]))
     else:
+        above0, from_left, from_seam = halos_out(below0_grad + corner_in, right_grad)
         probe_total = lax.psum(jnp.where(core == 0, jnp.stack([keep, send]), jnp.stack([send, keep])), AXES)
-    return combined(tile_grad, from_left, from_seam, above0, above1), probe_total
+    return combined(where, tile_grad, from_left, from_seam, above0, above1), probe_total
 
 
 def solution(mesh):

time: 146 us -> 139 us (0.952); the launches traced: 146 us -> 137 us
  starting transfers between devices: 68.7 us -> 55.5 us
  waiting for transfers between devices: 30.7 us -> 35.8 us
  other arithmetic: 1.5 us -> 5.83 us
  local copies, waits for them, and re-layouts: 6.21 us -> 3.08 us
    ppermute x8, starting transfers between devices: 21.2 us -> 7.69 us  [moved(): return lax.ppermute(value, AXES, route)]
    ppermute x5 -> x6, waiting for transfers between devices: 3.18 us -> 15.7 us  [shifted(): return lax.ppermute(block, axis, route)]
    ppermute x5 -> x6, starting transfers between devices: 11.8 us -> 19.9 us  [shifted(): return lax.ppermute(block, axis, route)]
    all_to_all x1, waiting for transfers between devices: 8.6 us -> 0.95 us  [z_exchange(): lax.all_to_all(chunks, AXES, 0, 0, tiled=True, axis_index_groups=groups)]
    ppermute x7 -> x5, starting transfers between devices: 29.3 us -> 24 us  [the longest x1 17.3 us: halos_in(): lax.ppermute(jnp.where(col == 0, relayed, below0), 'col', plain + [(0, se...]
    pallas_call x1, Pallas kernels: 10.3 us -> 14.9 us  [slot_terms(): pl.pallas_call(functools.partial(slots_kernel, w, t), out_shape=[f32((2,...]
    pallas_call x1, Pallas kernels: 6.34 us -> 3.24 us  [combined(): pl.pallas_call(functools.partial(combine_kernel, w), out_shape=jax.ShapeD...]
    all_to_all x1, starting transfers between devices: 6.43 us -> 3.83 us  [z_exchange(): lax.all_to_all(chunks, AXES, 0, 0, tiled=True, axis_index_groups=groups)]
  transfers between devices with their start and end apart: 21 -> 20, of which waited for: 9 -> 9; matrix products, arithmetic and copies ran while one was open for 1% -> 2% of each run, Pallas kernels for 4% -> 2%
where the time goes in v1:
time: 139 us; the launch traced here: 137 us
  starting transfers between devices  55.5 us (40%)
  waiting for transfers between devices  35.8 us (26%)
  Pallas kernels  18.2 us (13%)
  blocking collectives  17.3 us (12%)
  other arithmetic  5.83 us (4%)
  local copies, waits for them, and re-layouts  3.08 us (2%)
  between operations  1.53 us (1%)
    ppermute x6, starting transfers between devices, shifted(): return lax.ppermute(block, axis, route)  19.9 us
    ppermute x8, waiting for transfers between devices, moved(): return lax.ppermute(value, AXES, route)  19 us
    ppermute x1, starting transfers between devices, halos_in(): lax.ppermute(jnp.where(col == 0, relayed, below0), 'col', plain + [(0, se...  17.3 us
    all_to_all x1, blocking collectives, z_exchange(): lax.all_to_all(chunks, AXES, 0, 0, tiled=True, axis_index_groups=groups)  17.3 us
    ppermute x6, waiting for transfers between devices, shifted(): return lax.ppermute(block, axis, route)  15.7 us
    pallas_call x1, Pallas kernels, slot_terms(): pl.pallas_call(functools.partial(slots_kernel, w, t), out_shape=[f32((2,...  14.9 us
    ppermute x8, starting transfers between devices, moved(): return lax.ppermute(value, AXES, route)  7.69 us
    all_to_all x1, starting transfers between devices, z_exchange(): lax.all_to_all(chunks, AXES, 0, 0, tiled=True, axis_index_groups=groups)  3.83 us
  transfers between devices with their start and end apart: 20, of which 9 were waited for; matrix products, arithmetic and copies ran while one was open for 2% of the time, Pallas kernels for 2%

profile of v1, /device:TPU:1, one launch (start us, length us, event | category | flops | bytes accessed | tf_op | source)
XLA Modules:
  0.0 137.2 jit_solution(4441673075633615434)
XLA Ops:
  0.6 1.6 %fusion = (f32[2,256,256]{2,1,0:T(8,128)S(1)}, f32[2,256,256]{2,1,0:T(8,128)S(1)}, f32[2,256,256]{2,1,0:T(8,128)S(1)}, f32[2,256,256]{2,1,0:T(8,128)S(1)}) fusion(f32[2,512,512]{2,1,0:T(8,128)} %object_hbm.1, pred[]{:T(512)S(6)} %eq.16), kind=kLoop, calls=%fused_computation.4 | loop fusion | flops 131072 | bytes 3670017 | tf_op jit(solution)/shard_map/slice | solution.py:319
  2.9 1.3 collective-permute-start.2
  4.2 5.7 %collective-permute-start = (f32[2,256,256]{2,1,0:T(8,128)S(1)}, f32[2,256,256]{2,1,0:T(8,128)}, u32[]{:S(2)}, u32[]{:S(2)}) collective-permute-start(f32[2,256,256]{2,1,0:T(8,128)S(1)} %get-tuple-element.34), channel_id=1, source_target_pairs={{1,0},{2,1},{3,2},{4,3},{5,4},{6,5},{7,6},{8,7},{9,8},{10,9},{11,1... | collective-permute-start | bytes 1572872 | tf_op jit(solution)/shard_map/ppermute | solution.py:24
  10.0 1.9 %collective-permute-start.1 = (f32[2,256,256]{2,1,0:T(8,128)S(1)}, f32[2,256,256]{2,1,0:T(8,128)}, u32[]{:S(2)}, u32[]{:S(2)}) collective-permute-start(f32[2,256,256]{2,1,0:T(8,128)S(1)} %get-tuple-element.33), channel_id=1, source_target_pairs={{1,0},{2,1},{3,2},{4,3},{5,4},{6,5},{7,6},{9,8},{10,9},{11,10},{12... | collective-permute-start | bytes 1572872 | tf_op jit(solution)/shard_map/ppermute | solution.py:327
  13.2 4.2 %collective-permute-done.2.below0_hbm = f32[2,256,256]{2,1,0:T(8,128)S(1)} collective-permute-done((f32[2,256,256]{2,1,0:T(8,128)S(1)}, f32[2,256,256]{2,1,0:T(8,128)S(1)}, u32[]{:S(2)}, u32[]{:S(2)}) %collective-permute-start.2) | collective-permute-done | bytes 524320 | tf_op jit(solution)/shard_map/ppermute | solution.py:24
  17.5 17.3 %collective-permute-start.5 = (f32[2,256,256]{2,1,0:T(8,128)S(1)}, f32[2,256,256]{2,1,0:T(8,128)S(1)}, u32[]{:S(2)}, u32[]{:S(2)}) collective-permute-start(f32[2,256,256]{2,1,0:T(8,128)S(1)} %broadcast_select_fusion), channel_id=1, source_target_pairs={{1,0},{2,1},{3,2},{4,3},{5,4},{6,5},{7,6},{9,8},{10,9},{11,10},{12... | collective-permute-start | bytes 1572872 | tf_op jit(solution)/shard_map/ppermute | solution.py:328
  37.2 14.9 %slot_terms.1 = (f32[2,512,512]{2,1,0:T(8,128)}, f32[2,512,256]{2,1,0:T(8,128)}, f32[2,256,256]{2,1,0:T(8,128)}, f32[2,256,256]{2,1,0:T(8,128)}, f32[2,256,256]{...) custom-call(s32[1]{0:T(128)S(6)} %copy.20.counts_ref, s32[2,2]{1,0:T(2,128)} %pos_ref.1, s32[3]{0:T(128)} %pad_add_fusion.place_ref, ...), custom_call_target="tpu_custom_call" | custom-call | flops 3000000000 | bytes 14680064 | tf_op jit(solution)/shard_map/slot_terms/pallas_call | solution.py:181
  52.1 5.3 %collective-permute-start.6 = (f32[256,256]{1,0:T(8,128)}, f32[256,256]{1,0:T(8,128)S(1)}, u32[]{:S(2)}, u32[]{:S(2)}) collective-permute-start(f32[256,256]{1,0:T(8,128)} %get-tuple-element.19), channel_id=1, source_target_pairs={{0,1},{1,0},{32,33},{33,32},{64,65},{65,64},{96,97},{97,96},{128,1... | collective-permute-start | bytes 786440 | tf_op jit(solution)/shard_map/ppermute | solution.py:274
  57.3 1.9 %collective-permute-start.7 = (f32[2,256,256]{2,1,0:T(8,128)}, f32[2,256,256]{2,1,0:T(8,128)S(1)}, u32[]{:S(2)}, u32[]{:S(2)}) collective-permute-start(f32[2,256,256]{2,1,0:T(8,128)} %get-tuple-element.21), channel_id=1, source_target_pairs={{0,1},{1,2},{2,3},{3,4},{4,5},{5,6},{6,7},{7,8},{8,9},{9,10},{10,1... | collective-permute-start | bytes 1572872 | tf_op jit(solution)/shard_map/ppermute | solution.py:24
  59.2 1.3 collective-permute-start.8
  60.6 1.7 %add.8 = f32[256,256]{1,0:T(8,128)} add(f32[256,256]{1,0:T(8,128)} %get-tuple-element.18, f32[256,256]{1,0:T(8,128)S(1)} %collective-permute-done.6) | non-fusion elementwise | flops 65536 | bytes 786432 | tf_op jit(solution)/shard_map/add | solution.py:353
  62.3 3.8 %all-to-all-start = ((f32[8,32,256]{2,1,0:T(8,128)}), f32[8,32,256]{2,1,0:T(8,128)S(1)}, u32[]{:S(2)}, u32[]{:S(2)}) async-start(f32[8,32,256]{2,1,0:T(8,128)} %bitcast.3), calls=%async_computation | async-start | bytes 524288 | tf_op jit(solution)/shard_map/all_to_all | solution.py:311
  66.1 11.4 %collective-permute-done.8.refs_4_ = f32[2,256,256]{2,1,0:T(8,128)S(1)} collective-permute-done((f32[2,256,256]{2,1,0:T(8,128)}, f32[2,256,256]{2,1,0:T(8,128)S(1)}, u32[]{:S(2)}, u32[]{:S(2)}) %collective-permute-start.8) | collective-permute-done | bytes 524320 | tf_op jit(solution)/shard_map/ppermute | solution.py:24
  81.6 3.3 %collective-permute-start.16 = (f32[2,512,256]{2,1,0:T(8,128)S(1)}, f32[2,512,256]{2,1,0:T(8,128)S(1)}, u32[]{:S(2)}, u32[]{:S(2)}) collective-permute-start(f32[2,512,256]{2,1,0:T(8,128)S(1)} %get-tuple-element.26), channel_id=1, source_target_pairs={{0,1},{1,2},{2,3},{3,4},{4,5},{5,6},{6,7},{8,9},{9,10},{10,11},{11... | collective-permute-start | bytes 3145736 | tf_op jit(solution)/shard_map/ppermute | solution.py:349
  84.9 8.4 %collective-permute-start.15 = (f32[2,256,256]{2,1,0:T(8,128)S(1)}, f32[2,256,256]{2,1,0:T(8,128)S(1)}, u32[]{:S(2)}, u32[]{:S(2)}) collective-permute-start(f32[2,256,256]{2,1,0:T(8,128)S(1)} %get-tuple-element.25), channel_id=1, source_target_pairs={{0,16},{16,32},{32,48},{48,64},{64,80},{80,96},{96,112},{112,128},... | collective-permute-start | bytes 1572872 | tf_op jit(solution)/shard_map/ppermute | solution.py:24
  93.5 2.7 %collective-permute-done.11.refs_3_ = f32[32,256]{1,0:T(8,128)S(1)} collective-permute-done((f32[32,256]{1,0:T(8,128)S(1)}, f32[32,256]{1,0:T(8,128)S(1)}, u32[]{:S(2)}, u32[]{:S(2)}) %collective-permute-start.11) | collective-permute-done | bytes 32800 | tf_op jit(solution)/shard_map/ppermute | solution.py:274
  96.1 8.9 %collective-permute-done.10.refs_2_ = f32[32,256]{1,0:T(8,128)S(1)} collective-permute-done((f32[32,256]{1,0:T(8,128)S(1)}, f32[32,256]{1,0:T(8,128)S(1)}, u32[]{:S(2)}, u32[]{:S(2)}) %collective-permute-start.10) | collective-permute-done | bytes 32800 | tf_op jit(solution)/shard_map/ppermute | solution.py:274
  105.2 2.9 %collective-permute-done.14.refs_3_ = f32[32,256]{1,0:T(8,128)S(1)} collective-permute-done((f32[32,256]{1,0:T(8,128)S(1)}, f32[32,256]{1,0:T(8,128)S(1)}, u32[]{:S(2)}, u32[]{:S(2)}) %collective-permute-start.14) | collective-permute-done | bytes 32800 | tf_op jit(solution)/shard_map/ppermute | solution.py:274
  108.1 2.1 %collective-permute-done.13.refs_2_ = f32[32,256]{1,0:T(8,128)S(1)} collective-permute-done((f32[32,256]{1,0:T(8,128)S(1)}, f32[32,256]{1,0:T(8,128)S(1)}, u32[]{:S(2)}, u32[]{:S(2)}) %collective-permute-start.13) | collective-permute-done | bytes 32800 | tf_op jit(solution)/shard_map/ppermute | solution.py:274
  110.2 2.4 %collective-permute-done.12.refs_1_ = f32[32,256]{1,0:T(8,128)S(1)} collective-permute-done((f32[32,256]{1,0:T(8,128)S(1)}, f32[32,256]{1,0:T(8,128)S(1)}, u32[]{:S(2)}, u32[]{:S(2)}) %collective-permute-start.12) | collective-permute-done | bytes 32800 | tf_op jit(solution)/shard_map/ppermute | solution.py:274
  112.7 17.3 %all_to_all.10 = f32[8,32,256]{2,1,0:T(8,128)S(1)} all-to-all(f32[8,32,256]{2,1,0:T(8,128)S(1)} %broadcast_in_dim.3), channel_id=1, replica_groups={{0,32,64,96,128,160,192,224},{1,33,65,97,129,161,193,225},{8,40,72,104,..., dimensions={0} | all-to-all | bytes 524288 | tf_op jit(solution)/shard_map/all_to_all | solution.py:311
  130.0 2.1 %collective-permute-start.18 = (f32[256,256]{1,0:T(8,128)S(1)}, f32[256,256]{1,0:T(8,128)}, u32[]{:S(2)}, u32[]{:S(2)}) collective-permute-start(f32[256,256]{1,0:T(8,128)S(1)} %bitcast.7), channel_id=1, source_target_pairs={{0,1},{1,0},{32,33},{33,32},{64,65},{65,64},{96,97},{97,96},{128,1... | collective-permute-start | bytes 786440 | tf_op jit(solution)/shard_map/ppermute | solution.py:274
  132.1 3.2 %combined.1 = f32[2,512,512]{2,1,0:T(8,128)} custom-call(s32[3]{0:T(128)S(1)} %copy-done.2, f32[2,512,512]{2,1,0:T(8,128)} %get-tuple-element.17.tile_hbm, f32[2,512,256]{2,1,0:T(8,128)S(1)} %get-tuple-element.27.left_hbm, f32[2,512,256]{2,1,0:T(8,128)S(1)} %get-tuple-element.28.seam_hbm, ...), custom_call_target="tpu_custom_call", output_to_operand_aliasing={{}: (1, {})} | custom-call | flops 1000000 | bytes 6291456 | tf_op jit(solution)/shard_map/combined/pallas_call | solution.py:240
  135.3 1.9 %maximum_select_fusion = f32[2,256,256]{2,1,0:T(8,128)} fusion(f32[1,256,256]{2,1,0:T(8,128)} %bitcast.6, f32[1,256,256]{2,1,0:T(8,128)S(1)} %bitcast.8, pred[]{:T(512)S(6)} %eq.18), kind=kLoop, calls=%fused_computation | loop fusion | flops 393216 | bytes 1048577 | tf_op jit(solution)/shard_map/jit(_where)/select_n | solution.py:361
  (38 shorter events, 8.1 us)
Async XLA Ops:
  2.2 11.0 %collective-permute-start.4 = (f32[2,256,256]{2,1,0:T(8,128)S(1)}, f32[2,256,256]{2,1,0:T(8,128)S(1)}, u32[]{:S(2)}, u32[]{:S(2)}) collective-permute-start(f32[2,256,256]{2,1,0:T(8,128)S(1)} %get-tuple-element.32), channel_id=1, source_target_pairs={{8,0},{24,16},{40,32},{56,48},{72,64},{88,80},{104,96},{120,112},{... | collective-permute-start | bytes 1572872 | tf_op jit(solution)/shard_map/ppermute | solution.py:323
  2.9 14.5 %collective-permute-start.2 = (f32[2,256,256]{2,1,0:T(8,128)S(1)}, f32[2,256,256]{2,1,0:T(8,128)S(1)}, u32[]{:S(2)}, u32[]{:S(2)}) collective-permute-start(f32[2,256,256]{2,1,0:T(8,128)S(1)} %get-tuple-element.34), channel_id=1, source_target_pairs={{16,0},{32,16},{48,32},{64,48},{80,64},{96,80},{112,96},{128,112},... | collective-permute-start | bytes 1572872 | tf_op jit(solution)/shard_map/ppermute | solution.py:24
  4.2 31.9 %collective-permute-start = (f32[2,256,256]{2,1,0:T(8,128)S(1)}, f32[2,256,256]{2,1,0:T(8,128)}, u32[]{:S(2)}, u32[]{:S(2)}) collective-permute-start(f32[2,256,256]{2,1,0:T(8,128)S(1)} %get-tuple-element.34), channel_id=1, source_target_pairs={{1,0},{2,1},{3,2},{4,3},{5,4},{6,5},{7,6},{8,7},{9,8},{10,9},{11,1... | collective-permute-start | bytes 1572872 | tf_op jit(solution)/shard_map/ppermute | solution.py:24
  10.0 26.2 %collective-permute-start.1 = (f32[2,256,256]{2,1,0:T(8,128)S(1)}, f32[2,256,256]{2,1,0:T(8,128)}, u32[]{:S(2)}, u32[]{:S(2)}) collective-permute-start(f32[2,256,256]{2,1,0:T(8,128)S(1)} %get-tuple-element.33), channel_id=1, source_target_pairs={{1,0},{2,1},{3,2},{4,3},{5,4},{6,5},{7,6},{9,8},{10,9},{11,10},{12... | collective-permute-start | bytes 1572872 | tf_op jit(solution)/shard_map/ppermute | solution.py:327
  11.9 24.3 %collective-permute-start.3 = (f32[2,256,256]{2,1,0:T(8,128)S(1)}, f32[2,256,256]{2,1,0:T(8,128)}, u32[]{:S(2)}, u32[]{:S(2)}) collective-permute-start(f32[2,256,256]{2,1,0:T(8,128)S(1)} %get-tuple-element.35), channel_id=1, source_target_pairs={{16,0},{32,16},{48,32},{64,48},{80,64},{96,80},{112,96},{128,112},... | collective-permute-start | bytes 1572872 | tf_op jit(solution)/shard_map/ppermute | solution.py:24
  17.5 18.9 %copy-start.3 = (f32[2,256,256]{2,1,0:T(8,128)}, f32[2,256,256]{2,1,0:T(8,128)S(1)}, u32[]{:S(2)}) copy-start(f32[2,256,256]{2,1,0:T(8,128)S(1)} %collective-permute-done.2.below0_hbm) | copy-start | bytes 1572868
  17.5 18.8 %collective-permute-start.5 = (f32[2,256,256]{2,1,0:T(8,128)S(1)}, f32[2,256,256]{2,1,0:T(8,128)S(1)}, u32[]{:S(2)}, u32[]{:S(2)}) collective-permute-start(f32[2,256,256]{2,1,0:T(8,128)S(1)} %broadcast_select_fusion), channel_id=1, source_target_pairs={{1,0},{2,1},{3,2},{4,3},{5,4},{6,5},{7,6},{9,8},{10,9},{11,10},{12... | collective-permute-start | bytes 1572872 | tf_op jit(solution)/shard_map/ppermute | solution.py:328
  52.1 8.5 %collective-permute-start.6 = (f32[256,256]{1,0:T(8,128)}, f32[256,256]{1,0:T(8,128)S(1)}, u32[]{:S(2)}, u32[]{:S(2)}) collective-permute-start(f32[256,256]{1,0:T(8,128)} %get-tuple-element.19), channel_id=1, source_target_pairs={{0,1},{1,0},{32,33},{33,32},{64,65},{65,64},{96,97},{97,96},{128,1... | collective-permute-start | bytes 786440 | tf_op jit(solution)/shard_map/ppermute | solution.py:274
  57.3 8.8 %collective-permute-start.7 = (f32[2,256,256]{2,1,0:T(8,128)}, f32[2,256,256]{2,1,0:T(8,128)S(1)}, u32[]{:S(2)}, u32[]{:S(2)}) collective-permute-start(f32[2,256,256]{2,1,0:T(8,128)} %get-tuple-element.21), channel_id=1, source_target_pairs={{0,1},{1,2},{2,3},{3,4},{4,5},{5,6},{6,7},{7,8},{8,9},{9,10},{10,1... | collective-permute-start | bytes 1572872 | tf_op jit(solution)/shard_map/ppermute | solution.py:24
  59.2 18.3 %collective-permute-start.8 = (f32[2,256,256]{2,1,0:T(8,128)}, f32[2,256,256]{2,1,0:T(8,128)S(1)}, u32[]{:S(2)}, u32[]{:S(2)}) collective-permute-start(f32[2,256,256]{2,1,0:T(8,128)} %get-tuple-element.23), channel_id=1, source_target_pairs={{0,16},{16,32},{32,48},{48,64},{64,80},{80,96},{96,112},{112,128},... | collective-permute-start | bytes 1572872 | tf_op jit(solution)/shard_map/ppermute | solution.py:24
  62.3 16.2 %all-to-all-start = ((f32[8,32,256]{2,1,0:T(8,128)}), f32[8,32,256]{2,1,0:T(8,128)S(1)}, u32[]{:S(2)}, u32[]{:S(2)}) async-start(f32[8,32,256]{2,1,0:T(8,128)} %bitcast.3), calls=%async_computation | async-start | bytes 524288 | tf_op jit(solution)/shard_map/all_to_all | solution.py:311
  78.5 1.2 copy-start
  79.7 1.0 copy-start.1
  80.8 51.3 %copy-start.2 = (s32[3]{0:T(128)S(1)}, s32[3]{0:T(128)}, u32[]{:S(2)}) copy-start(s32[3]{0:T(128)} %pad_add_fusion.place_ref) | copy-start | bytes 40
  80.8 31.8 %collective-permute-start.17 = (f32[2,512,256]{2,1,0:T(8,128)S(1)}, f32[2,512,256]{2,1,0:T(8,128)S(1)}, u32[]{:S(2)}, u32[]{:S(2)}) collective-permute-start(f32[2,512,256]{2,1,0:T(8,128)S(1)} %get-tuple-element.26), channel_id=1, source_target_pairs={{7,8},{23,24},{39,40},{55,56},{71,72},{87,88},{103,104},{119,120},... | collective-permute-start | bytes 3145736 | tf_op jit(solution)/shard_map/ppermute | solution.py:350
  81.6 31.1 %collective-permute-start.16 = (f32[2,512,256]{2,1,0:T(8,128)S(1)}, f32[2,512,256]{2,1,0:T(8,128)S(1)}, u32[]{:S(2)}, u32[]{:S(2)}) collective-permute-start(f32[2,512,256]{2,1,0:T(8,128)S(1)} %get-tuple-element.26), channel_id=1, source_target_pairs={{0,1},{1,2},{2,3},{3,4},{4,5},{5,6},{6,7},{8,9},{9,10},{10,11},{11... | collective-permute-start | bytes 3145736 | tf_op jit(solution)/shard_map/ppermute | solution.py:349
  84.9 27.8 %collective-permute-start.15 = (f32[2,256,256]{2,1,0:T(8,128)S(1)}, f32[2,256,256]{2,1,0:T(8,128)S(1)}, u32[]{:S(2)}, u32[]{:S(2)}) collective-permute-start(f32[2,256,256]{2,1,0:T(8,128)S(1)} %get-tuple-element.25), channel_id=1, source_target_pairs={{0,16},{16,32},{32,48},{48,64},{64,80},{80,96},{96,112},{112,128},... | collective-permute-start | bytes 1572872 | tf_op jit(solution)/shard_map/ppermute | solution.py:24
  93.3 2.8 %collective-permute-start.11 = (f32[32,256]{1,0:T(8,128)S(1)}, f32[32,256]{1,0:T(8,128)S(1)}, u32[]{:S(2)}, u32[]{:S(2)}) collective-permute-start(f32[32,256]{1,0:T(8,128)S(1)} %get-tuple-element.24.refs_0_), channel_id=1, source_target_pairs={{0,6},{1,7},{32,38},{33,39},{64,70},{65,71},{96,102},{97,103},{128... | collective-permute-start | bytes 98312 | tf_op jit(solution)/shard_map/ppermute | solution.py:274
  93.4 11.6 %collective-permute-start.10 = (f32[32,256]{1,0:T(8,128)S(1)}, f32[32,256]{1,0:T(8,128)S(1)}, u32[]{:S(2)}, u32[]{:S(2)}) collective-permute-start(f32[32,256]{1,0:T(8,128)S(1)} %get-tuple-element.24.refs_0_), channel_id=1, source_target_pairs={{0,4},{1,5},{32,36},{33,37},{64,68},{65,69},{96,100},{97,101},{128... | collective-permute-start | bytes 98312 | tf_op jit(solution)/shard_map/ppermute | solution.py:274
  96.1 8.9 %collective-permute-start.9 = (f32[32,256]{1,0:T(8,128)S(1)}, f32[32,256]{1,0:T(8,128)S(1)}, u32[]{:S(2)}, u32[]{:S(2)}) collective-permute-start(f32[32,256]{1,0:T(8,128)S(1)} %get-tuple-element.24.refs_0_), channel_id=1, source_target_pairs={{0,2},{1,3},{32,34},{33,35},{64,66},{65,67},{96,98},{97,99},{128,1... | collective-permute-start | bytes 98312 | tf_op jit(solution)/shard_map/ppermute | solution.py:274
  105.0 3.1 %collective-permute-start.14 = (f32[32,256]{1,0:T(8,128)S(1)}, f32[32,256]{1,0:T(8,128)S(1)}, u32[]{:S(2)}, u32[]{:S(2)}) collective-permute-start(f32[32,256]{1,0:T(8,128)S(1)} %added.4.refs_0_), channel_id=1, source_target_pairs={{0,24},{1,25},{32,56},{33,57},{64,88},{65,89},{96,120},{97,121},{1... | collective-permute-start | bytes 98312 | tf_op jit(solution)/shard_map/ppermute | solution.py:274
  105.1 5.1 %collective-permute-start.13 = (f32[32,256]{1,0:T(8,128)S(1)}, f32[32,256]{1,0:T(8,128)S(1)}, u32[]{:S(2)}, u32[]{:S(2)}) collective-permute-start(f32[32,256]{1,0:T(8,128)S(1)} %added.4.refs_0_), channel_id=1, source_target_pairs={{0,16},{1,17},{32,48},{33,49},{64,80},{65,81},{96,112},{97,113},{1... | collective-permute-start | bytes 98312 | tf_op jit(solution)/shard_map/ppermute | solution.py:274
  108.1 4.5 %collective-permute-start.12 = (f32[32,256]{1,0:T(8,128)S(1)}, f32[32,256]{1,0:T(8,128)S(1)}, u32[]{:S(2)}, u32[]{:S(2)}) collective-permute-start(f32[32,256]{1,0:T(8,128)S(1)} %added.4.refs_0_), channel_id=1, source_target_pairs={{0,8},{1,9},{32,40},{33,41},{64,72},{65,73},{96,104},{97,105},{128... | collective-permute-start | bytes 98312 | tf_op jit(solution)/shard_map/ppermute | solution.py:274
  130.0 5.3 %collective-permute-start.18 = (f32[256,256]{1,0:T(8,128)S(1)}, f32[256,256]{1,0:T(8,128)}, u32[]{:S(2)}, u32[]{:S(2)}) collective-permute-start(f32[256,256]{1,0:T(8,128)S(1)} %bitcast.7), channel_id=1, source_target_pairs={{0,1},{1,0},{32,33},{33,32},{64,65},{65,64},{96,97},{97,96},{128,1... | collective-permute-start | bytes 786440 | tf_op jit(solution)/shard_map/ppermute | solution.py:274
  (1 other events, 0.8 us)

commit v2 on v1

--- a/solution.py
+++ b/solution.py
@@ -301,9 +301,8 @@
     return result
 
 
-def summed(value, axis, *arrived):
-    parts = [moved(value, **{axis: d}) for d in range(1, SIZES[axis])]
-    return added([[value] + parts], *arrived)
+def neighbours(value, axis):
+    return [moved(value, **{axis: d}) for d in range(1, SIZES[axis])]
 
 
 def z_exchange(chunks):
@@ -344,23 +343,21 @@
     rows, cols = lax.axis_size("row"), lax.axis_size("col")
     plain = [(i, i + 1) for i in range(cols - 1) if i + 1 != seam]
 
-    def halos_out(below0_grad, right_grad):
-        above0 = shifted(below0_grad, "row", 1)
-        from_left = lax.ppermute(right_grad, "col", plain)
-        return above0, from_left, lax.ppermute(right_grad, "col", [(seam - 1, seam)])
-
+    from_left = lax.ppermute(right_grad, "col", plain)
+    from_seam = lax.ppermute(right_grad, "col", [(seam - 1, seam)])
     if (rows, cols) == (16, 16):
         value = keep + moved(send, core=1)
         value = z_exchange(value.reshape(8, window // 8, window))
-        value, below0_grad, right_grad, above1 = added([[value], [below0_grad, corner_in]], right_grad, above1, vmem=8)
-        above0, from_left, from_seam = halos_out(below0_grad, right_grad)
-        value = summed(value, "x")[0]
-        value, above0, from_left, from_seam = summed(value, "y", above0, from_left, from_seam)
+        value = added([[value]])[0]
+        parts = [value] + neighbours(value, "x")
+        value, below0_grad, above1, from_left = added([parts, [below0_grad, corner_in]], above1, from_left, vmem=8)
+        above0 = shifted(below0_grad, "row", 1)
+        value = added([[value] + neighbours(value, "y")])[0]
         value = z_exchange(jnp.broadcast_to(value, (8,) + value.shape)).reshape(window, window)
         other = moved(value, core=1)
         probe_total = jnp.where(core == 0, jnp.stack([value, other]), jnp.stack([other, value]))
     else:
-        above0, from_left, from_seam = halos_out(below0_grad + corner_in, right_grad)
+        above0 = shifted(below0_grad + corner_in, "row", 1)
         probe_total = lax.psum(jnp.where(core == 0, jnp.stack([keep, send]), jnp.stack([send, keep])), AXES)
     return combined(where, tile_grad, from_left, from_seam, above0, above1), probe_total
 

time: 139 us -> 134 us (0.964)
  the two profiles are of different devices: /device:TPU:1 before, /device:TPU:32 now
where the time goes in v2:
time: 134 us; the launch traced here: 132 us
  starting transfers between devices  54.3 us (41%)
  waiting for transfers between devices  53.8 us (40%)
  Pallas kernels  13.6 us (10%)
  other arithmetic  5.83 us (4%)
  local copies, waits for them, and re-layouts  3.36 us (3%)
  between operations  1.48 us (1%)
    all_to_all x2, starting transfers between devices, z_exchange(): lax.all_to_all(chunks, AXES, 0, 0, tiled=True, axis_index_groups=groups)  19.6 us
    all_to_all x2, waiting for transfers between devices, z_exchange(): lax.all_to_all(chunks, AXES, 0, 0, tiled=True, axis_index_groups=groups)  17.8 us
    ppermute x6, starting transfers between devices, shifted(): return lax.ppermute(block, axis, route)  16.8 us
    ppermute x1, waiting for transfers between devices, halos_in(): relayed = lax.ppermute(own1, 'col', [(seam, 0)])  14.8 us
    ppermute x8, starting transfers between devices, moved(): return lax.ppermute(value, AXES, route)  11.2 us
    pallas_call x1, Pallas kernels, slot_terms(): pl.pallas_call(functools.partial(slots_kernel, w, t), out_shape=[f32((2,...  10.2 us
    ppermute x6, waiting for transfers between devices, shifted(): return lax.ppermute(block, axis, route)  8.19 us
    ppermute x8, waiting for transfers between devices, moved(): return lax.ppermute(value, AXES, route)  7.58 us
  transfers between devices with their start and end apart: 21, of which 10 were waited for; matrix products, arithmetic and copies ran while one was open for 2% of the time, Pallas kernels for 3%

profile of v2, /device:TPU:32, one launch (start us, length us, event | category | flops | bytes accessed | tf_op | source)
XLA Modules:
  0.0 132.4 jit_solution(11614401336916573324)
XLA Ops:
  0.6 1.6 %fusion = (f32[2,256,256]{2,1,0:T(8,128)S(1)}, f32[2,256,256]{2,1,0:T(8,128)S(1)}, f32[2,256,256]{2,1,0:T(8,128)S(1)}, f32[2,256,256]{2,1,0:T(8,128)S(1)}) fusion(f32[2,512,512]{2,1,0:T(8,128)} %object_hbm.1, pred[]{:T(512)S(6)} %eq.16), kind=kLoop, calls=%fused_computation.4 | loop fusion | flops 131072 | bytes 3670017 | tf_op jit(solution)/shard_map/slice | solution.py:318
  3.5 4.6 %collective-permute-start.2 = (f32[2,256,256]{2,1,0:T(8,128)S(1)}, f32[2,256,256]{2,1,0:T(8,128)S(1)}, u32[]{:S(2)}, u32[]{:S(2)}) collective-permute-start(f32[2,256,256]{2,1,0:T(8,128)S(1)} %get-tuple-element.26), channel_id=1, source_target_pairs={{16,0},{32,16},{48,32},{64,48},{80,64},{96,80},{112,96},{128,112},... | collective-permute-start | bytes 1572872 | tf_op jit(solution)/shard_map/ppermute | solution.py:24
  10.8 4.0 %collective-permute-start.3 = (f32[2,256,256]{2,1,0:T(8,128)S(1)}, f32[2,256,256]{2,1,0:T(8,128)}, u32[]{:S(2)}, u32[]{:S(2)}) collective-permute-start(f32[2,256,256]{2,1,0:T(8,128)S(1)} %get-tuple-element.27), channel_id=1, source_target_pairs={{16,0},{32,16},{48,32},{64,48},{80,64},{96,80},{112,96},{128,112},... | collective-permute-start | bytes 1572872 | tf_op jit(solution)/shard_map/ppermute | solution.py:24
  14.8 14.8 %collective-permute-done.4 = f32[2,256,256]{2,1,0:T(8,128)S(1)} collective-permute-done((f32[2,256,256]{2,1,0:T(8,128)S(1)}, f32[2,256,256]{2,1,0:T(8,128)S(1)}, u32[]{:S(2)}, u32[]{:S(2)}) %collective-permute-start.4) | collective-permute-done | bytes 524320 | tf_op jit(solution)/shard_map/ppermute | solution.py:322
  29.7 1.9 %collective-permute-start.5 = (f32[2,256,256]{2,1,0:T(8,128)S(1)}, f32[2,256,256]{2,1,0:T(8,128)S(1)}, u32[]{:S(2)}, u32[]{:S(2)}) collective-permute-start(f32[2,256,256]{2,1,0:T(8,128)S(1)} %broadcast_select_fusion), channel_id=1, source_target_pairs={{1,0},{2,1},{3,2},{4,3},{5,4},{6,5},{7,6},{9,8},{10,9},{11,10},{12... | collective-permute-start | bytes 1572872 | tf_op jit(solution)/shard_map/ppermute | solution.py:327
  32.9 5.4 %collective-permute-done.5.corner_hbm = f32[2,256,256]{2,1,0:T(8,128)S(1)} collective-permute-done((f32[2,256,256]{2,1,0:T(8,128)S(1)}, f32[2,256,256]{2,1,0:T(8,128)S(1)}, u32[]{:S(2)}, u32[]{:S(2)}) %collective-permute-start.5) | collective-permute-done | bytes 524320 | tf_op jit(solution)/shard_map/ppermute | solution.py:327
  39.1 10.2 %slot_terms.1 = (f32[2,512,512]{2,1,0:T(8,128)}, f32[2,512,256]{2,1,0:T(8,128)}, f32[2,256,256]{2,1,0:T(8,128)}, f32[2,256,256]{2,1,0:T(8,128)}, f32[2,256,256]{...) custom-call(s32[1]{0:T(128)S(6)} %copy.14.counts_ref, s32[2,2]{1,0:T(2,128)} %pos_ref.1, s32[3]{0:T(128)} %pad_add_fusion.place_ref, ...), custom_call_target="tpu_custom_call" | custom-call | flops 3000000000 | bytes 14680064 | tf_op jit(solution)/shard_map/slot_terms/pallas_call | solution.py:181
  49.3 1.4 %collective-permute-start.12 = (f32[2,512,256]{2,1,0:T(8,128)}, f32[2,512,256]{2,1,0:T(8,128)S(1)}, u32[]{:S(2)}, u32[]{:S(2)}) collective-permute-start(f32[2,512,256]{2,1,0:T(8,128)} %get-tuple-element.19), channel_id=1, source_target_pairs={{0,1},{1,2},{2,3},{3,4},{4,5},{5,6},{6,7},{8,9},{9,10},{10,11},{11... | collective-permute-start | bytes 3145736 | tf_op jit(solution)/shard_map/ppermute | solution.py:346
  50.7 2.4 %collective-permute-start.10 = (f32[2,256,256]{2,1,0:T(8,128)}, f32[2,256,256]{2,1,0:T(8,128)S(1)}, u32[]{:S(2)}, u32[]{:S(2)}) collective-permute-start(f32[2,256,256]{2,1,0:T(8,128)} %get-tuple-element.17), channel_id=1, source_target_pairs={{0,1},{1,2},{2,3},{3,4},{4,5},{5,6},{6,7},{7,8},{8,9},{9,10},{10,1... | collective-permute-start | bytes 1572872 | tf_op jit(solution)/shard_map/ppermute | solution.py:24
  53.2 1.9 %collective-permute-start.11 = (f32[2,256,256]{2,1,0:T(8,128)}, f32[2,256,256]{2,1,0:T(8,128)S(1)}, u32[]{:S(2)}, u32[]{:S(2)}) collective-permute-start(f32[2,256,256]{2,1,0:T(8,128)} %get-tuple-element.18), channel_id=1, source_target_pairs={{0,16},{16,32},{32,48},{48,64},{64,80},{80,96},{96,112},{112,128},... | collective-permute-start | bytes 1572872 | tf_op jit(solution)/shard_map/ppermute | solution.py:24
  55.1 1.7 %add.8 = f32[256,256]{1,0:T(8,128)} add(f32[256,256]{1,0:T(8,128)} %get-tuple-element.14, f32[256,256]{1,0:T(8,128)S(1)} %collective-permute-done.6) | non-fusion elementwise | flops 65536 | bytes 786432 | tf_op jit(solution)/shard_map/add | solution.py:349
  56.8 12.1 %all-to-all-start = ((f32[8,32,256]{2,1,0:T(8,128)}), f32[8,32,256]{2,1,0:T(8,128)S(1)}, u32[]{:S(2)}, u32[]{:S(2)}) async-start(f32[8,32,256]{2,1,0:T(8,128)} %bitcast.3), calls=%async_computation | async-start | bytes 524288 | tf_op jit(solution)/shard_map/all_to_all | solution.py:310
  69.7 11.0 %all-to-all-done.refs_0_ = f32[8,32,256]{2,1,0:T(8,128)S(1)} async-done(((f32[8,32,256]{2,1,0:T(8,128)}), f32[8,32,256]{2,1,0:T(8,128)S(1)}, u32[]{:S(2)}, u32[]{:S(2)}) %all-to-all-start) | async-done | bytes 262176 | tf_op jit(solution)/shard_map/all_to_all | solution.py:310
  80.7 6.1 %collective-permute-start.9 = (f32[32,256]{1,0:T(8,128)S(1)}, f32[32,256]{1,0:T(8,128)S(1)}, u32[]{:S(2)}, u32[]{:S(2)}) collective-permute-start(f32[32,256]{1,0:T(8,128)S(1)} %added.3.refs_0_), channel_id=1, source_target_pairs={{0,6},{1,7},{32,38},{33,39},{64,70},{65,71},{96,102},{97,103},{128... | collective-permute-start | bytes 98312 | tf_op jit(solution)/shard_map/ppermute | solution.py:274
  89.0 3.2 %collective-permute-done.8.refs_2_ = f32[32,256]{1,0:T(8,128)S(1)} collective-permute-done((f32[32,256]{1,0:T(8,128)S(1)}, f32[32,256]{1,0:T(8,128)S(1)}, u32[]{:S(2)}, u32[]{:S(2)}) %collective-permute-start.8) | collective-permute-done | bytes 32800 | tf_op jit(solution)/shard_map/ppermute | solution.py:274
  94.8 1.4 %collective-permute-start.16 = (f32[32,256]{1,0:T(8,128)S(1)}, f32[32,256]{1,0:T(8,128)S(1)}, u32[]{:S(2)}, u32[]{:S(2)}) collective-permute-start(f32[32,256]{1,0:T(8,128)S(1)} %get-tuple-element.23.refs_0_), channel_id=1, source_target_pairs={{0,16},{1,17},{32,48},{33,49},{64,80},{65,81},{96,112},{97,113},{1... | collective-permute-start | bytes 98312 | tf_op jit(solution)/shard_map/ppermute | solution.py:274
  96.2 1.4 %collective-permute-start.15 = (f32[32,256]{1,0:T(8,128)S(1)}, f32[32,256]{1,0:T(8,128)S(1)}, u32[]{:S(2)}, u32[]{:S(2)}) collective-permute-start(f32[32,256]{1,0:T(8,128)S(1)} %get-tuple-element.23.refs_0_), channel_id=1, source_target_pairs={{0,8},{1,9},{32,40},{33,41},{64,72},{65,73},{96,104},{97,105},{128... | collective-permute-start | bytes 98312 | tf_op jit(solution)/shard_map/ppermute | solution.py:274
  98.7 1.5 %collective-permute-done.16.refs_2_ = f32[32,256]{1,0:T(8,128)S(1)} collective-permute-done((f32[32,256]{1,0:T(8,128)S(1)}, f32[32,256]{1,0:T(8,128)S(1)}, u32[]{:S(2)}, u32[]{:S(2)}) %collective-permute-start.16) | collective-permute-done | bytes 32800 | tf_op jit(solution)/shard_map/ppermute | solution.py:274
  102.1 7.6 %all-to-all-start.1 = ((f32[8,32,256]{2,1,0:T(8,128)}), f32[8,32,256]{2,1,0:T(8,128)S(1)}, u32[]{:S(2)}, u32[]{:S(2)}) async-start(f32[8,32,256]{2,1,0:T(8,128)} %broadcast_in_dim.3), calls=%async_computation.1 | async-start | bytes 524288 | tf_op jit(solution)/shard_map/all_to_all | solution.py:310
  109.7 2.5 %collective-permute-start.14 = (f32[2,256,256]{2,1,0:T(8,128)}, f32[2,256,256]{2,1,0:T(8,128)S(1)}, u32[]{:S(2)}, u32[]{:S(2)}) collective-permute-start(f32[2,256,256]{2,1,0:T(8,128)} %copy-done.2), channel_id=1, source_target_pairs={{0,16},{16,32},{32,48},{48,64},{64,80},{80,96},{96,112},{112,128},... | collective-permute-start | bytes 1572872 | tf_op jit(solution)/shard_map/ppermute | solution.py:24
  112.2 6.9 %all-to-all-done.1 = f32[8,32,256]{2,1,0:T(8,128)S(1)} async-done(((f32[8,32,256]{2,1,0:T(8,128)}), f32[8,32,256]{2,1,0:T(8,128)S(1)}, u32[]{:S(2)}, u32[]{:S(2)}) %all-to-all-start.1) | async-done | bytes 262176 | tf_op jit(solution)/shard_map/all_to_all | solution.py:310
  119.0 8.2 %collective-permute-done.14.above0_hbm = f32[2,256,256]{2,1,0:T(8,128)S(1)} collective-permute-done((f32[2,256,256]{2,1,0:T(8,128)}, f32[2,256,256]{2,1,0:T(8,128)S(1)}, u32[]{:S(2)}, u32[]{:S(2)}) %collective-permute-start.14) | collective-permute-done | bytes 524320 | tf_op jit(solution)/shard_map/ppermute | solution.py:24
  127.2 3.2 %combined.1 = f32[2,512,512]{2,1,0:T(8,128)} custom-call(s32[3]{0:T(128)S(1)} %copy-done.1, f32[2,512,512]{2,1,0:T(8,128)} %get-tuple-element.13.tile_hbm, f32[2,512,256]{2,1,0:T(8,128)S(1)} %get-tuple-element.20.left_hbm, f32[2,512,256]{2,1,0:T(8,128)S(1)} %collective-permute-done.13.seam_hbm, ...), custom_call_target="tpu_custom_call", output_to_operand_aliasing={{}: (1, {})} | custom-call | flops 1000000 | bytes 6291456 | tf_op jit(solution)/shard_map/combined/pallas_call | solution.py:240
  130.5 1.9 %maximum_select_fusion = f32[2,256,256]{2,1,0:T(8,128)} fusion(f32[1,256,256]{2,1,0:T(8,128)} %bitcast.6, f32[1,256,256]{2,1,0:T(8,128)S(1)} %bitcast.8, pred[]{:T(512)S(6)} %eq.18), kind=kLoop, calls=%fused_computation | loop fusion | flops 393216 | bytes 1048577 | tf_op jit(solution)/shard_map/jit(_where)/select_n | solution.py:358
  (39 shorter events, 14.1 us)
Async XLA Ops:
  2.2 27.4 %collective-permute-start.4 = (f32[2,256,256]{2,1,0:T(8,128)S(1)}, f32[2,256,256]{2,1,0:T(8,128)S(1)}, u32[]{:S(2)}, u32[]{:S(2)}) collective-permute-start(f32[2,256,256]{2,1,0:T(8,128)S(1)} %get-tuple-element.24), channel_id=1, source_target_pairs={{8,0},{24,16},{40,32},{56,48},{72,64},{88,80},{104,96},{120,112},{... | collective-permute-start | bytes 1572872 | tf_op jit(solution)/shard_map/ppermute | solution.py:322
  3.5 26.1 %collective-permute-start.2 = (f32[2,256,256]{2,1,0:T(8,128)S(1)}, f32[2,256,256]{2,1,0:T(8,128)S(1)}, u32[]{:S(2)}, u32[]{:S(2)}) collective-permute-start(f32[2,256,256]{2,1,0:T(8,128)S(1)} %get-tuple-element.26), channel_id=1, source_target_pairs={{16,0},{32,16},{48,32},{64,48},{80,64},{96,80},{112,96},{128,112},... | collective-permute-start | bytes 1572872 | tf_op jit(solution)/shard_map/ppermute | solution.py:24
  8.2 24.7 %collective-permute-start = (f32[2,256,256]{2,1,0:T(8,128)S(1)}, f32[2,256,256]{2,1,0:T(8,128)}, u32[]{:S(2)}, u32[]{:S(2)}) collective-permute-start(f32[2,256,256]{2,1,0:T(8,128)S(1)} %get-tuple-element.26), channel_id=1, source_target_pairs={{1,0},{2,1},{3,2},{4,3},{5,4},{6,5},{7,6},{8,7},{9,8},{10,9},{11,1... | collective-permute-start | bytes 1572872 | tf_op jit(solution)/shard_map/ppermute | solution.py:24
  9.5 23.4 %collective-permute-start.1 = (f32[2,256,256]{2,1,0:T(8,128)S(1)}, f32[2,256,256]{2,1,0:T(8,128)}, u32[]{:S(2)}, u32[]{:S(2)}) collective-permute-start(f32[2,256,256]{2,1,0:T(8,128)S(1)} %get-tuple-element.25), channel_id=1, source_target_pairs={{1,0},{2,1},{3,2},{4,3},{5,4},{6,5},{7,6},{9,8},{10,9},{11,10},{12... | collective-permute-start | bytes 1572872 | tf_op jit(solution)/shard_map/ppermute | solution.py:326
  10.8 22.1 %collective-permute-start.3 = (f32[2,256,256]{2,1,0:T(8,128)S(1)}, f32[2,256,256]{2,1,0:T(8,128)}, u32[]{:S(2)}, u32[]{:S(2)}) collective-permute-start(f32[2,256,256]{2,1,0:T(8,128)S(1)} %get-tuple-element.27), channel_id=1, source_target_pairs={{16,0},{32,16},{48,32},{64,48},{80,64},{96,80},{112,96},{128,112},... | collective-permute-start | bytes 1572872 | tf_op jit(solution)/shard_map/ppermute | solution.py:24
  29.6 8.7 %copy-start.3 = (f32[2,256,256]{2,1,0:T(8,128)}, f32[2,256,256]{2,1,0:T(8,128)S(1)}, u32[]{:S(2)}) copy-start(f32[2,256,256]{2,1,0:T(8,128)S(1)} %collective-permute-done.2.below0_hbm) | copy-start | bytes 1572868
  29.7 8.6 %collective-permute-start.5 = (f32[2,256,256]{2,1,0:T(8,128)S(1)}, f32[2,256,256]{2,1,0:T(8,128)S(1)}, u32[]{:S(2)}, u32[]{:S(2)}) collective-permute-start(f32[2,256,256]{2,1,0:T(8,128)S(1)} %broadcast_select_fusion), channel_id=1, source_target_pairs={{1,0},{2,1},{3,2},{4,3},{5,4},{6,5},{7,6},{9,8},{10,9},{11,10},{12... | collective-permute-start | bytes 1572872 | tf_op jit(solution)/shard_map/ppermute | solution.py:327
  49.3 43.6 %collective-permute-start.12 = (f32[2,512,256]{2,1,0:T(8,128)}, f32[2,512,256]{2,1,0:T(8,128)S(1)}, u32[]{:S(2)}, u32[]{:S(2)}) collective-permute-start(f32[2,512,256]{2,1,0:T(8,128)} %get-tuple-element.19), channel_id=1, source_target_pairs={{0,1},{1,2},{2,3},{3,4},{4,5},{5,6},{6,7},{8,9},{9,10},{10,11},{11... | collective-permute-start | bytes 3145736 | tf_op jit(solution)/shard_map/ppermute | solution.py:346
  50.6 4.5 %collective-permute-start.6 = (f32[256,256]{1,0:T(8,128)}, f32[256,256]{1,0:T(8,128)S(1)}, u32[]{:S(2)}, u32[]{:S(2)}) collective-permute-start(f32[256,256]{1,0:T(8,128)} %get-tuple-element.15), channel_id=1, source_target_pairs={{0,1},{1,0},{32,33},{33,32},{64,65},{65,64},{96,97},{97,96},{128,1... | collective-permute-start | bytes 786440 | tf_op jit(solution)/shard_map/ppermute | solution.py:274
  50.7 36.1 %collective-permute-start.10 = (f32[2,256,256]{2,1,0:T(8,128)}, f32[2,256,256]{2,1,0:T(8,128)S(1)}, u32[]{:S(2)}, u32[]{:S(2)}) collective-permute-start(f32[2,256,256]{2,1,0:T(8,128)} %get-tuple-element.17), channel_id=1, source_target_pairs={{0,1},{1,2},{2,3},{3,4},{4,5},{5,6},{6,7},{7,8},{8,9},{9,10},{10,1... | collective-permute-start | bytes 1572872 | tf_op jit(solution)/shard_map/ppermute | solution.py:24
  53.2 34.5 %collective-permute-start.11 = (f32[2,256,256]{2,1,0:T(8,128)}, f32[2,256,256]{2,1,0:T(8,128)S(1)}, u32[]{:S(2)}, u32[]{:S(2)}) collective-permute-start(f32[2,256,256]{2,1,0:T(8,128)} %get-tuple-element.18), channel_id=1, source_target_pairs={{0,16},{16,32},{32,48},{48,64},{64,80},{80,96},{96,112},{112,128},... | collective-permute-start | bytes 1572872 | tf_op jit(solution)/shard_map/ppermute | solution.py:24
  56.8 23.9 %all-to-all-start = ((f32[8,32,256]{2,1,0:T(8,128)}), f32[8,32,256]{2,1,0:T(8,128)S(1)}, u32[]{:S(2)}, u32[]{:S(2)}) async-start(f32[8,32,256]{2,1,0:T(8,128)} %bitcast.3), calls=%async_computation | async-start | bytes 524288 | tf_op jit(solution)/shard_map/all_to_all | solution.py:310
  68.9 58.4 %copy-start.1 = (s32[3]{0:T(128)S(1)}, s32[3]{0:T(128)}, u32[]{:S(2)}) copy-start(s32[3]{0:T(128)} %pad_add_fusion.place_ref) | copy-start | bytes 40
  68.9 50.2 %collective-permute-start.13 = (f32[2,512,256]{2,1,0:T(8,128)}, f32[2,512,256]{2,1,0:T(8,128)S(1)}, u32[]{:S(2)}, u32[]{:S(2)}) collective-permute-start(f32[2,512,256]{2,1,0:T(8,128)} %get-tuple-element.19), channel_id=1, source_target_pairs={{7,8},{23,24},{39,40},{55,56},{71,72},{87,88},{103,104},{119,120},... | collective-permute-start | bytes 3145736 | tf_op jit(solution)/shard_map/ppermute | solution.py:347
  80.7 8.3 %collective-permute-start.9 = (f32[32,256]{1,0:T(8,128)S(1)}, f32[32,256]{1,0:T(8,128)S(1)}, u32[]{:S(2)}, u32[]{:S(2)}) collective-permute-start(f32[32,256]{1,0:T(8,128)S(1)} %added.3.refs_0_), channel_id=1, source_target_pairs={{0,6},{1,7},{32,38},{33,39},{64,70},{65,71},{96,102},{97,103},{128... | collective-permute-start | bytes 98312 | tf_op jit(solution)/shard_map/ppermute | solution.py:274
  86.8 5.4 %collective-permute-start.8 = (f32[32,256]{1,0:T(8,128)S(1)}, f32[32,256]{1,0:T(8,128)S(1)}, u32[]{:S(2)}, u32[]{:S(2)}) collective-permute-start(f32[32,256]{1,0:T(8,128)S(1)} %added.3.refs_0_), channel_id=1, source_target_pairs={{0,4},{1,5},{32,36},{33,37},{64,68},{65,69},{96,100},{97,101},{128... | collective-permute-start | bytes 98312 | tf_op jit(solution)/shard_map/ppermute | solution.py:274
  87.7 5.1 %collective-permute-start.7 = (f32[32,256]{1,0:T(8,128)S(1)}, f32[32,256]{1,0:T(8,128)S(1)}, u32[]{:S(2)}, u32[]{:S(2)}) collective-permute-start(f32[32,256]{1,0:T(8,128)S(1)} %added.3.refs_0_), channel_id=1, source_target_pairs={{0,2},{1,3},{32,34},{33,35},{64,66},{65,67},{96,98},{97,99},{128,1... | collective-permute-start | bytes 98312 | tf_op jit(solution)/shard_map/ppermute | solution.py:274
  92.8 1.0 copy-start
  94.8 3.9 %collective-permute-start.17 = (f32[32,256]{1,0:T(8,128)S(1)}, f32[32,256]{1,0:T(8,128)S(1)}, u32[]{:S(2)}, u32[]{:S(2)}) collective-permute-start(f32[32,256]{1,0:T(8,128)S(1)} %get-tuple-element.23.refs_0_), channel_id=1, source_target_pairs={{0,24},{1,25},{32,56},{33,57},{64,88},{65,89},{96,120},{97,121},{1... | collective-permute-start | bytes 98312 | tf_op jit(solution)/shard_map/ppermute | solution.py:274
  94.8 5.4 %collective-permute-start.16 = (f32[32,256]{1,0:T(8,128)S(1)}, f32[32,256]{1,0:T(8,128)S(1)}, u32[]{:S(2)}, u32[]{:S(2)}) collective-permute-start(f32[32,256]{1,0:T(8,128)S(1)} %get-tuple-element.23.refs_0_), channel_id=1, source_target_pairs={{0,16},{1,17},{32,48},{33,49},{64,80},{65,81},{96,112},{97,113},{1... | collective-permute-start | bytes 98312 | tf_op jit(solution)/shard_map/ppermute | solution.py:274
  96.2 5.2 %collective-permute-start.15 = (f32[32,256]{1,0:T(8,128)S(1)}, f32[32,256]{1,0:T(8,128)S(1)}, u32[]{:S(2)}, u32[]{:S(2)}) collective-permute-start(f32[32,256]{1,0:T(8,128)S(1)} %get-tuple-element.23.refs_0_), channel_id=1, source_target_pairs={{0,8},{1,9},{32,40},{33,41},{64,72},{65,73},{96,104},{97,105},{128... | collective-permute-start | bytes 98312 | tf_op jit(solution)/shard_map/ppermute | solution.py:274
  102.1 16.9 %all-to-all-start.1 = ((f32[8,32,256]{2,1,0:T(8,128)}), f32[8,32,256]{2,1,0:T(8,128)S(1)}, u32[]{:S(2)}, u32[]{:S(2)}) async-start(f32[8,32,256]{2,1,0:T(8,128)} %broadcast_in_dim.3), calls=%async_computation.1 | async-start | bytes 524288 | tf_op jit(solution)/shard_map/all_to_all | solution.py:310
  109.7 17.6 %collective-permute-start.14 = (f32[2,256,256]{2,1,0:T(8,128)}, f32[2,256,256]{2,1,0:T(8,128)S(1)}, u32[]{:S(2)}, u32[]{:S(2)}) collective-permute-start(f32[2,256,256]{2,1,0:T(8,128)} %copy-done.2), channel_id=1, source_target_pairs={{0,16},{16,32},{32,48},{48,64},{64,80},{80,96},{96,112},{112,128},... | collective-permute-start | bytes 1572872 | tf_op jit(solution)/shard_map/ppermute | solution.py:24
  119.0 11.4 %collective-permute-start.18 = (f32[256,256]{1,0:T(8,128)S(1)}, f32[256,256]{1,0:T(8,128)}, u32[]{:S(2)}, u32[]{:S(2)}) collective-permute-start(f32[256,256]{1,0:T(8,128)S(1)} %bitcast.7), channel_id=1, source_target_pairs={{0,1},{1,0},{32,33},{33,32},{64,65},{65,64},{96,97},{97,96},{128,1... | collective-permute-start | bytes 786440 | tf_op jit(solution)/shard_map/ppermute | solution.py:274
  (2 other events, 1.6 us)

commit v3 on v2

--- a/solution.py
+++ b/solution.py
@@ -66,7 +66,7 @@
 
 def slots_kernel(
     window, tile,
-    counts_ref, pos_ref, place_ref, object_hbm, right0_hbm, right1_hbm, below0_hbm, below1_hbm,
+    counts_ref, pos_ref, place_ref, object_hbm, below1_hbm, below0_hbm, right0_hbm, right1_hbm,
     corner_hbm, probe_hbm, amp_hbm, tables_hbm,
     tile_out, right_out, below0_out, below1_out, corner_out, keep_out, send_out,
     ext, grad, probe, turned, amp, tables, patch, probe_grad, sems,
@@ -201,14 +201,15 @@
 
 
 def combine_kernel(
-    window, place_ref, tile_hbm, left_hbm, seam_hbm, above0_hbm, above1_hbm, out_hbm, tile, side, above0, above1, sems
+    window, place_ref, tile_hbm, left_hbm, seam_hbm, upper_hbm, lower_hbm, above1_hbm, out_hbm, tile, side, above0, above1, sems
 ):
     w, t = window, tile.shape[1]
     after_seam = place_ref[2]
     mine = [
         pltpu.make_async_copy(tile_hbm.at[:, 0:w, :], tile.at[:, 0:w, :], sems.at[0]),
         pltpu.make_async_copy(tile_hbm.at[:, w:t, 0:w], tile.at[:, w:t, 0:w], sems.at[1]),
-        pltpu.make_async_copy(above0_hbm, above0, sems.at[2]),
+        pltpu.make_async_copy(upper_hbm, above0.at[:, 0 : w // 2], sems.at[2]),
+        pltpu.make_async_copy(lower_hbm, above0.at[:, w // 2 : w], sems.at[5]),
         pltpu.make_async_copy(above1_hbm, above1, sems.at[3]),
     ]
     for copy in mine:
@@ -235,25 +236,25 @@
     low.wait()
 
 
-def combined(where, tile_grad, from_left, from_seam, above0, above1):
+def combined(where, tile_grad, from_left, from_seam, upper, lower, above1):
     t, w = tile_grad.shape[1], from_left.shape[2]
     return pl.pallas_call(
         functools.partial(combine_kernel, w),
         out_shape=jax.ShapeDtypeStruct(tile_grad.shape, jnp.float32),
-        in_specs=[SMEM] + [HBM] * 5,
+        in_specs=[SMEM] + [HBM] * 6,
         out_specs=HBM,
         scratch_shapes=[
             pltpu.VMEM((2, t, t), jnp.float32),
             pltpu.VMEM((2, t, w), jnp.float32),
             pltpu.VMEM((2, w, w), jnp.float32),
             pltpu.VMEM((2, w, w), jnp.float32),
-            pltpu.SemaphoreType.DMA((5,)),
+            pltpu.SemaphoreType.DMA((6,)),
         ],
         input_output_aliases={1: 0},
         compiler_params=pltpu.CompilerParams(vmem_limit_bytes=12 * MIB),
         cost_estimate=pl.CostEstimate(flops=10**6, bytes_accessed=6 * MIB, transcendentals=0),
         name="combined",
-    )(where, tile_grad, from_left, from_seam, above0, above1)
+    )(where, tile_grad, from_left, from_seam, upper, lower, above1)
 
 
 def place(x, y, z, core):
@@ -305,6 +306,53 @@
     return [moved(value, **{axis: d}) for d in range(1, SIZES[axis])]
 
 
+def middle_kernel(first, second, third, fourth, below_ref, corner_ref, *refs):
+    sum_out, upper_out, lower_out = refs[2:5]
+    half = upper_out.shape[1]
+    sum_out[...] = first[...] + second[...] + third[...] + fourth[...]
+    upper_out[...] = below_ref[:, :half] + corner_ref[:, :half]
+    lower_out[...] = below_ref[:, half:] + corner_ref[:, half:]
+
+
+def middle(parts, below0, corner, above1, from_left):
+    f32 = functools.partial(jax.ShapeDtypeStruct, dtype=jnp.float32)
+    planes, w, _ = below0.shape
+    half = f32((planes, w // 2, w))
+    return pl.pallas_call(
+        middle_kernel,
+        out_shape=[f32(parts[0].shape), half, half, f32(above1.shape), f32(from_left.shape)],
+        in_specs=[VMEM] * 6 + [HBM] * 2,
+        out_specs=[VMEM] * 3 + [HBM] * 2,
+        input_output_aliases={6: 3, 7: 4},
+        compiler_params=pltpu.CompilerParams(vmem_limit_bytes=8 * MIB),
+        name="middle",
+    )(*parts, below0, corner, above1, from_left)
+
+
+def planes_kernel(place_ref, own_hbm, other_hbm, out_hbm, sems):
+    core = place_ref[0]
+    copies = [
+        pltpu.make_async_copy(own_hbm, out_hbm.at[core], sems.at[0]),
+        pltpu.make_async_copy(other_hbm, out_hbm.at[1 - core], sems.at[1]),
+    ]
+    for copy in copies:
+        copy.start()
+    for copy in copies:
+        copy.wait()
+
+
+def both_planes(where, own, other):
+    return pl.pallas_call(
+        planes_kernel,
+        out_shape=jax.ShapeDtypeStruct((2,) + own.shape, own.dtype),
+        in_specs=[SMEM, HBM, HBM],
+        out_specs=HBM,
+        scratch_shapes=[pltpu.SemaphoreType.DMA((2,))],
+        compiler_params=pltpu.CompilerParams(vmem_limit_bytes=2 * MIB),
+        name="both_planes",
+    )(where, own, other)
+
+
 def z_exchange(chunks):
     groups = [[place(x, y, z, c) for z in range(8)] for x in range(4) for y in range(4) for c in range(2)]
     return lax.all_to_all(chunks, AXES, 0, 0, tiled=True, axis_index_groups=groups)
@@ -325,7 +373,7 @@
     route += [((r + 1) * cols + seam, r * cols + seam - 1) for r in range(rows - 1)]
     right1 = lax.ppermute(jnp.where(col == seam, own0, own1), AXES, route)
     corner = lax.ppermute(jnp.where(col == 0, relayed, below0), "col", plain + [(0, seam - 1)])
-    return right0, right1, below0, below1, corner
+    return below1, below0, right0, right1, corner
 
 
 def shards(object_field, probe, positions, amplitudes, counts):
@@ -350,16 +398,18 @@
         value = z_exchange(value.reshape(8, window // 8, window))
         value = added([[value]])[0]
         parts = [value] + neighbours(value, "x")
-        value, below0_grad, above1, from_left = added([parts, [below0_grad, corner_in]], above1, from_left, vmem=8)
-        above0 = shifted(below0_grad, "row", 1)
-        value = added([[value] + neighbours(value, "y")])[0]
+        value, upper, lower, above1, from_left = middle(parts, below0_grad, corner_in, above1, from_left)
+        upper = shifted(upper, "row", 1)
+        lower = shifted(lower, "row", 1)
+        value, upper = added([[value] + neighbours(value, "y")], upper)
         value = z_exchange(jnp.broadcast_to(value, (8,) + value.shape)).reshape(window, window)
         other = moved(value, core=1)
-        probe_total = jnp.where(core == 0, jnp.stack([value, other]), jnp.stack([other, value]))
+        probe_total = both_planes(where, value, other)
     else:
         above0 = shifted(below0_grad + corner_in, "row", 1)
+        upper, lower = above0[:, : window // 2], above0[:, window // 2 :]
         probe_total = lax.psum(jnp.where(core == 0, jnp.stack([keep, send]), jnp.stack([send, keep])), AXES)
-    return combined(where, tile_grad, from_left, from_seam, above0, above1), probe_total
+    return combined(where, tile_grad, from_left, from_seam, upper, lower, above1), probe_total
 
 
 def solution(mesh):

time: 134 us -> 134 us (level)
  the two profiles are of different devices: /device:TPU:32 before, /device:TPU:1 now
where the time goes in v3:
time: 134 us; the launch traced here: 133 us
  starting transfers between devices  78.9 us (59%)
  waiting for transfers between devices  31 us (23%)
  Pallas kernels  14.9 us (11%)
  other arithmetic  3.93 us (3%)
  local copies, waits for them, and re-layouts  2.57 us (2%)
  between operations  1.5 us (1%)
    ppermute x8, starting transfers between devices, moved(): return lax.ppermute(value, AXES, route)  22.8 us
    all_to_all x2, waiting for transfers between devices, z_exchange(): lax.all_to_all(chunks, AXES, 0, 0, tiled=True, axis_index_groups=groups)  19.5 us
    all_to_all x2, starting transfers between devices, z_exchange(): lax.all_to_all(chunks, AXES, 0, 0, tiled=True, axis_index_groups=groups)  18.1 us
    ppermute x1, starting transfers between devices, halos_in(): lax.ppermute(jnp.where(col == 0, relayed, below0), 'col', plain + [(0, se...  17.3 us
    ppermute x7, starting transfers between devices, shifted(): return lax.ppermute(block, axis, route)  15.4 us
    pallas_call x1, Pallas kernels, slot_terms(): pl.pallas_call(functools.partial(slots_kernel, w, t), out_shape=[f32((2,...  10.2 us
    ppermute x8, waiting for transfers between devices, moved(): return lax.ppermute(value, AXES, route)  6.94 us
    ppermute x7, waiting for transfers between devices, shifted(): return lax.ppermute(block, axis, route)  4.26 us
  transfers between devices with their start and end apart: 22, of which 9 were waited for; matrix products, arithmetic and copies ran while one was open for 2% of the time, Pallas kernels for 3%

profile of v3, /device:TPU:1, one launch (start us, length us, event | category | flops | bytes accessed | tf_op | source)
XLA Modules:
  0.0 132.9 jit_solution(1147640506277582696)
XLA Ops:
  0.6 1.6 %fusion = (f32[2,256,256]{2,1,0:T(8,128)S(1)}, f32[2,256,256]{2,1,0:T(8,128)S(1)}, f32[2,256,256]{2,1,0:T(8,128)S(1)}, f32[2,256,256]{2,1,0:T(8,128)S(1)}) fusion(f32[2,512,512]{2,1,0:T(8,128)} %object_hbm.1, pred[]{:T(512)S(6)} %eq.13), kind=kLoop, calls=%fused_computation.3 | loop fusion | flops 131072 | bytes 3670017 | tf_op jit(solution)/shard_map/slice | solution.py:366
  4.2 5.7 %collective-permute-start.2 = (f32[2,256,256]{2,1,0:T(8,128)S(1)}, f32[2,256,256]{2,1,0:T(8,128)}, u32[]{:S(2)}, u32[]{:S(2)}) collective-permute-start(f32[2,256,256]{2,1,0:T(8,128)S(1)} %get-tuple-element.32), channel_id=1, source_target_pairs={{1,0},{2,1},{3,2},{4,3},{5,4},{6,5},{7,6},{8,7},{9,8},{10,9},{11,1... | collective-permute-start | bytes 1572872 | tf_op jit(solution)/shard_map/ppermute | solution.py:24
  10.0 1.9 %collective-permute-start.3 = (f32[2,256,256]{2,1,0:T(8,128)S(1)}, f32[2,256,256]{2,1,0:T(8,128)}, u32[]{:S(2)}, u32[]{:S(2)}) collective-permute-start(f32[2,256,256]{2,1,0:T(8,128)S(1)} %get-tuple-element.31), channel_id=1, source_target_pairs={{1,0},{2,1},{3,2},{4,3},{5,4},{6,5},{7,6},{9,8},{10,9},{11,10},{12... | collective-permute-start | bytes 1572872 | tf_op jit(solution)/shard_map/ppermute | solution.py:374
  13.2 4.2 %collective-permute-done.1.below0_hbm = f32[2,256,256]{2,1,0:T(8,128)S(1)} collective-permute-done((f32[2,256,256]{2,1,0:T(8,128)S(1)}, f32[2,256,256]{2,1,0:T(8,128)S(1)}, u32[]{:S(2)}, u32[]{:S(2)}) %collective-permute-start.1) | collective-permute-done | bytes 524320 | tf_op jit(solution)/shard_map/ppermute | solution.py:24
  17.5 17.3 %collective-permute-start.5 = (f32[2,256,256]{2,1,0:T(8,128)S(1)}, f32[2,256,256]{2,1,0:T(8,128)S(1)}, u32[]{:S(2)}, u32[]{:S(2)}) collective-permute-start(f32[2,256,256]{2,1,0:T(8,128)S(1)} %broadcast_select_fusion), channel_id=1, source_target_pairs={{1,0},{2,1},{3,2},{4,3},{5,4},{6,5},{7,6},{9,8},{10,9},{11,10},{12... | collective-permute-start | bytes 1572872 | tf_op jit(solution)/shard_map/ppermute | solution.py:375
  37.2 10.2 %slot_terms.1 = (f32[2,512,512]{2,1,0:T(8,128)}, f32[2,512,256]{2,1,0:T(8,128)}, f32[2,256,256]{2,1,0:T(8,128)}, f32[2,256,256]{2,1,0:T(8,128)}, f32[2,256,256]{...) custom-call(s32[1]{0:T(128)S(6)} %copy.16.counts_ref, s32[2,2]{1,0:T(2,128)} %pos_ref.1, s32[3]{0:T(128)} %pad_add_fusion.place_ref, ...), custom_call_target="tpu_custom_call" | custom-call | flops 3000000000 | bytes 14680064 | tf_op jit(solution)/shard_map/slot_terms/pallas_call | solution.py:181
  47.4 1.9 %collective-permute-start.12 = (f32[2,512,256]{2,1,0:T(8,128)}, f32[2,512,256]{2,1,0:T(8,128)S(1)}, u32[]{:S(2)}, u32[]{:S(2)}) collective-permute-start(f32[2,512,256]{2,1,0:T(8,128)} %get-tuple-element.22), channel_id=1, source_target_pairs={{0,1},{1,2},{2,3},{3,4},{4,5},{5,6},{6,7},{8,9},{9,10},{10,11},{11... | collective-permute-start | bytes 3145736 | tf_op jit(solution)/shard_map/ppermute | solution.py:394
  49.3 4.7 %collective-permute-start.6 = (f32[256,256]{1,0:T(8,128)}, f32[256,256]{1,0:T(8,128)S(1)}, u32[]{:S(2)}, u32[]{:S(2)}) collective-permute-start(f32[256,256]{1,0:T(8,128)} %get-tuple-element.18), channel_id=1, source_target_pairs={{0,1},{1,0},{32,33},{33,32},{64,65},{65,64},{96,97},{97,96},{128,1... | collective-permute-start | bytes 786440 | tf_op jit(solution)/shard_map/ppermute | solution.py:275
  54.0 1.9 %collective-permute-start.10 = (f32[2,256,256]{2,1,0:T(8,128)}, f32[2,256,256]{2,1,0:T(8,128)S(1)}, u32[]{:S(2)}, u32[]{:S(2)}) collective-permute-start(f32[2,256,256]{2,1,0:T(8,128)} %get-tuple-element.20), channel_id=1, source_target_pairs={{0,1},{1,2},{2,3},{3,4},{4,5},{5,6},{6,7},{7,8},{8,9},{9,10},{10,1... | collective-permute-start | bytes 1572872 | tf_op jit(solution)/shard_map/ppermute | solution.py:24
  56.0 1.3 collective-permute-start.11
  57.3 1.7 %add.8 = f32[256,256]{1,0:T(8,128)} add(f32[256,256]{1,0:T(8,128)} %get-tuple-element.17, f32[256,256]{1,0:T(8,128)S(1)} %collective-permute-done.6) | non-fusion elementwise | flops 65536 | bytes 786432 | tf_op jit(solution)/shard_map/add | solution.py:397
  59.0 7.1 %all-to-all-start = ((f32[8,32,256]{2,1,0:T(8,128)}), f32[8,32,256]{2,1,0:T(8,128)S(1)}, u32[]{:S(2)}, u32[]{:S(2)}) async-start(f32[8,32,256]{2,1,0:T(8,128)} %bitcast.3), calls=%async_computation | async-start | bytes 524288 | tf_op jit(solution)/shard_map/all_to_all | solution.py:358
  66.8 10.1 %all-to-all-done.refs_0_ = f32[8,32,256]{2,1,0:T(8,128)S(1)} async-done(((f32[8,32,256]{2,1,0:T(8,128)}), f32[8,32,256]{2,1,0:T(8,128)S(1)}, u32[]{:S(2)}, u32[]{:S(2)}) %all-to-all-start) | async-done | bytes 262176 | tf_op jit(solution)/shard_map/all_to_all | solution.py:358
  77.0 12.0 %collective-permute-start.9 = (f32[32,256]{1,0:T(8,128)S(1)}, f32[32,256]{1,0:T(8,128)S(1)}, u32[]{:S(2)}, u32[]{:S(2)}) collective-permute-start(f32[32,256]{1,0:T(8,128)S(1)} %added.2.first), channel_id=1, source_target_pairs={{0,6},{1,7},{32,38},{33,39},{64,70},{65,71},{96,102},{97,103},{128... | collective-permute-start | bytes 98312 | tf_op jit(solution)/shard_map/ppermute | solution.py:275
  90.0 3.4 %collective-permute-done.8.third = f32[32,256]{1,0:T(8,128)S(1)} collective-permute-done((f32[32,256]{1,0:T(8,128)S(1)}, f32[32,256]{1,0:T(8,128)S(1)}, u32[]{:S(2)}, u32[]{:S(2)}) %collective-permute-start.8) | collective-permute-done | bytes 32800 | tf_op jit(solution)/shard_map/ppermute | solution.py:275
  94.6 2.6 %collective-permute-start.17 = (f32[2,128,256]{2,1,0:T(8,128)S(1)}, f32[2,128,256]{2,1,0:T(8,128)S(1)}, u32[]{:S(2)}, u32[]{:S(2)}) collective-permute-start(f32[2,128,256]{2,1,0:T(8,128)S(1)} %get-tuple-element.25), channel_id=1, source_target_pairs={{0,16},{16,32},{32,48},{48,64},{64,80},{80,96},{96,112},{112,128},... | collective-permute-start | bytes 786440 | tf_op jit(solution)/shard_map/ppermute | solution.py:24
  97.1 1.6 %collective-permute-start.16 = (f32[32,256]{1,0:T(8,128)S(1)}, f32[32,256]{1,0:T(8,128)S(1)}, u32[]{:S(2)}, u32[]{:S(2)}) collective-permute-start(f32[32,256]{1,0:T(8,128)S(1)} %get-tuple-element.24.refs_0_), channel_id=1, source_target_pairs={{0,24},{1,25},{32,56},{33,57},{64,88},{65,89},{96,120},{97,121},{1... | collective-permute-start | bytes 98312 | tf_op jit(solution)/shard_map/ppermute | solution.py:275
  100.9 2.1 %collective-permute-done.15.refs_2_ = f32[32,256]{1,0:T(8,128)S(1)} collective-permute-done((f32[32,256]{1,0:T(8,128)S(1)}, f32[32,256]{1,0:T(8,128)S(1)}, u32[]{:S(2)}, u32[]{:S(2)}) %collective-permute-start.15) | collective-permute-done | bytes 32800 | tf_op jit(solution)/shard_map/ppermute | solution.py:275
  104.4 11.0 %all-to-all-start.1 = ((f32[8,32,256]{2,1,0:T(8,128)}), f32[8,32,256]{2,1,0:T(8,128)S(1)}, u32[]{:S(2)}, u32[]{:S(2)}) async-start(f32[8,32,256]{2,1,0:T(8,128)} %broadcast_in_dim.3), calls=%async_computation.1 | async-start | bytes 524288 | tf_op jit(solution)/shard_map/all_to_all | solution.py:358
  115.4 1.3 collective-permute-start.18
  116.7 9.4 %all-to-all-done.1 = f32[8,32,256]{2,1,0:T(8,128)S(1)} async-done(((f32[8,32,256]{2,1,0:T(8,128)}), f32[8,32,256]{2,1,0:T(8,128)S(1)}, u32[]{:S(2)}, u32[]{:S(2)}) %all-to-all-start.1) | async-done | bytes 262176 | tf_op jit(solution)/shard_map/all_to_all | solution.py:358
  126.1 2.1 %collective-permute-start.19 = (f32[256,256]{1,0:T(8,128)S(1)}, f32[256,256]{1,0:T(8,128)S(1)}, u32[]{:S(2)}, u32[]{:S(2)}) collective-permute-start(f32[256,256]{1,0:T(8,128)S(1)} %bitcast.5), channel_id=1, source_target_pairs={{0,1},{1,0},{32,33},{33,32},{64,65},{65,64},{96,97},{97,96},{128,1... | collective-permute-start | bytes 786440 | tf_op jit(solution)/shard_map/ppermute | solution.py:275
  128.3 3.3 %combined.1 = f32[2,512,512]{2,1,0:T(8,128)} custom-call(s32[3]{0:T(128)S(1)} %copy-done.1, f32[2,512,512]{2,1,0:T(8,128)} %get-tuple-element.16.tile_hbm, f32[2,512,256]{2,1,0:T(8,128)S(1)} %get-tuple-element.23.left_hbm, f32[2,512,256]{2,1,0:T(8,128)S(1)} %collective-permute-done.13.seam_hbm, ...), custom_call_target="tpu_custom_call", output_to_operand_aliasing={{}: (1, {})} | custom-call | flops 1000000 | bytes 6291456 | tf_op jit(solution)/shard_map/combined/pallas_call | solution.py:241
  131.5 1.4 %both_planes.1 = f32[2,256,256]{2,1,0:T(8,128)} custom-call(s32[3]{0:T(128)S(1)} %copy-done.1, f32[256,256]{1,0:T(8,128)S(1)} %bitcast.6, f32[256,256]{1,0:T(8,128)S(1)} %collective-permute-done.19.other_hbm), custom_call_target="tpu_custom_call" | custom-call | tf_op jit(solution)/shard_map/both_planes/pallas_call | solution.py:345
  (41 shorter events, 11.5 us)
Async XLA Ops:
  2.2 11.0 %collective-permute-start.4 = (f32[2,256,256]{2,1,0:T(8,128)S(1)}, f32[2,256,256]{2,1,0:T(8,128)S(1)}, u32[]{:S(2)}, u32[]{:S(2)}) collective-permute-start(f32[2,256,256]{2,1,0:T(8,128)S(1)} %get-tuple-element.30), channel_id=1, source_target_pairs={{8,0},{24,16},{40,32},{56,48},{72,64},{88,80},{104,96},{120,112},{... | collective-permute-start | bytes 1572872 | tf_op jit(solution)/shard_map/ppermute | solution.py:370
  2.9 14.5 %collective-permute-start.1 = (f32[2,256,256]{2,1,0:T(8,128)S(1)}, f32[2,256,256]{2,1,0:T(8,128)S(1)}, u32[]{:S(2)}, u32[]{:S(2)}) collective-permute-start(f32[2,256,256]{2,1,0:T(8,128)S(1)} %get-tuple-element.32), channel_id=1, source_target_pairs={{16,0},{32,16},{48,32},{64,48},{80,64},{96,80},{112,96},{128,112},... | collective-permute-start | bytes 1572872 | tf_op jit(solution)/shard_map/ppermute | solution.py:24
  4.2 31.9 %collective-permute-start.2 = (f32[2,256,256]{2,1,0:T(8,128)S(1)}, f32[2,256,256]{2,1,0:T(8,128)}, u32[]{:S(2)}, u32[]{:S(2)}) collective-permute-start(f32[2,256,256]{2,1,0:T(8,128)S(1)} %get-tuple-element.32), channel_id=1, source_target_pairs={{1,0},{2,1},{3,2},{4,3},{5,4},{6,5},{7,6},{8,7},{9,8},{10,9},{11,1... | collective-permute-start | bytes 1572872 | tf_op jit(solution)/shard_map/ppermute | solution.py:24
  10.0 26.2 %collective-permute-start.3 = (f32[2,256,256]{2,1,0:T(8,128)S(1)}, f32[2,256,256]{2,1,0:T(8,128)}, u32[]{:S(2)}, u32[]{:S(2)}) collective-permute-start(f32[2,256,256]{2,1,0:T(8,128)S(1)} %get-tuple-element.31), channel_id=1, source_target_pairs={{1,0},{2,1},{3,2},{4,3},{5,4},{6,5},{7,6},{9,8},{10,9},{11,10},{12... | collective-permute-start | bytes 1572872 | tf_op jit(solution)/shard_map/ppermute | solution.py:374
  11.9 24.2 %collective-permute-start = (f32[2,256,256]{2,1,0:T(8,128)S(1)}, f32[2,256,256]{2,1,0:T(8,128)}, u32[]{:S(2)}, u32[]{:S(2)}) collective-permute-start(f32[2,256,256]{2,1,0:T(8,128)S(1)} %get-tuple-element.33), channel_id=1, source_target_pairs={{16,0},{32,16},{48,32},{64,48},{80,64},{96,80},{112,96},{128,112},... | collective-permute-start | bytes 1572872 | tf_op jit(solution)/shard_map/ppermute | solution.py:24
  17.5 18.9 %copy-start.3 = (f32[2,256,256]{2,1,0:T(8,128)}, f32[2,256,256]{2,1,0:T(8,128)S(1)}, u32[]{:S(2)}) copy-start(f32[2,256,256]{2,1,0:T(8,128)S(1)} %collective-permute-done.1.below0_hbm) | copy-start | bytes 1572868
  17.5 18.8 %collective-permute-start.5 = (f32[2,256,256]{2,1,0:T(8,128)S(1)}, f32[2,256,256]{2,1,0:T(8,128)S(1)}, u32[]{:S(2)}, u32[]{:S(2)}) collective-permute-start(f32[2,256,256]{2,1,0:T(8,128)S(1)} %broadcast_select_fusion), channel_id=1, source_target_pairs={{1,0},{2,1},{3,2},{4,3},{5,4},{6,5},{7,6},{9,8},{10,9},{11,10},{12... | collective-permute-start | bytes 1572872 | tf_op jit(solution)/shard_map/ppermute | solution.py:375
  47.4 46.0 %collective-permute-start.12 = (f32[2,512,256]{2,1,0:T(8,128)}, f32[2,512,256]{2,1,0:T(8,128)S(1)}, u32[]{:S(2)}, u32[]{:S(2)}) collective-permute-start(f32[2,512,256]{2,1,0:T(8,128)} %get-tuple-element.22), channel_id=1, source_target_pairs={{0,1},{1,2},{2,3},{3,4},{4,5},{5,6},{6,7},{8,9},{9,10},{10,11},{11... | collective-permute-start | bytes 3145736 | tf_op jit(solution)/shard_map/ppermute | solution.py:394
  49.3 7.9 %collective-permute-start.6 = (f32[256,256]{1,0:T(8,128)}, f32[256,256]{1,0:T(8,128)S(1)}, u32[]{:S(2)}, u32[]{:S(2)}) collective-permute-start(f32[256,256]{1,0:T(8,128)} %get-tuple-element.18), channel_id=1, source_target_pairs={{0,1},{1,0},{32,33},{33,32},{64,65},{65,64},{96,97},{97,96},{128,1... | collective-permute-start | bytes 786440 | tf_op jit(solution)/shard_map/ppermute | solution.py:275
  54.0 35.0 %collective-permute-start.10 = (f32[2,256,256]{2,1,0:T(8,128)}, f32[2,256,256]{2,1,0:T(8,128)S(1)}, u32[]{:S(2)}, u32[]{:S(2)}) collective-permute-start(f32[2,256,256]{2,1,0:T(8,128)} %get-tuple-element.20), channel_id=1, source_target_pairs={{0,1},{1,2},{2,3},{3,4},{4,5},{5,6},{6,7},{7,8},{8,9},{9,10},{10,1... | collective-permute-start | bytes 1572872 | tf_op jit(solution)/shard_map/ppermute | solution.py:24
  56.0 33.1 %collective-permute-start.11 = (f32[2,256,256]{2,1,0:T(8,128)}, f32[2,256,256]{2,1,0:T(8,128)S(1)}, u32[]{:S(2)}, u32[]{:S(2)}) collective-permute-start(f32[2,256,256]{2,1,0:T(8,128)} %get-tuple-element.21), channel_id=1, source_target_pairs={{0,16},{16,32},{32,48},{48,64},{64,80},{80,96},{96,112},{112,128},... | collective-permute-start | bytes 1572872 | tf_op jit(solution)/shard_map/ppermute | solution.py:24
  59.0 18.0 %all-to-all-start = ((f32[8,32,256]{2,1,0:T(8,128)}), f32[8,32,256]{2,1,0:T(8,128)S(1)}, u32[]{:S(2)}, u32[]{:S(2)}) async-start(f32[8,32,256]{2,1,0:T(8,128)} %bitcast.3), calls=%async_computation | async-start | bytes 524288 | tf_op jit(solution)/shard_map/all_to_all | solution.py:358
  66.1 62.2 %copy-start.1 = (s32[3]{0:T(128)S(1)}, s32[3]{0:T(128)}, u32[]{:S(2)}) copy-start(s32[3]{0:T(128)} %pad_add_fusion.place_ref) | copy-start | bytes 40
  66.1 62.2 %collective-permute-start.13 = (f32[2,512,256]{2,1,0:T(8,128)}, f32[2,512,256]{2,1,0:T(8,128)S(1)}, u32[]{:S(2)}, u32[]{:S(2)}) collective-permute-start(f32[2,512,256]{2,1,0:T(8,128)} %get-tuple-element.22), channel_id=1, source_target_pairs={{7,8},{23,24},{39,40},{55,56},{71,72},{87,88},{103,104},{119,120},... | collective-permute-start | bytes 3145736 | tf_op jit(solution)/shard_map/ppermute | solution.py:395
  77.0 13.1 %collective-permute-start.9 = (f32[32,256]{1,0:T(8,128)S(1)}, f32[32,256]{1,0:T(8,128)S(1)}, u32[]{:S(2)}, u32[]{:S(2)}) collective-permute-start(f32[32,256]{1,0:T(8,128)S(1)} %added.2.first), channel_id=1, source_target_pairs={{0,6},{1,7},{32,38},{33,39},{64,70},{65,71},{96,102},{97,103},{128... | collective-permute-start | bytes 98312 | tf_op jit(solution)/shard_map/ppermute | solution.py:275
  89.0 4.4 %collective-permute-start.8 = (f32[32,256]{1,0:T(8,128)S(1)}, f32[32,256]{1,0:T(8,128)S(1)}, u32[]{:S(2)}, u32[]{:S(2)}) collective-permute-start(f32[32,256]{1,0:T(8,128)S(1)} %added.2.first), channel_id=1, source_target_pairs={{0,4},{1,5},{32,36},{33,37},{64,68},{65,69},{96,100},{97,101},{128... | collective-permute-start | bytes 98312 | tf_op jit(solution)/shard_map/ppermute | solution.py:275
  89.0 4.4 %collective-permute-start.7 = (f32[32,256]{1,0:T(8,128)S(1)}, f32[32,256]{1,0:T(8,128)S(1)}, u32[]{:S(2)}, u32[]{:S(2)}) collective-permute-start(f32[32,256]{1,0:T(8,128)S(1)} %added.2.first), channel_id=1, source_target_pairs={{0,2},{1,3},{32,34},{33,35},{64,66},{65,67},{96,98},{97,99},{128,1... | collective-permute-start | bytes 98312 | tf_op jit(solution)/shard_map/ppermute | solution.py:275
  94.6 9.1 %collective-permute-start.17 = (f32[2,128,256]{2,1,0:T(8,128)S(1)}, f32[2,128,256]{2,1,0:T(8,128)S(1)}, u32[]{:S(2)}, u32[]{:S(2)}) collective-permute-start(f32[2,128,256]{2,1,0:T(8,128)S(1)} %get-tuple-element.25), channel_id=1, source_target_pairs={{0,16},{16,32},{32,48},{48,64},{64,80},{80,96},{96,112},{112,128},... | collective-permute-start | bytes 786440 | tf_op jit(solution)/shard_map/ppermute | solution.py:24
  97.1 3.7 %collective-permute-start.16 = (f32[32,256]{1,0:T(8,128)S(1)}, f32[32,256]{1,0:T(8,128)S(1)}, u32[]{:S(2)}, u32[]{:S(2)}) collective-permute-start(f32[32,256]{1,0:T(8,128)S(1)} %get-tuple-element.24.refs_0_), channel_id=1, source_target_pairs={{0,24},{1,25},{32,56},{33,57},{64,88},{65,89},{96,120},{97,121},{1... | collective-permute-start | bytes 98312 | tf_op jit(solution)/shard_map/ppermute | solution.py:275
  98.7 4.3 %collective-permute-start.15 = (f32[32,256]{1,0:T(8,128)S(1)}, f32[32,256]{1,0:T(8,128)S(1)}, u32[]{:S(2)}, u32[]{:S(2)}) collective-permute-start(f32[32,256]{1,0:T(8,128)S(1)} %get-tuple-element.24.refs_0_), channel_id=1, source_target_pairs={{0,16},{1,17},{32,48},{33,49},{64,80},{65,81},{96,112},{97,113},{1... | collective-permute-start | bytes 98312 | tf_op jit(solution)/shard_map/ppermute | solution.py:275
  99.7 4.0 %collective-permute-start.14 = (f32[32,256]{1,0:T(8,128)S(1)}, f32[32,256]{1,0:T(8,128)S(1)}, u32[]{:S(2)}, u32[]{:S(2)}) collective-permute-start(f32[32,256]{1,0:T(8,128)S(1)} %get-tuple-element.24.refs_0_), channel_id=1, source_target_pairs={{0,8},{1,9},{32,40},{33,41},{64,72},{65,73},{96,104},{97,105},{128... | collective-permute-start | bytes 98312 | tf_op jit(solution)/shard_map/ppermute | solution.py:275
  104.4 21.7 %all-to-all-start.1 = ((f32[8,32,256]{2,1,0:T(8,128)}), f32[8,32,256]{2,1,0:T(8,128)S(1)}, u32[]{:S(2)}, u32[]{:S(2)}) async-start(f32[8,32,256]{2,1,0:T(8,128)} %broadcast_in_dim.3), calls=%async_computation.1 | async-start | bytes 524288 | tf_op jit(solution)/shard_map/all_to_all | solution.py:358
  115.4 12.8 %collective-permute-start.18 = (f32[2,128,256]{2,1,0:T(8,128)}, f32[2,128,256]{2,1,0:T(8,128)S(1)}, u32[]{:S(2)}, u32[]{:S(2)}) collective-permute-start(f32[2,128,256]{2,1,0:T(8,128)} %copy-done.2), channel_id=1, source_target_pairs={{0,16},{16,32},{32,48},{48,64},{64,80},{80,96},{96,112},{112,128},... | collective-permute-start | bytes 786440 | tf_op jit(solution)/shard_map/ppermute | solution.py:24
  126.1 5.4 %collective-permute-start.19 = (f32[256,256]{1,0:T(8,128)S(1)}, f32[256,256]{1,0:T(8,128)S(1)}, u32[]{:S(2)}, u32[]{:S(2)}) collective-permute-start(f32[256,256]{1,0:T(8,128)S(1)} %bitcast.5), channel_id=1, source_target_pairs={{0,1},{1,0},{32,33},{33,32},{64,65},{65,64},{96,97},{97,96},{128,1... | collective-permute-start | bytes 786440 | tf_op jit(solution)/shard_map/ppermute | solution.py:275
  (3 other events, 11.0 us)

commit v4 on v2

--- a/solution.py
+++ b/solution.py
@@ -66,7 +66,7 @@
 
 def slots_kernel(
     window, tile,
-    counts_ref, pos_ref, place_ref, object_hbm, right0_hbm, right1_hbm, below0_hbm, below1_hbm,
+    counts_ref, pos_ref, place_ref, object_hbm, below1_hbm, below0_hbm, right0_hbm, right1_hbm,
     corner_hbm, probe_hbm, amp_hbm, tables_hbm,
     tile_out, right_out, below0_out, below1_out, corner_out, keep_out, send_out,
     ext, grad, probe, turned, amp, tables, patch, probe_grad, sems,
@@ -305,6 +305,47 @@
     return [moved(value, **{axis: d}) for d in range(1, SIZES[axis])]
 
 
+def idle_kernel(array_ref, out_ref):
+    del array_ref, out_ref
+
+
+def awaited(array, flops):
+    return pl.pallas_call(
+        idle_kernel,
+        out_shape=jax.ShapeDtypeStruct(array.shape, array.dtype),
+        in_specs=[HBM],
+        out_specs=HBM,
+        input_output_aliases={0: 0},
+        cost_estimate=pl.CostEstimate(flops=flops, bytes_accessed=0, transcendentals=0),
+        compiler_params=pltpu.CompilerParams(vmem_limit_bytes=2 * MIB, has_side_effects=True),
+        name="awaited",
+    )(array)
+
+
+def planes_kernel(place_ref, own_hbm, other_hbm, out_hbm, sems):
+    core = place_ref[0]
+    copies = [
+        pltpu.make_async_copy(own_hbm, out_hbm.at[core], sems.at[0]),
+        pltpu.make_async_copy(other_hbm, out_hbm.at[1 - core], sems.at[1]),
+    ]
+    for copy in copies:
+        copy.start()
+    for copy in copies:
+        copy.wait()
+
+
+def both_planes(where, own, other):
+    return pl.pallas_call(
+        planes_kernel,
+        out_shape=jax.ShapeDtypeStruct((2,) + own.shape, own.dtype),
+        in_specs=[SMEM, HBM, HBM],
+        out_specs=HBM,
+        scratch_shapes=[pltpu.SemaphoreType.DMA((2,))],
+        compiler_params=pltpu.CompilerParams(vmem_limit_bytes=2 * MIB),
+        name="both_planes",
+    )(where, own, other)
+
+
 def z_exchange(chunks):
     groups = [[place(x, y, z, c) for z in range(8)] for x in range(4) for y in range(4) for c in range(2)]
     return lax.all_to_all(chunks, AXES, 0, 0, tiled=True, axis_index_groups=groups)
@@ -318,14 +359,14 @@
     own0, own1 = object_field[:, :w, :w], object_field[:, w:, :w]
     plain = [(i + 1, i) for i in range(cols - 1) if i + 1 != seam]
     below0 = shifted(own0, "row", -1)
-    below1 = shifted(object_field[:, :w, w:], "row", -1)
+    below1 = awaited(shifted(object_field[:, :w, w:], "row", -1), 5 * 10**9)
     relayed = lax.ppermute(own1, "col", [(seam, 0)])
     right0 = shifted(own0, "col", -1)
     route = [(r * cols + a, r * cols + b) for r in range(rows) for a, b in plain]
     route += [((r + 1) * cols + seam, r * cols + seam - 1) for r in range(rows - 1)]
     right1 = lax.ppermute(jnp.where(col == seam, own0, own1), AXES, route)
     corner = lax.ppermute(jnp.where(col == 0, relayed, below0), "col", plain + [(0, seam - 1)])
-    return right0, right1, below0, below1, corner
+    return below1, below0, right0, right1, corner
 
 
 def shards(object_field, probe, positions, amplitudes, counts):
@@ -348,14 +389,13 @@
     if (rows, cols) == (16, 16):
         value = keep + moved(send, core=1)
         value = z_exchange(value.reshape(8, window // 8, window))
-        value = added([[value]])[0]
-        parts = [value] + neighbours(value, "x")
-        value, below0_grad, above1, from_left = added([parts, [below0_grad, corner_in]], above1, from_left, vmem=8)
+        value, below0_grad = added([[value], [below0_grad, corner_in]], vmem=8)
         above0 = shifted(below0_grad, "row", 1)
-        value = added([[value] + neighbours(value, "y")])[0]
+        value, above1, from_left = added([[value] + neighbours(value, "x")], above1, from_left)
+        value, above0, from_seam = added([[value] + neighbours(value, "y")], above0, from_seam)
         value = z_exchange(jnp.broadcast_to(value, (8,) + value.shape)).reshape(window, window)
         other = moved(value, core=1)
-        probe_total = jnp.where(core == 0, jnp.stack([value, other]), jnp.stack([other, value]))
+        probe_total = both_planes(where, value, other)
     else:
         above0 = shifted(below0_grad + corner_in, "row", 1)
         probe_total = lax.psum(jnp.where(core == 0, jnp.stack([keep, send]), jnp.stack([send, keep])), AXES)

time: 134 us -> 138 us (1.030)
  the two profiles are of different devices: /device:TPU:32 before, /device:TPU:1 now
where the time goes in v4:
time: 138 us; the launch traced here: 137 us
  starting transfers between devices  72 us (52%)
  waiting for transfers between devices  21.1 us (15%)
  blocking collectives  20.2 us (15%)
  Pallas kernels  14.9 us (11%)
  other arithmetic  4.75 us (3%)
  local copies, waits for them, and re-layouts  2.64 us (2%)
  between operations  1.53 us (1%)
    ppermute x8, starting transfers between devices, moved(): return lax.ppermute(value, AXES, route)  23.7 us
    ppermute x1, starting transfers between devices, halos_in(): lax.ppermute(jnp.where(col == 0, relayed, below0), 'col', plain + [(0, se...  23.7 us
    all_to_all x1, blocking collectives, z_exchange(): lax.all_to_all(chunks, AXES, 0, 0, tiled=True, axis_index_groups=groups)  20.2 us
    ppermute x6, starting transfers between devices, shifted(): return lax.ppermute(block, axis, route)  12.9 us
    ppermute x6, waiting for transfers between devices, shifted(): return lax.ppermute(block, axis, route)  10.9 us
    pallas_call x1, Pallas kernels, slot_terms(): pl.pallas_call(functools.partial(slots_kernel, w, t), out_shape=[f32((2,...  10.2 us
    all_to_all x1, starting transfers between devices, z_exchange(): lax.all_to_all(chunks, AXES, 0, 0, tiled=True, axis_index_groups=groups)  6.45 us
    ppermute x8, waiting for transfers between devices, moved(): return lax.ppermute(value, AXES, route)  6.38 us
  transfers between devices with their start and end apart: 20, of which 8 were waited for; matrix products, arithmetic and copies ran while one was open for 2% of the time, Pallas kernels for 2%

profile of v4, /device:TPU:1, one launch (start us, length us, event | category | flops | bytes accessed | tf_op | source)
XLA Modules:
  0.0 137.0 jit_solution(13696075245792541947)
XLA Ops:
  0.6 2.4 %fusion = (f32[2,256,256]{2,1,0:T(8,128)}, f32[2,256,256]{2,1,0:T(8,128)S(1)}, f32[2,256,256]{2,1,0:T(8,128)S(1)}, f32[2,256,256]{2,1,0:T(8,128)S(1)}) fusion(f32[2,512,512]{2,1,0:T(8,128)} %object_hbm.1, pred[]{:T(512)S(6)} %eq.13), kind=kLoop, calls=%fused_computation.3 | loop fusion | flops 131072 | bytes 3670017 | tf_op jit(solution)/shard_map/slice | solution.py:359
  3.7 1.3 collective-permute-start.1
  6.3 5.7 %collective-permute-start.2 = (f32[2,256,256]{2,1,0:T(8,128)S(1)}, f32[2,256,256]{2,1,0:T(8,128)}, u32[]{:S(2)}, u32[]{:S(2)}) collective-permute-start(f32[2,256,256]{2,1,0:T(8,128)S(1)} %get-tuple-element.34), channel_id=1, source_target_pairs={{1,0},{2,1},{3,2},{4,3},{5,4},{6,5},{7,6},{8,7},{9,8},{10,9},{11,1... | collective-permute-start | bytes 1572872 | tf_op jit(solution)/shard_map/ppermute | solution.py:24
  12.1 1.9 %collective-permute-start.3 = (f32[2,256,256]{2,1,0:T(8,128)S(1)}, f32[2,256,256]{2,1,0:T(8,128)}, u32[]{:S(2)}, u32[]{:S(2)}) collective-permute-start(f32[2,256,256]{2,1,0:T(8,128)S(1)} %get-tuple-element.33), channel_id=1, source_target_pairs={{1,0},{2,1},{3,2},{4,3},{5,4},{6,5},{7,6},{9,8},{10,9},{11,10},{12... | collective-permute-start | bytes 1572872 | tf_op jit(solution)/shard_map/ppermute | solution.py:367
  14.0 4.2 %collective-permute-done.1.below0_hbm = f32[2,256,256]{2,1,0:T(8,128)S(1)} collective-permute-done((f32[2,256,256]{2,1,0:T(8,128)S(1)}, f32[2,256,256]{2,1,0:T(8,128)S(1)}, u32[]{:S(2)}, u32[]{:S(2)}) %collective-permute-start.1) | collective-permute-done | bytes 524320 | tf_op jit(solution)/shard_map/ppermute | solution.py:24
  18.3 23.7 %collective-permute-start.5 = (f32[2,256,256]{2,1,0:T(8,128)S(1)}, f32[2,256,256]{2,1,0:T(8,128)S(1)}, u32[]{:S(2)}, u32[]{:S(2)}) collective-permute-start(f32[2,256,256]{2,1,0:T(8,128)S(1)} %broadcast_select_fusion), channel_id=1, source_target_pairs={{1,0},{2,1},{3,2},{4,3},{5,4},{6,5},{7,6},{9,8},{10,9},{11,10},{12... | collective-permute-start | bytes 1572872 | tf_op jit(solution)/shard_map/ppermute | solution.py:368
  44.9 10.2 %slot_terms.1 = (f32[2,512,512]{2,1,0:T(8,128)}, f32[2,512,256]{2,1,0:T(8,128)}, f32[2,256,256]{2,1,0:T(8,128)}, f32[2,256,256]{2,1,0:T(8,128)}, f32[2,256,256]{...) custom-call(s32[1]{0:T(128)S(6)} %copy.20.counts_ref, s32[2,2]{1,0:T(2,128)} %pos_ref.1, s32[3]{0:T(128)} %pad_add_fusion.place_ref, ...), custom_call_target="tpu_custom_call" | custom-call | flops 3000000000 | bytes 14680064 | tf_op jit(solution)/shard_map/slot_terms/pallas_call | solution.py:181
  55.1 4.7 %collective-permute-start.6 = (f32[256,256]{1,0:T(8,128)}, f32[256,256]{1,0:T(8,128)S(1)}, u32[]{:S(2)}, u32[]{:S(2)}) collective-permute-start(f32[256,256]{1,0:T(8,128)} %get-tuple-element.19), channel_id=1, source_target_pairs={{0,1},{1,0},{32,33},{33,32},{64,65},{65,64},{96,97},{97,96},{128,1... | collective-permute-start | bytes 786440 | tf_op jit(solution)/shard_map/ppermute | solution.py:274
  59.8 1.9 %collective-permute-start.12 = (f32[2,512,256]{2,1,0:T(8,128)}, f32[2,512,256]{2,1,0:T(8,128)S(1)}, u32[]{:S(2)}, u32[]{:S(2)}) collective-permute-start(f32[2,512,256]{2,1,0:T(8,128)} %get-tuple-element.24), channel_id=1, source_target_pairs={{0,1},{1,2},{2,3},{3,4},{4,5},{5,6},{6,7},{8,9},{9,10},{10,11},{11... | collective-permute-start | bytes 3145736 | tf_op jit(solution)/shard_map/ppermute | solution.py:387
  61.7 1.9 %collective-permute-start.7 = (f32[2,256,256]{2,1,0:T(8,128)}, f32[2,256,256]{2,1,0:T(8,128)S(1)}, u32[]{:S(2)}, u32[]{:S(2)}) collective-permute-start(f32[2,256,256]{2,1,0:T(8,128)} %get-tuple-element.21), channel_id=1, source_target_pairs={{0,1},{1,2},{2,3},{3,4},{4,5},{5,6},{6,7},{7,8},{8,9},{9,10},{10,1... | collective-permute-start | bytes 1572872 | tf_op jit(solution)/shard_map/ppermute | solution.py:24
  64.4 1.7 %add.8 = f32[256,256]{1,0:T(8,128)} add(f32[256,256]{1,0:T(8,128)} %get-tuple-element.18, f32[256,256]{1,0:T(8,128)S(1)} %collective-permute-done.6) | non-fusion elementwise | flops 65536 | bytes 786432 | tf_op jit(solution)/shard_map/add | solution.py:390
  66.0 6.5 %all-to-all-start = ((f32[8,32,256]{2,1,0:T(8,128)}), f32[8,32,256]{2,1,0:T(8,128)S(1)}, u32[]{:S(2)}, u32[]{:S(2)}) async-start(f32[8,32,256]{2,1,0:T(8,128)} %bitcast.3), calls=%async_computation | async-start | bytes 524288 | tf_op jit(solution)/shard_map/all_to_all | solution.py:351
  72.5 1.3 collective-permute-start.11
  73.8 5.5 %collective-permute-done.7.refs_2_ = f32[2,256,256]{2,1,0:T(8,128)S(1)} collective-permute-done((f32[2,256,256]{2,1,0:T(8,128)}, f32[2,256,256]{2,1,0:T(8,128)S(1)}, u32[]{:S(2)}, u32[]{:S(2)}) %collective-permute-start.7) | collective-permute-done | bytes 524320 | tf_op jit(solution)/shard_map/ppermute | solution.py:24
  79.3 3.8 %all-to-all-done.refs_0_ = f32[8,32,256]{2,1,0:T(8,128)S(1)} async-done(((f32[8,32,256]{2,1,0:T(8,128)}), f32[8,32,256]{2,1,0:T(8,128)S(1)}, u32[]{:S(2)}, u32[]{:S(2)}) %all-to-all-start) | async-done | bytes 262176 | tf_op jit(solution)/shard_map/all_to_all | solution.py:351
  84.3 1.3 collective-permute-start.16
  85.6 7.5 %collective-permute-start.10 = (f32[32,256]{1,0:T(8,128)S(1)}, f32[32,256]{1,0:T(8,128)S(1)}, u32[]{:S(2)}, u32[]{:S(2)}) collective-permute-start(f32[32,256]{1,0:T(8,128)S(1)} %get-tuple-element.22.refs_0_), channel_id=1, source_target_pairs={{0,6},{1,7},{32,38},{33,39},{64,70},{65,71},{96,102},{97,103},{128... | collective-permute-start | bytes 98312 | tf_op jit(solution)/shard_map/ppermute | solution.py:274
  95.7 2.8 %collective-permute-done.9.refs_2_ = f32[32,256]{1,0:T(8,128)S(1)} collective-permute-done((f32[32,256]{1,0:T(8,128)S(1)}, f32[32,256]{1,0:T(8,128)S(1)}, u32[]{:S(2)}, u32[]{:S(2)}) %collective-permute-start.9) | collective-permute-done | bytes 32800 | tf_op jit(solution)/shard_map/ppermute | solution.py:274
  99.0 3.7 %collective-permute-start.14 = (f32[32,256]{1,0:T(8,128)S(1)}, f32[32,256]{1,0:T(8,128)S(1)}, u32[]{:S(2)}, u32[]{:S(2)}) collective-permute-start(f32[32,256]{1,0:T(8,128)S(1)} %get-tuple-element.26.refs_0_), channel_id=1, source_target_pairs={{0,16},{1,17},{32,48},{33,49},{64,80},{65,81},{96,112},{97,113},{1... | collective-permute-start | bytes 98312 | tf_op jit(solution)/shard_map/ppermute | solution.py:274
  103.4 2.4 %collective-permute-done.14.refs_2_ = f32[32,256]{1,0:T(8,128)S(1)} collective-permute-done((f32[32,256]{1,0:T(8,128)S(1)}, f32[32,256]{1,0:T(8,128)S(1)}, u32[]{:S(2)}, u32[]{:S(2)}) %collective-permute-start.14) | collective-permute-done | bytes 32800 | tf_op jit(solution)/shard_map/ppermute | solution.py:274
  106.7 20.2 %all_to_all.10 = f32[8,32,256]{2,1,0:T(8,128)S(1)} all-to-all(f32[8,32,256]{2,1,0:T(8,128)S(1)} %broadcast_in_dim.3), channel_id=1, replica_groups={{0,32,64,96,128,160,192,224},{1,33,65,97,129,161,193,225},{8,40,72,104,..., dimensions={0} | all-to-all | bytes 524288 | tf_op jit(solution)/shard_map/all_to_all | solution.py:351
  126.9 5.6 %collective-permute-start.18 = (f32[256,256]{1,0:T(8,128)S(1)}, f32[256,256]{1,0:T(8,128)S(1)}, u32[]{:S(2)}, u32[]{:S(2)}) collective-permute-start(f32[256,256]{1,0:T(8,128)S(1)} %bitcast.5), channel_id=1, source_target_pairs={{0,1},{1,0},{32,33},{33,32},{64,65},{65,64},{96,97},{97,96},{128,1... | collective-permute-start | bytes 786440 | tf_op jit(solution)/shard_map/ppermute | solution.py:274
  132.4 3.2 %combined.1 = f32[2,512,512]{2,1,0:T(8,128)} custom-call(s32[3]{0:T(128)S(1)} %copy-done.1, f32[2,512,512]{2,1,0:T(8,128)} %get-tuple-element.17.tile_hbm, f32[2,512,256]{2,1,0:T(8,128)S(1)} %get-tuple-element.25.left_hbm, f32[2,512,256]{2,1,0:T(8,128)S(1)} %get-tuple-element.28.seam_hbm, ...), custom_call_target="tpu_custom_call", output_to_operand_aliasing={{}: (1, {})} | custom-call | flops 1000000 | bytes 6291456 | tf_op jit(solution)/shard_map/combined/pallas_call | solution.py:240
  135.7 1.4 both_planes.1
  (39 shorter events, 10.7 us)
Async XLA Ops:
  3.0 11.0 %collective-permute-start.4 = (f32[2,256,256]{2,1,0:T(8,128)}, f32[2,256,256]{2,1,0:T(8,128)S(1)}, u32[]{:S(2)}, u32[]{:S(2)}) collective-permute-start(f32[2,256,256]{2,1,0:T(8,128)} %get-tuple-element.32), channel_id=1, source_target_pairs={{8,0},{24,16},{40,32},{56,48},{72,64},{88,80},{104,96},{120,112},{... | collective-permute-start | bytes 1572872 | tf_op jit(solution)/shard_map/ppermute | solution.py:363
  3.7 14.5 %collective-permute-start.1 = (f32[2,256,256]{2,1,0:T(8,128)S(1)}, f32[2,256,256]{2,1,0:T(8,128)S(1)}, u32[]{:S(2)}, u32[]{:S(2)}) collective-permute-start(f32[2,256,256]{2,1,0:T(8,128)S(1)} %get-tuple-element.34), channel_id=1, source_target_pairs={{16,0},{32,16},{48,32},{64,48},{80,64},{96,80},{112,96},{128,112},... | collective-permute-start | bytes 1572872 | tf_op jit(solution)/shard_map/ppermute | solution.py:24
  5.0 38.3 %collective-permute-start = (f32[2,256,256]{2,1,0:T(8,128)S(1)}, f32[2,256,256]{2,1,0:T(8,128)S(1)}, u32[]{:S(2)}, u32[]{:S(2)}) collective-permute-start(f32[2,256,256]{2,1,0:T(8,128)S(1)} %get-tuple-element.35), channel_id=1, source_target_pairs={{16,0},{32,16},{48,32},{64,48},{80,64},{96,80},{112,96},{128,112},... | collective-permute-start | bytes 1572872 | tf_op jit(solution)/shard_map/ppermute | solution.py:24
  6.3 37.8 %collective-permute-start.2 = (f32[2,256,256]{2,1,0:T(8,128)S(1)}, f32[2,256,256]{2,1,0:T(8,128)}, u32[]{:S(2)}, u32[]{:S(2)}) collective-permute-start(f32[2,256,256]{2,1,0:T(8,128)S(1)} %get-tuple-element.34), channel_id=1, source_target_pairs={{1,0},{2,1},{3,2},{4,3},{5,4},{6,5},{7,6},{8,7},{9,8},{10,9},{11,1... | collective-permute-start | bytes 1572872 | tf_op jit(solution)/shard_map/ppermute | solution.py:24
  12.1 32.0 %collective-permute-start.3 = (f32[2,256,256]{2,1,0:T(8,128)S(1)}, f32[2,256,256]{2,1,0:T(8,128)}, u32[]{:S(2)}, u32[]{:S(2)}) collective-permute-start(f32[2,256,256]{2,1,0:T(8,128)S(1)} %get-tuple-element.33), channel_id=1, source_target_pairs={{1,0},{2,1},{3,2},{4,3},{5,4},{6,5},{7,6},{9,8},{10,9},{11,10},{12... | collective-permute-start | bytes 1572872 | tf_op jit(solution)/shard_map/ppermute | solution.py:367
  18.2 25.0 %copy-start.3 = (f32[2,256,256]{2,1,0:T(8,128)}, f32[2,256,256]{2,1,0:T(8,128)S(1)}, u32[]{:S(2)}) copy-start(f32[2,256,256]{2,1,0:T(8,128)S(1)} %collective-permute-done.1.below0_hbm) | copy-start | bytes 1572868
  18.3 25.8 %collective-permute-start.5 = (f32[2,256,256]{2,1,0:T(8,128)S(1)}, f32[2,256,256]{2,1,0:T(8,128)S(1)}, u32[]{:S(2)}, u32[]{:S(2)}) collective-permute-start(f32[2,256,256]{2,1,0:T(8,128)S(1)} %broadcast_select_fusion), channel_id=1, source_target_pairs={{1,0},{2,1},{3,2},{4,3},{5,4},{6,5},{7,6},{9,8},{10,9},{11,10},{12... | collective-permute-start | bytes 1572872 | tf_op jit(solution)/shard_map/ppermute | solution.py:368
  43.3 0.8 copy-start.2
  55.1 9.2 %collective-permute-start.6 = (f32[256,256]{1,0:T(8,128)}, f32[256,256]{1,0:T(8,128)S(1)}, u32[]{:S(2)}, u32[]{:S(2)}) collective-permute-start(f32[256,256]{1,0:T(8,128)} %get-tuple-element.19), channel_id=1, source_target_pairs={{0,1},{1,0},{32,33},{33,32},{64,65},{65,64},{96,97},{97,96},{128,1... | collective-permute-start | bytes 786440 | tf_op jit(solution)/shard_map/ppermute | solution.py:274
  59.8 39.1 %collective-permute-start.12 = (f32[2,512,256]{2,1,0:T(8,128)}, f32[2,512,256]{2,1,0:T(8,128)S(1)}, u32[]{:S(2)}, u32[]{:S(2)}) collective-permute-start(f32[2,512,256]{2,1,0:T(8,128)} %get-tuple-element.24), channel_id=1, source_target_pairs={{0,1},{1,2},{2,3},{3,4},{4,5},{5,6},{6,7},{8,9},{9,10},{10,11},{11... | collective-permute-start | bytes 3145736 | tf_op jit(solution)/shard_map/ppermute | solution.py:387
  61.7 17.7 %collective-permute-start.7 = (f32[2,256,256]{2,1,0:T(8,128)}, f32[2,256,256]{2,1,0:T(8,128)S(1)}, u32[]{:S(2)}, u32[]{:S(2)}) collective-permute-start(f32[2,256,256]{2,1,0:T(8,128)} %get-tuple-element.21), channel_id=1, source_target_pairs={{0,1},{1,2},{2,3},{3,4},{4,5},{5,6},{6,7},{7,8},{8,9},{9,10},{10,1... | collective-permute-start | bytes 1572872 | tf_op jit(solution)/shard_map/ppermute | solution.py:24
  63.6 39.8 %collective-permute-start.17 = (f32[2,512,256]{2,1,0:T(8,128)}, f32[2,512,256]{2,1,0:T(8,128)S(1)}, u32[]{:S(2)}, u32[]{:S(2)}) collective-permute-start(f32[2,512,256]{2,1,0:T(8,128)} %get-tuple-element.24), channel_id=1, source_target_pairs={{7,8},{23,24},{39,40},{55,56},{71,72},{87,88},{103,104},{119,120},... | collective-permute-start | bytes 3145736 | tf_op jit(solution)/shard_map/ppermute | solution.py:388
  66.0 17.1 %all-to-all-start = ((f32[8,32,256]{2,1,0:T(8,128)}), f32[8,32,256]{2,1,0:T(8,128)S(1)}, u32[]{:S(2)}, u32[]{:S(2)}) async-start(f32[8,32,256]{2,1,0:T(8,128)} %bitcast.3), calls=%async_computation | async-start | bytes 524288 | tf_op jit(solution)/shard_map/all_to_all | solution.py:351
  72.5 21.8 %collective-permute-start.11 = (f32[2,256,256]{2,1,0:T(8,128)}, f32[2,256,256]{2,1,0:T(8,128)S(1)}, u32[]{:S(2)}, u32[]{:S(2)}) collective-permute-start(f32[2,256,256]{2,1,0:T(8,128)} %get-tuple-element.23), channel_id=1, source_target_pairs={{0,16},{16,32},{32,48},{48,64},{64,80},{80,96},{96,112},{112,128},... | collective-permute-start | bytes 1572872 | tf_op jit(solution)/shard_map/ppermute | solution.py:24
  83.2 1.0 copy-start
  84.3 22.4 %collective-permute-start.16 = (f32[2,256,256]{2,1,0:T(8,128)S(1)}, f32[2,256,256]{2,1,0:T(8,128)S(1)}, u32[]{:S(2)}, u32[]{:S(2)}) collective-permute-start(f32[2,256,256]{2,1,0:T(8,128)S(1)} %get-tuple-element.27), channel_id=1, source_target_pairs={{0,16},{16,32},{32,48},{48,64},{64,80},{80,96},{96,112},{112,128},... | collective-permute-start | bytes 1572872 | tf_op jit(solution)/shard_map/ppermute | solution.py:24
  85.6 46.8 %copy-start.1 = (s32[3]{0:T(128)S(1)}, s32[3]{0:T(128)}, u32[]{:S(2)}) copy-start(s32[3]{0:T(128)} %pad_add_fusion.place_ref) | copy-start | bytes 40
  85.6 9.2 %collective-permute-start.10 = (f32[32,256]{1,0:T(8,128)S(1)}, f32[32,256]{1,0:T(8,128)S(1)}, u32[]{:S(2)}, u32[]{:S(2)}) collective-permute-start(f32[32,256]{1,0:T(8,128)S(1)} %get-tuple-element.22.refs_0_), channel_id=1, source_target_pairs={{0,6},{1,7},{32,38},{33,39},{64,70},{65,71},{96,102},{97,103},{128... | collective-permute-start | bytes 98312 | tf_op jit(solution)/shard_map/ppermute | solution.py:274
  94.3 4.3 %collective-permute-start.9 = (f32[32,256]{1,0:T(8,128)S(1)}, f32[32,256]{1,0:T(8,128)S(1)}, u32[]{:S(2)}, u32[]{:S(2)}) collective-permute-start(f32[32,256]{1,0:T(8,128)S(1)} %get-tuple-element.22.refs_0_), channel_id=1, source_target_pairs={{0,4},{1,5},{32,36},{33,37},{64,68},{65,69},{96,100},{97,101},{128... | collective-permute-start | bytes 98312 | tf_op jit(solution)/shard_map/ppermute | solution.py:274
  94.8 4.0 %collective-permute-start.8 = (f32[32,256]{1,0:T(8,128)S(1)}, f32[32,256]{1,0:T(8,128)S(1)}, u32[]{:S(2)}, u32[]{:S(2)}) collective-permute-start(f32[32,256]{1,0:T(8,128)S(1)} %get-tuple-element.22.refs_0_), channel_id=1, source_target_pairs={{0,2},{1,3},{32,34},{33,35},{64,66},{65,67},{96,98},{97,99},{128,1... | collective-permute-start | bytes 98312 | tf_op jit(solution)/shard_map/ppermute | solution.py:274
  98.9 4.5 %collective-permute-start.15 = (f32[32,256]{1,0:T(8,128)S(1)}, f32[32,256]{1,0:T(8,128)S(1)}, u32[]{:S(2)}, u32[]{:S(2)}) collective-permute-start(f32[32,256]{1,0:T(8,128)S(1)} %get-tuple-element.26.refs_0_), channel_id=1, source_target_pairs={{0,24},{1,25},{32,56},{33,57},{64,88},{65,89},{96,120},{97,121},{1... | collective-permute-start | bytes 98312 | tf_op jit(solution)/shard_map/ppermute | solution.py:274
  99.0 6.9 %collective-permute-start.14 = (f32[32,256]{1,0:T(8,128)S(1)}, f32[32,256]{1,0:T(8,128)S(1)}, u32[]{:S(2)}, u32[]{:S(2)}) collective-permute-start(f32[32,256]{1,0:T(8,128)S(1)} %get-tuple-element.26.refs_0_), channel_id=1, source_target_pairs={{0,16},{1,17},{32,48},{33,49},{64,80},{65,81},{96,112},{97,113},{1... | collective-permute-start | bytes 98312 | tf_op jit(solution)/shard_map/ppermute | solution.py:274
  102.7 4.0 %collective-permute-start.13 = (f32[32,256]{1,0:T(8,128)S(1)}, f32[32,256]{1,0:T(8,128)S(1)}, u32[]{:S(2)}, u32[]{:S(2)}) collective-permute-start(f32[32,256]{1,0:T(8,128)S(1)} %get-tuple-element.26.refs_0_), channel_id=1, source_target_pairs={{0,8},{1,9},{32,40},{33,41},{64,72},{65,73},{96,104},{97,105},{128... | collective-permute-start | bytes 98312 | tf_op jit(solution)/shard_map/ppermute | solution.py:274
  126.9 8.8 %collective-permute-start.18 = (f32[256,256]{1,0:T(8,128)S(1)}, f32[256,256]{1,0:T(8,128)S(1)}, u32[]{:S(2)}, u32[]{:S(2)}) collective-permute-start(f32[256,256]{1,0:T(8,128)S(1)} %bitcast.5), channel_id=1, source_target_pairs={{0,1},{1,0},{32,33},{33,32},{64,65},{65,64},{96,97},{97,96},{128,1... | collective-permute-start | bytes 786440 | tf_op jit(solution)/shard_map/ppermute | solution.py:274
  (1 other events, 0.8 us)

commit v5 on v4

--- a/solution.py
+++ b/solution.py
@@ -201,30 +201,22 @@
 
 
 def combine_kernel(
-    window, place_ref, tile_hbm, left_hbm, seam_hbm, above0_hbm, above1_hbm, out_hbm, tile, side, above0, above1, sems
+    window, tile_hbm, left_hbm, above0_hbm, above1_hbm, out_hbm, tile, side, above0, above1, sems
 ):
     w, t = window, tile.shape[1]
-    after_seam = place_ref[2]
-    mine = [
+    copies = [
         pltpu.make_async_copy(tile_hbm.at[:, 0:w, :], tile.at[:, 0:w, :], sems.at[0]),
         pltpu.make_async_copy(tile_hbm.at[:, w:t, 0:w], tile.at[:, w:t, 0:w], sems.at[1]),
         pltpu.make_async_copy(above0_hbm, above0, sems.at[2]),
         pltpu.make_async_copy(above1_hbm, above1, sems.at[3]),
+        pltpu.make_async_copy(left_hbm, side, sems.at[4]),
     ]
-    for copy in mine:
+    for copy in copies:
         copy.start()
-
-    def choose(act):
-        for flag, source in enumerate((left_hbm, seam_hbm)):
-            @pl.when(after_seam == flag)
-            def _():
-                act(pltpu.make_async_copy(source, side, sems.at[4]))
-
-    choose(lambda copy: copy.start())
-    for copy in mine:
+    for copy in copies[:-1]:
         copy.wait()
     tile[:, 0:w, w:t] += above1[...]
-    choose(lambda copy: copy.wait())
+    copies[-1].wait()
     tile[:, 0:w, 0:w] += above0[...] + side[:, 0:w]
     top = pltpu.make_async_copy(tile.at[:, 0:w, :], out_hbm.at[:, 0:w, :], sems.at[0])
     top.start()
@@ -235,12 +227,12 @@
     low.wait()
 
 
-def combined(where, tile_grad, from_left, from_seam, above0, above1):
+def combined(tile_grad, from_left, above0, above1):
     t, w = tile_grad.shape[1], from_left.shape[2]
     return pl.pallas_call(
         functools.partial(combine_kernel, w),
         out_shape=jax.ShapeDtypeStruct(tile_grad.shape, jnp.float32),
-        in_specs=[SMEM] + [HBM] * 5,
+        in_specs=[HBM] * 4,
         out_specs=HBM,
         scratch_shapes=[
             pltpu.VMEM((2, t, t), jnp.float32),
@@ -249,11 +241,11 @@
             pltpu.VMEM((2, w, w), jnp.float32),
             pltpu.SemaphoreType.DMA((5,)),
         ],
-        input_output_aliases={1: 0},
+        input_output_aliases={0: 0},
         compiler_params=pltpu.CompilerParams(vmem_limit_bytes=12 * MIB),
-        cost_estimate=pl.CostEstimate(flops=10**6, bytes_accessed=6 * MIB, transcendentals=0),
+        cost_estimate=pl.CostEstimate(flops=5 * 10**9, bytes_accessed=6 * MIB, transcendentals=0),
         name="combined",
-    )(where, tile_grad, from_left, from_seam, above0, above1)
+    )(tile_grad, from_left, above0, above1)
 
 
 def place(x, y, z, core):
@@ -305,23 +297,6 @@
     return [moved(value, **{axis: d}) for d in range(1, SIZES[axis])]
 
 
-def idle_kernel(array_ref, out_ref):
-    del array_ref, out_ref
-
-
-def awaited(array, flops):
-    return pl.pallas_call(
-        idle_kernel,
-        out_shape=jax.ShapeDtypeStruct(array.shape, array.dtype),
-        in_specs=[HBM],
-        out_specs=HBM,
-        input_output_aliases={0: 0},
-        cost_estimate=pl.CostEstimate(flops=flops, bytes_accessed=0, transcendentals=0),
-        compiler_params=pltpu.CompilerParams(vmem_limit_bytes=2 * MIB, has_side_effects=True),
-        name="awaited",
-    )(array)
-
-
 def planes_kernel(place_ref, own_hbm, other_hbm, out_hbm, sems):
     core = place_ref[0]
     copies = [
@@ -359,7 +334,7 @@
     own0, own1 = object_field[:, :w, :w], object_field[:, w:, :w]
     plain = [(i + 1, i) for i in range(cols - 1) if i + 1 != seam]
     below0 = shifted(own0, "row", -1)
-    below1 = awaited(shifted(object_field[:, :w, w:], "row", -1), 5 * 10**9)
+    below1 = shifted(object_field[:, :w, w:], "row", -1)
     relayed = lax.ppermute(own1, "col", [(seam, 0)])
     right0 = shifted(own0, "col", -1)
     route = [(r * cols + a, r * cols + b) for r in range(rows) for a, b in plain]
@@ -375,7 +350,7 @@
     core = col % 2
     seam = lax.axis_size("col") // 2
     halos = halos_in(object_field, window)
-    where = jnp.stack([core, (col == seam - 1).astype(jnp.int32), (col == seam).astype(jnp.int32)])
+    where = jnp.stack([core, (col == seam - 1).astype(jnp.int32)])
     tile_grad, right_grad, below0_grad, below1_grad, corner_grad, keep, send = slot_terms(
         counts, positions, where, object_field, halos, probe, amplitudes
     )
@@ -384,22 +359,21 @@
     rows, cols = lax.axis_size("row"), lax.axis_size("col")
     plain = [(i, i + 1) for i in range(cols - 1) if i + 1 != seam]
 
-    from_left = lax.ppermute(right_grad, "col", plain)
-    from_seam = lax.ppermute(right_grad, "col", [(seam - 1, seam)])
-    if (rows, cols) == (16, 16):
+    from_left = shifted(right_grad, "col", 1)
+    if (lax.axis_size("row"), lax.axis_size("col")) == (16, 16):
         value = keep + moved(send, core=1)
         value = z_exchange(value.reshape(8, window // 8, window))
-        value, below0_grad = added([[value], [below0_grad, corner_in]], vmem=8)
+        value, below0_grad, above1 = added([[value], [below0_grad, corner_in]], above1, vmem=8)
         above0 = shifted(below0_grad, "row", 1)
-        value, above1, from_left = added([[value] + neighbours(value, "x")], above1, from_left)
-        value, above0, from_seam = added([[value] + neighbours(value, "y")], above0, from_seam)
+        value = added([[value] + neighbours(value, "x")])[0]
+        value, above0, from_left = added([[value] + neighbours(value, "y")], above0, from_left)
         value = z_exchange(jnp.broadcast_to(value, (8,) + value.shape)).reshape(window, window)
         other = moved(value, core=1)
         probe_total = both_planes(where, value, other)
     else:
         above0 = shifted(below0_grad + corner_in, "row", 1)
         probe_total = lax.psum(jnp.where(core == 0, jnp.stack([keep, send]), jnp.stack([send, keep])), AXES)
-    return combined(where, tile_grad, from_left, from_seam, above0, above1), probe_total
+    return combined(tile_grad, from_left, above0, above1), probe_total
 
 
 def solution(mesh):

time: 138 us -> 131 us (0.949)
  starting transfers between devices: 72 us -> 64.1 us
  waiting for transfers between devices: 21.1 us -> 26.1 us
  blocking collectives: 20.2 us -> 18.5 us
    ppermute x8, starting transfers between devices: 23.7 us -> 11.4 us  [moved(): return lax.ppermute(value, AXES, route)]
    ppermute x6 -> x7, starting transfers between devices: 12.9 us -> 22.4 us  [shifted(): return lax.ppermute(block, axis, route)]
    ppermute x6 -> x7, waiting for transfers between devices: 10.9 us -> 18.4 us  [shifted(): return lax.ppermute(block, axis, route)]
    ppermute x1, starting transfers between devices: 23.7 us -> 17.3 us  [halos_in(): lax.ppermute(jnp.where(col == 0, relayed, below0), 'col', plain + [(0, se...]
    all_to_all x1, starting transfers between devices: 6.45 us -> 10.4 us  [z_exchange(): lax.all_to_all(chunks, AXES, 0, 0, tiled=True, axis_index_groups=groups)]
    all_to_all x1, waiting for transfers between devices: 3.82 us -> 0.01 us  [z_exchange(): lax.all_to_all(chunks, AXES, 0, 0, tiled=True, axis_index_groups=groups)]
    ppermute x2 -> x0, starting transfers between devices: 2.64 us -> none  [the longest x1 1.91 us: shards(): from_left = lax.ppermute(right_grad, 'col', plain)]
    all_to_all x1, blocking collectives: 20.2 us -> 18.5 us  [z_exchange(): lax.all_to_all(chunks, AXES, 0, 0, tiled=True, axis_index_groups=groups)]
  transfers between devices with their start and end apart: 20 -> 19, of which waited for: 8 -> 9; matrix products, arithmetic and copies ran while one was open for 2% -> 2% of each run, Pallas kernels for 2% -> 2%
where the time goes in v5:
time: 131 us; the launch traced here: 130 us
  starting transfers between devices  64.1 us (49%)
  waiting for transfers between devices  26.1 us (20%)
  blocking collectives  18.5 us (14%)
  Pallas kernels  14.3 us (11%)
  other arithmetic  3.94 us (3%)
  local copies, waits for them, and re-layouts  1.86 us (1%)
  between operations  1.49 us (1%)
    ppermute x7, starting transfers between devices, shifted(): return lax.ppermute(block, axis, route)  22.4 us
    all_to_all x1, blocking collectives, z_exchange(): lax.all_to_all(chunks, AXES, 0, 0, tiled=True, axis_index_groups=groups)  18.5 us
    ppermute x7, waiting for transfers between devices, shifted(): return lax.ppermute(block, axis, route)  18.4 us
    ppermute x1, starting transfers between devices, halos_in(): lax.ppermute(jnp.where(col == 0, relayed, below0), 'col', plain + [(0, se...  17.3 us
    ppermute x8, starting transfers between devices, moved(): return lax.ppermute(value, AXES, route)  11.4 us
    all_to_all x1, starting transfers between devices, z_exchange(): lax.all_to_all(chunks, AXES, 0, 0, tiled=True, axis_index_groups=groups)  10.4 us
    pallas_call x1, Pallas kernels, slot_terms(): pl.pallas_call(functools.partial(slots_kernel, w, t), out_shape=[f32((2,...  10.2 us
    ppermute x8, waiting for transfers between devices, moved(): return lax.ppermute(value, AXES, route)  7.39 us
  transfers between devices with their start and end apart: 19, of which 9 were waited for; matrix products, arithmetic and copies ran while one was open for 2% of the time, Pallas kernels for 2%

profile of v5, /device:TPU:1, one launch (start us, length us, event | category | flops | bytes accessed | tf_op | source)
XLA Modules:
  0.0 130.4 jit_solution(14731420238217470503)
XLA Ops:
  0.6 1.6 %fusion = (f32[2,256,256]{2,1,0:T(8,128)S(1)}, f32[2,256,256]{2,1,0:T(8,128)S(1)}, f32[2,256,256]{2,1,0:T(8,128)S(1)}, f32[2,256,256]{2,1,0:T(8,128)S(1)}) fusion(f32[2,512,512]{2,1,0:T(8,128)} %object_hbm.1, pred[]{:T(512)S(6)} %eq.12), kind=kLoop, calls=%fused_computation.3 | loop fusion | flops 131072 | bytes 3670017 | tf_op jit(solution)/shard_map/slice | solution.py:334
  2.9 1.3 collective-permute-start.1
  4.2 5.7 %collective-permute-start.2 = (f32[2,256,256]{2,1,0:T(8,128)S(1)}, f32[2,256,256]{2,1,0:T(8,128)}, u32[]{:S(2)}, u32[]{:S(2)}) collective-permute-start(f32[2,256,256]{2,1,0:T(8,128)S(1)} %get-tuple-element.30), channel_id=1, source_target_pairs={{1,0},{2,1},{3,2},{4,3},{5,4},{6,5},{7,6},{8,7},{9,8},{10,9},{11,1... | collective-permute-start | bytes 1572872 | tf_op jit(solution)/shard_map/ppermute | solution.py:24
  10.0 1.9 %collective-permute-start.3 = (f32[2,256,256]{2,1,0:T(8,128)S(1)}, f32[2,256,256]{2,1,0:T(8,128)}, u32[]{:S(2)}, u32[]{:S(2)}) collective-permute-start(f32[2,256,256]{2,1,0:T(8,128)S(1)} %get-tuple-element.29), channel_id=1, source_target_pairs={{1,0},{2,1},{3,2},{4,3},{5,4},{6,5},{7,6},{9,8},{10,9},{11,10},{12... | collective-permute-start | bytes 1572872 | tf_op jit(solution)/shard_map/ppermute | solution.py:342
  11.9 1.3 collective-permute-start
  13.2 4.2 %collective-permute-done.1.below0_hbm = f32[2,256,256]{2,1,0:T(8,128)S(1)} collective-permute-done((f32[2,256,256]{2,1,0:T(8,128)S(1)}, f32[2,256,256]{2,1,0:T(8,128)S(1)}, u32[]{:S(2)}, u32[]{:S(2)}) %collective-permute-start.1) | collective-permute-done | bytes 524320 | tf_op jit(solution)/shard_map/ppermute | solution.py:24
  17.5 17.3 %collective-permute-start.5 = (f32[2,256,256]{2,1,0:T(8,128)S(1)}, f32[2,256,256]{2,1,0:T(8,128)S(1)}, u32[]{:S(2)}, u32[]{:S(2)}) collective-permute-start(f32[2,256,256]{2,1,0:T(8,128)S(1)} %broadcast_select_fusion), channel_id=1, source_target_pairs={{1,0},{2,1},{3,2},{4,3},{5,4},{6,5},{7,6},{9,8},{10,9},{11,10},{12... | collective-permute-start | bytes 1572872 | tf_op jit(solution)/shard_map/ppermute | solution.py:343
  37.2 10.2 %slot_terms.1 = (f32[2,512,512]{2,1,0:T(8,128)}, f32[2,512,256]{2,1,0:T(8,128)}, f32[2,256,256]{2,1,0:T(8,128)}, f32[2,256,256]{2,1,0:T(8,128)}, f32[2,256,256]{...) custom-call(s32[1]{0:T(128)S(6)} %copy.16.counts_ref, s32[2,2]{1,0:T(2,128)} %pos_ref.1, s32[2]{0:T(128)} %pad_add_fusion.place_ref, ...), custom_call_target="tpu_custom_call" | custom-call | flops 3000000000 | bytes 14680064 | tf_op jit(solution)/shard_map/slot_terms/pallas_call | solution.py:181
  47.4 5.3 %collective-permute-start.6 = (f32[256,256]{1,0:T(8,128)}, f32[256,256]{1,0:T(8,128)S(1)}, u32[]{:S(2)}, u32[]{:S(2)}) collective-permute-start(f32[256,256]{1,0:T(8,128)} %get-tuple-element.17), channel_id=1, source_target_pairs={{0,1},{1,0},{32,33},{33,32},{64,65},{65,64},{96,97},{97,96},{128,1... | collective-permute-start | bytes 786440 | tf_op jit(solution)/shard_map/ppermute | solution.py:266
  52.7 1.9 %collective-permute-start.7 = (f32[2,256,256]{2,1,0:T(8,128)}, f32[2,256,256]{2,1,0:T(8,128)S(1)}, u32[]{:S(2)}, u32[]{:S(2)}) collective-permute-start(f32[2,256,256]{2,1,0:T(8,128)} %get-tuple-element.19), channel_id=1, source_target_pairs={{0,1},{1,2},{2,3},{3,4},{4,5},{5,6},{6,7},{7,8},{8,9},{9,10},{10,1... | collective-permute-start | bytes 1572872 | tf_op jit(solution)/shard_map/ppermute | solution.py:24
  54.6 1.3 %collective-permute-start.8 = (f32[2,256,256]{2,1,0:T(8,128)}, f32[2,256,256]{2,1,0:T(8,128)S(1)}, u32[]{:S(2)}, u32[]{:S(2)}) collective-permute-start(f32[2,256,256]{2,1,0:T(8,128)} %get-tuple-element.20), channel_id=1, source_target_pairs={{0,16},{16,32},{32,48},{48,64},{64,80},{80,96},{96,112},{112,128},... | collective-permute-start | bytes 1572872 | tf_op jit(solution)/shard_map/ppermute | solution.py:24
  55.9 1.9 %collective-permute-start.16 = (f32[2,512,256]{2,1,0:T(8,128)}, f32[2,512,256]{2,1,0:T(8,128)S(1)}, u32[]{:S(2)}, u32[]{:S(2)}) collective-permute-start(f32[2,512,256]{2,1,0:T(8,128)} %get-tuple-element.23), channel_id=1, source_target_pairs={{0,1},{1,2},{2,3},{3,4},{4,5},{5,6},{6,7},{7,8},{8,9},{9,10},{10,1... | collective-permute-start | bytes 3145736 | tf_op jit(solution)/shard_map/ppermute | solution.py:24
  57.8 1.7 %add.8 = f32[256,256]{1,0:T(8,128)} add(f32[256,256]{1,0:T(8,128)} %get-tuple-element.16, f32[256,256]{1,0:T(8,128)S(1)} %collective-permute-done.6) | non-fusion elementwise | flops 65536 | bytes 786432 | tf_op jit(solution)/shard_map/add | solution.py:364
  59.5 10.4 %all-to-all-start = ((f32[8,32,256]{2,1,0:T(8,128)}), f32[8,32,256]{2,1,0:T(8,128)S(1)}, u32[]{:S(2)}, u32[]{:S(2)}) async-start(f32[8,32,256]{2,1,0:T(8,128)} %bitcast.2), calls=%async_computation | async-start | bytes 524288 | tf_op jit(solution)/shard_map/all_to_all | solution.py:326
  69.9 14.2 %collective-permute-done.8.refs_3_ = f32[2,256,256]{2,1,0:T(8,128)S(1)} collective-permute-done((f32[2,256,256]{2,1,0:T(8,128)}, f32[2,256,256]{2,1,0:T(8,128)S(1)}, u32[]{:S(2)}, u32[]{:S(2)}) %collective-permute-start.8) | collective-permute-done | bytes 524320 | tf_op jit(solution)/shard_map/ppermute | solution.py:24
  85.2 8.9 %collective-permute-start.15 = (f32[2,256,256]{2,1,0:T(8,128)S(1)}, f32[2,256,256]{2,1,0:T(8,128)S(1)}, u32[]{:S(2)}, u32[]{:S(2)}) collective-permute-start(f32[2,256,256]{2,1,0:T(8,128)S(1)} %get-tuple-element.22), channel_id=1, source_target_pairs={{0,16},{16,32},{32,48},{48,64},{64,80},{80,96},{96,112},{112,128},... | collective-permute-start | bytes 1572872 | tf_op jit(solution)/shard_map/ppermute | solution.py:24
  95.7 1.3 collective-permute-done.11.refs_3_
  97.0 1.6 %collective-permute-done.10.refs_2_ = f32[32,256]{1,0:T(8,128)S(1)} collective-permute-done((f32[32,256]{1,0:T(8,128)S(1)}, f32[32,256]{1,0:T(8,128)S(1)}, u32[]{:S(2)}, u32[]{:S(2)}) %collective-permute-start.10) | collective-permute-done | bytes 32800 | tf_op jit(solution)/shard_map/ppermute | solution.py:266
  101.0 1.3 %collective-permute-done.14.refs_3_ = f32[32,256]{1,0:T(8,128)S(1)} collective-permute-done((f32[32,256]{1,0:T(8,128)S(1)}, f32[32,256]{1,0:T(8,128)S(1)}, u32[]{:S(2)}, u32[]{:S(2)}) %collective-permute-start.14) | collective-permute-done | bytes 32800 | tf_op jit(solution)/shard_map/ppermute | solution.py:266
  102.3 1.6 %collective-permute-done.13.refs_2_ = f32[32,256]{1,0:T(8,128)S(1)} collective-permute-done((f32[32,256]{1,0:T(8,128)S(1)}, f32[32,256]{1,0:T(8,128)S(1)}, u32[]{:S(2)}, u32[]{:S(2)}) %collective-permute-start.13) | collective-permute-done | bytes 32800 | tf_op jit(solution)/shard_map/ppermute | solution.py:266
  104.7 18.5 %all_to_all.10 = f32[8,32,256]{2,1,0:T(8,128)S(1)} all-to-all(f32[8,32,256]{2,1,0:T(8,128)S(1)} %broadcast_in_dim.3), channel_id=1, replica_groups={{0,32,64,96,128,160,192,224},{1,33,65,97,129,161,193,225},{8,40,72,104,..., dimensions={0} | all-to-all | bytes 524288 | tf_op jit(solution)/shard_map/all_to_all | solution.py:326
  123.2 3.1 %collective-permute-start.17 = (f32[256,256]{1,0:T(8,128)S(1)}, f32[256,256]{1,0:T(8,128)S(1)}, u32[]{:S(2)}, u32[]{:S(2)}) collective-permute-start(f32[256,256]{1,0:T(8,128)S(1)} %bitcast.4), channel_id=1, source_target_pairs={{0,1},{1,0},{32,33},{33,32},{64,65},{65,64},{96,97},{97,96},{128,1... | collective-permute-start | bytes 786440 | tf_op jit(solution)/shard_map/ppermute | solution.py:266
  126.3 2.7 %combined.1 = f32[2,512,512]{2,1,0:T(8,128)} custom-call(f32[2,512,512]{2,1,0:T(8,128)} %get-tuple-element.15.tile_hbm, f32[2,512,256]{2,1,0:T(8,128)S(1)} %get-tuple-element.24.left_hbm, f32[2,256,256]{2,1,0:T(8,128)S(1)} %get-tuple-element.25.above0_hbm, f32[2,256,256]{2,1,0:T(8,128)S(1)} %get-tuple-element.26.above1_hbm), custom_call_target="tpu_custom_call", output_to_operand_aliasing={{}: (0, {})} | custom-call | flops 5000000000 | bytes 6291456 | tf_op jit(solution)/shard_map/combined/pallas_call | solution.py:232
  129.0 1.4 %both_planes.1 = f32[2,256,256]{2,1,0:T(8,128)} custom-call(s32[2]{0:T(128)S(1)} %copy-done.1, f32[256,256]{1,0:T(8,128)S(1)} %bitcast.5, f32[256,256]{1,0:T(8,128)S(1)} %collective-permute-done.17.other_hbm), custom_call_target="tpu_custom_call" | custom-call | tf_op jit(solution)/shard_map/both_planes/pallas_call | solution.py:313
  (34 shorter events, 8.2 us)
Async XLA Ops:
  2.2 11.0 %collective-permute-start.4 = (f32[2,256,256]{2,1,0:T(8,128)S(1)}, f32[2,256,256]{2,1,0:T(8,128)S(1)}, u32[]{:S(2)}, u32[]{:S(2)}) collective-permute-start(f32[2,256,256]{2,1,0:T(8,128)S(1)} %get-tuple-element.28), channel_id=1, source_target_pairs={{8,0},{24,16},{40,32},{56,48},{72,64},{88,80},{104,96},{120,112},{... | collective-permute-start | bytes 1572872 | tf_op jit(solution)/shard_map/ppermute | solution.py:338
  2.9 14.5 %collective-permute-start.1 = (f32[2,256,256]{2,1,0:T(8,128)S(1)}, f32[2,256,256]{2,1,0:T(8,128)S(1)}, u32[]{:S(2)}, u32[]{:S(2)}) collective-permute-start(f32[2,256,256]{2,1,0:T(8,128)S(1)} %get-tuple-element.30), channel_id=1, source_target_pairs={{16,0},{32,16},{48,32},{64,48},{80,64},{96,80},{112,96},{128,112},... | collective-permute-start | bytes 1572872 | tf_op jit(solution)/shard_map/ppermute | solution.py:24
  4.2 31.9 %collective-permute-start.2 = (f32[2,256,256]{2,1,0:T(8,128)S(1)}, f32[2,256,256]{2,1,0:T(8,128)}, u32[]{:S(2)}, u32[]{:S(2)}) collective-permute-start(f32[2,256,256]{2,1,0:T(8,128)S(1)} %get-tuple-element.30), channel_id=1, source_target_pairs={{1,0},{2,1},{3,2},{4,3},{5,4},{6,5},{7,6},{8,7},{9,8},{10,9},{11,1... | collective-permute-start | bytes 1572872 | tf_op jit(solution)/shard_map/ppermute | solution.py:24
  10.0 26.2 %collective-permute-start.3 = (f32[2,256,256]{2,1,0:T(8,128)S(1)}, f32[2,256,256]{2,1,0:T(8,128)}, u32[]{:S(2)}, u32[]{:S(2)}) collective-permute-start(f32[2,256,256]{2,1,0:T(8,128)S(1)} %get-tuple-element.29), channel_id=1, source_target_pairs={{1,0},{2,1},{3,2},{4,3},{5,4},{6,5},{7,6},{9,8},{10,9},{11,10},{12... | collective-permute-start | bytes 1572872 | tf_op jit(solution)/shard_map/ppermute | solution.py:342
  11.9 24.2 %collective-permute-start = (f32[2,256,256]{2,1,0:T(8,128)S(1)}, f32[2,256,256]{2,1,0:T(8,128)}, u32[]{:S(2)}, u32[]{:S(2)}) collective-permute-start(f32[2,256,256]{2,1,0:T(8,128)S(1)} %get-tuple-element.31), channel_id=1, source_target_pairs={{16,0},{32,16},{48,32},{64,48},{80,64},{96,80},{112,96},{128,112},... | collective-permute-start | bytes 1572872 | tf_op jit(solution)/shard_map/ppermute | solution.py:24
  17.5 18.9 %copy-start.2 = (f32[2,256,256]{2,1,0:T(8,128)}, f32[2,256,256]{2,1,0:T(8,128)S(1)}, u32[]{:S(2)}) copy-start(f32[2,256,256]{2,1,0:T(8,128)S(1)} %collective-permute-done.1.below0_hbm) | copy-start | bytes 1572868
  17.5 18.8 %collective-permute-start.5 = (f32[2,256,256]{2,1,0:T(8,128)S(1)}, f32[2,256,256]{2,1,0:T(8,128)S(1)}, u32[]{:S(2)}, u32[]{:S(2)}) collective-permute-start(f32[2,256,256]{2,1,0:T(8,128)S(1)} %broadcast_select_fusion), channel_id=1, source_target_pairs={{1,0},{2,1},{3,2},{4,3},{5,4},{6,5},{7,6},{9,8},{10,9},{11,10},{12... | collective-permute-start | bytes 1572872 | tf_op jit(solution)/shard_map/ppermute | solution.py:343
  36.4 0.8 copy-start.3
  47.4 10.4 %collective-permute-start.6 = (f32[256,256]{1,0:T(8,128)}, f32[256,256]{1,0:T(8,128)S(1)}, u32[]{:S(2)}, u32[]{:S(2)}) collective-permute-start(f32[256,256]{1,0:T(8,128)} %get-tuple-element.17), channel_id=1, source_target_pairs={{0,1},{1,0},{32,33},{33,32},{64,65},{65,64},{96,97},{97,96},{128,1... | collective-permute-start | bytes 786440 | tf_op jit(solution)/shard_map/ppermute | solution.py:266
  52.7 17.3 %collective-permute-start.7 = (f32[2,256,256]{2,1,0:T(8,128)}, f32[2,256,256]{2,1,0:T(8,128)S(1)}, u32[]{:S(2)}, u32[]{:S(2)}) collective-permute-start(f32[2,256,256]{2,1,0:T(8,128)} %get-tuple-element.19), channel_id=1, source_target_pairs={{0,1},{1,2},{2,3},{3,4},{4,5},{5,6},{6,7},{7,8},{8,9},{9,10},{10,1... | collective-permute-start | bytes 1572872 | tf_op jit(solution)/shard_map/ppermute | solution.py:24
  54.6 29.5 %collective-permute-start.8 = (f32[2,256,256]{2,1,0:T(8,128)}, f32[2,256,256]{2,1,0:T(8,128)S(1)}, u32[]{:S(2)}, u32[]{:S(2)}) collective-permute-start(f32[2,256,256]{2,1,0:T(8,128)} %get-tuple-element.20), channel_id=1, source_target_pairs={{0,16},{16,32},{32,48},{48,64},{64,80},{80,96},{96,112},{112,128},... | collective-permute-start | bytes 1572872 | tf_op jit(solution)/shard_map/ppermute | solution.py:24
  55.9 48.7 %collective-permute-start.16 = (f32[2,512,256]{2,1,0:T(8,128)}, f32[2,512,256]{2,1,0:T(8,128)S(1)}, u32[]{:S(2)}, u32[]{:S(2)}) collective-permute-start(f32[2,512,256]{2,1,0:T(8,128)} %get-tuple-element.23), channel_id=1, source_target_pairs={{0,1},{1,2},{2,3},{3,4},{4,5},{5,6},{6,7},{7,8},{8,9},{9,10},{10,1... | collective-permute-start | bytes 3145736 | tf_op jit(solution)/shard_map/ppermute | solution.py:24
  59.5 24.6 %all-to-all-start = ((f32[8,32,256]{2,1,0:T(8,128)}), f32[8,32,256]{2,1,0:T(8,128)S(1)}, u32[]{:S(2)}, u32[]{:S(2)}) async-start(f32[8,32,256]{2,1,0:T(8,128)} %bitcast.2), calls=%async_computation | async-start | bytes 524288 | tf_op jit(solution)/shard_map/all_to_all | solution.py:326
  84.1 1.0 copy-start
  85.2 19.4 %collective-permute-start.15 = (f32[2,256,256]{2,1,0:T(8,128)S(1)}, f32[2,256,256]{2,1,0:T(8,128)S(1)}, u32[]{:S(2)}, u32[]{:S(2)}) collective-permute-start(f32[2,256,256]{2,1,0:T(8,128)S(1)} %get-tuple-element.22), channel_id=1, source_target_pairs={{0,16},{16,32},{32,48},{48,64},{64,80},{80,96},{96,112},{112,128},... | collective-permute-start | bytes 1572872 | tf_op jit(solution)/shard_map/ppermute | solution.py:24
  94.2 2.8 %collective-permute-start.11 = (f32[32,256]{1,0:T(8,128)S(1)}, f32[32,256]{1,0:T(8,128)S(1)}, u32[]{:S(2)}, u32[]{:S(2)}) collective-permute-start(f32[32,256]{1,0:T(8,128)S(1)} %get-tuple-element.21.refs_0_), channel_id=1, source_target_pairs={{0,6},{1,7},{32,38},{33,39},{64,70},{65,71},{96,102},{97,103},{128... | collective-permute-start | bytes 98312 | tf_op jit(solution)/shard_map/ppermute | solution.py:266
  94.2 4.4 %collective-permute-start.10 = (f32[32,256]{1,0:T(8,128)S(1)}, f32[32,256]{1,0:T(8,128)S(1)}, u32[]{:S(2)}, u32[]{:S(2)}) collective-permute-start(f32[32,256]{1,0:T(8,128)S(1)} %get-tuple-element.21.refs_0_), channel_id=1, source_target_pairs={{0,4},{1,5},{32,36},{33,37},{64,68},{65,69},{96,100},{97,101},{128... | collective-permute-start | bytes 98312 | tf_op jit(solution)/shard_map/ppermute | solution.py:266
  94.6 4.8 %collective-permute-start.9 = (f32[32,256]{1,0:T(8,128)S(1)}, f32[32,256]{1,0:T(8,128)S(1)}, u32[]{:S(2)}, u32[]{:S(2)}) collective-permute-start(f32[32,256]{1,0:T(8,128)S(1)} %get-tuple-element.21.refs_0_), channel_id=1, source_target_pairs={{0,2},{1,3},{32,34},{33,35},{64,66},{65,67},{96,98},{97,99},{128,1... | collective-permute-start | bytes 98312 | tf_op jit(solution)/shard_map/ppermute | solution.py:266
  99.4 2.9 %collective-permute-start.14 = (f32[32,256]{1,0:T(8,128)S(1)}, f32[32,256]{1,0:T(8,128)S(1)}, u32[]{:S(2)}, u32[]{:S(2)}) collective-permute-start(f32[32,256]{1,0:T(8,128)S(1)} %added.4.refs_0_), channel_id=1, source_target_pairs={{0,24},{1,25},{32,56},{33,57},{64,88},{65,89},{96,120},{97,121},{1... | collective-permute-start | bytes 98312 | tf_op jit(solution)/shard_map/ppermute | solution.py:266
  99.5 4.4 %collective-permute-start.13 = (f32[32,256]{1,0:T(8,128)S(1)}, f32[32,256]{1,0:T(8,128)S(1)}, u32[]{:S(2)}, u32[]{:S(2)}) collective-permute-start(f32[32,256]{1,0:T(8,128)S(1)} %added.4.refs_0_), channel_id=1, source_target_pairs={{0,16},{1,17},{32,48},{33,49},{64,80},{65,81},{96,112},{97,113},{1... | collective-permute-start | bytes 98312 | tf_op jit(solution)/shard_map/ppermute | solution.py:266
  100.1 4.5 %collective-permute-start.12 = (f32[32,256]{1,0:T(8,128)S(1)}, f32[32,256]{1,0:T(8,128)S(1)}, u32[]{:S(2)}, u32[]{:S(2)}) collective-permute-start(f32[32,256]{1,0:T(8,128)S(1)} %added.4.refs_0_), channel_id=1, source_target_pairs={{0,8},{1,9},{32,40},{33,41},{64,72},{65,73},{96,104},{97,105},{128... | collective-permute-start | bytes 98312 | tf_op jit(solution)/shard_map/ppermute | solution.py:266
  123.2 5.8 %collective-permute-start.17 = (f32[256,256]{1,0:T(8,128)S(1)}, f32[256,256]{1,0:T(8,128)S(1)}, u32[]{:S(2)}, u32[]{:S(2)}) collective-permute-start(f32[256,256]{1,0:T(8,128)S(1)} %bitcast.4), channel_id=1, source_target_pairs={{0,1},{1,0},{32,33},{33,32},{64,65},{65,64},{96,97},{97,96},{128,1... | collective-permute-start | bytes 786440 | tf_op jit(solution)/shard_map/ppermute | solution.py:266
  126.3 2.7 %copy-start.1 = (s32[2]{0:T(128)S(1)}, s32[2]{0:T(128)}, u32[]{:S(2)}) copy-start(s32[2]{0:T(128)} %pad_add_fusion.place_ref) | copy-start | bytes 28
